TPU v7x, 256 devices: a whole 4x4x8 slice. The times are simulated.
256 devices in a mesh: pipe: 16 (over y_lo, z), dp: 8 (over x, core), tensor: 2 (over y_hi).
Axes of the slice: x: 4, y: 4 (y_hi: 2, y_lo: 2; y = y_hi * 2 + y_lo), z: 8, core: 2. Of those that a mesh axis runs over, the one named last changes fastest.
Arguments:
- layer_input: bfloat16 [16, 1024, 8192], P('pipe', 'dp'), may hold values from -6 to 6
- norm_gain: bfloat16 [16, 8192], P('pipe'), may hold values from 0.5 to 1.5
- kv_weight: bfloat16 [16, 2, 8192, 512], P('pipe', None, 'dp', 'tensor'), may hold values from -0.0625 to 0.0625
- queries: bfloat16 [16, 1024, 4096], P('pipe', 'dp', 'tensor'), may hold values from -170 to 170
- out_grad: bfloat16 [16, 1024, 4096], P('pipe', 'dp', 'tensor'), may hold values from -6 to 6
- top_grad: bfloat16 [1024, 8192], P('dp', 'tensor'), may hold values from -4 to 4
- segment_ids: int32 [1024], P('dp'), may hold values from 0 to 31, never falling along the last dimension, each value on 1 to 128 neighbouring positions
- scale_exp: int32 [16, 2, 64, 4], P('pipe', None, 'dp', 'tensor'), may hold values from 3 to 6
Outputs:
- input_grad: bfloat16 [16, 1024, 8192], P('pipe', 'dp', 'tensor')
- kv_weight_grad: bfloat16 [16, 2, 8192, 512], P('pipe', None, 'dp', 'tensor')
Inputs may be any that keep to these rules, and one draw needn't show every extreme that they name: `segment_ids`: document numbers never fall; each document has 1 to 128 tokens.
All inputs are finite; a program needn't handle non-finite values.
Results may differ from a plain program's by a relative error of at most 0.019.
Values may be sent and summed in bfloat16 or wider, within the bound.
No kernel may reach another device: no remote copies, remote signals or barrier semaphores. Data moves between devices by JAX's collectives and lax.ppermute only.
A program may use at most 128 MiB of HBM per device.

v0:
```python
import jax
import jax.numpy as jnp
from jax import lax
from jax.sharding import PartitionSpec as P

HD = 128
BLOCK = 128
SPANS = 2


EPS = 1e-05


def carried_in(array, axis, combine, identity):
    count, mine = (lax.axis_size(axis), lax.axis_index(axis))
    everything = lax.all_gather(array, axis)
    start = jnp.broadcast_to(jnp.asarray(identity, array.dtype), array.shape)

    def turn(k, before):
        at = count - 1 - k
        reached = at > mine
        new = combine(before, everything[at])
        return jnp.where(reached, new, before)

    return lax.fori_loop(0, count, turn, start)


def add_terms(earlier, later):
    return earlier + later


def attend(query, grad_out, key_rows, value_rows, seg_query, seg_key, offset):
    count_q = query.shape[0]
    count_k = key_rows.shape[0]
    kv_local = key_rows.shape[1] // HD
    group_size = query.shape[1] // key_rows.shape[1]
    score_scale = HD ** (-0.5)
    query_h = query.reshape(count_q, kv_local, group_size, HD)
    grad_h = grad_out.reshape(count_q, kv_local, group_size, HD)
    key_h = key_rows.reshape(count_k, kv_local, HD)
    value_h = value_rows.reshape(count_k, kv_local, HD)
    scores = (
        jnp.einsum("qkgd,mkd->kgqm", query_h, key_h, preferred_element_type=jnp.float32)
        * score_scale
    )
    query_pos = offset + jnp.arange(count_q, dtype=jnp.int32)
    key_pos = jnp.arange(count_k, dtype=jnp.int32)
    allowed = (key_pos[None, :] <= query_pos[:, None]) & (seg_key[None, :] == seg_query[:, None])
    scores = jnp.where(allowed, scores, jnp.float32(-1e30))
    row_max = jnp.max(scores, -1, keepdims=True)
    probability = jnp.exp(scores - row_max)
    probability = probability / jnp.sum(probability, -1, keepdims=True)
    dprob = jnp.einsum("qkgd,mkd->kgqm", grad_h, value_h, preferred_element_type=jnp.float32)
    delta = jnp.sum(probability * dprob, -1, keepdims=True)
    dscore_b = (probability * (dprob - delta)).astype(jnp.bfloat16)
    prob_b = probability.astype(jnp.bfloat16)
    value_grad = jnp.einsum("kgqm,qkgd->mkd", prob_b, grad_h, preferred_element_type=jnp.float32)
    key_grad = (
        jnp.einsum("kgqm,qkgd->mkd", dscore_b, query_h, preferred_element_type=jnp.float32)
        * score_scale
    )
    return (key_grad.reshape(count_k, kv_local * HD), value_grad.reshape(count_k, kv_local * HD))


def finish(d_normed, x_hat_rows, inv_rms_rows, gain_f, tensor_pos, half_width):
    full_sum = lax.psum(d_normed, "tensor")
    gated_grad = gain_f * full_sum
    inner_mean = jnp.mean(gated_grad * x_hat_rows, -1, keepdims=True)
    whole_term = inv_rms_rows * (gated_grad - x_hat_rows * inner_mean)
    phase_term = lax.dynamic_slice_in_dim(whole_term, tensor_pos * half_width, half_width, 1)
    return phase_term


def on_device(
    layer_input, norm_gain, kv_weight, queries, out_grad, top_grad, segment_ids, scale_exp
):
    inputs = layer_input[0]
    query_all = queries[0]
    grad_all = out_grad[0]
    weights = lax.all_gather(kv_weight[0], "dp", axis=1, tiled=True)
    token_count = inputs.shape[0]
    feature_count = inputs.shape[1]
    kv_width = weights.shape[2]
    span_rows = token_count // SPANS
    half_width = feature_count // lax.axis_size("tensor")
    tensor_pos = lax.axis_index("tensor")
    x_float = inputs.astype(jnp.float32)
    inv_rms = lax.rsqrt(jnp.mean(x_float * x_float, -1, keepdims=True) + EPS)
    x_hat = x_float * inv_rms
    gain_f = norm_gain[0].astype(jnp.float32)
    normed = (x_hat * gain_f).astype(jnp.bfloat16)
    key_rows = jnp.dot(normed, weights[0], preferred_element_type=jnp.float32).astype(jnp.bfloat16)
    value_rows = jnp.dot(normed, weights[1], preferred_element_type=jnp.float32).astype(
        jnp.bfloat16
    )
    top_float = top_grad.astype(jnp.float32)
    key_acc = jnp.zeros((token_count, kv_width), jnp.float32)
    value_acc = jnp.zeros((token_count, kv_width), jnp.float32)
    pieces = []
    for span_index in reversed(range(SPANS)):
        row_start = span_index * span_rows
        row_end = row_start + span_rows
        key_part, value_part = attend(
            query_all[row_start:row_end],
            grad_all[row_start:row_end],
            key_rows[:row_end],
            value_rows[:row_end],
            segment_ids[row_start:row_end],
            segment_ids[:row_end],
            row_start,
        )
        padding = ((0, token_count - row_end), (0, 0))
        key_acc = key_acc + jnp.pad(key_part, padding)
        value_acc = value_acc + jnp.pad(value_part, padding)
        key_b = key_acc[row_start:row_end].astype(jnp.bfloat16)
        value_b = value_acc[row_start:row_end].astype(jnp.bfloat16)
        d_normed = jnp.einsum("tc,dc->td", key_b, weights[0], preferred_element_type=jnp.float32)
        d_normed = d_normed + jnp.einsum(
            "tc,dc->td", value_b, weights[1], preferred_element_type=jnp.float32
        )
        phase_term = finish(
            d_normed,
            x_hat[row_start:row_end],
            inv_rms[row_start:row_end],
            gain_f,
            tensor_pos,
            half_width,
        )
        pieces.append(phase_term)
    stacked = jnp.concatenate(pieces[::-1], 0)
    later_all = carried_in(stacked, "pipe", add_terms, jnp.zeros_like(stacked))
    stacked = stacked + later_all + top_float
    input_grad = stacked.astype(jnp.bfloat16)[None]
    grads_b = jnp.concatenate([key_acc.astype(jnp.bfloat16), value_acc.astype(jnp.bfloat16)], 1)
    summed = lax.psum_scatter(
        jnp.einsum("tr,tc->rc", normed, grads_b, preferred_element_type=jnp.float32).astype(
            jnp.bfloat16
        ),
        "dp",
        scatter_dimension=0,
        tiled=True,
    ).astype(jnp.float32)
    factor = jnp.exp2(-scale_exp[0].astype(jnp.float32))
    factor = jnp.repeat(jnp.repeat(factor, BLOCK, 1), HD, 2)
    both_grads = jnp.stack([summed[:, :kv_width], summed[:, kv_width:]])
    weight_grad = (both_grads * factor).astype(jnp.bfloat16)[None]
    return (input_grad, weight_grad)


def solution(mesh):
    placed = (
        P("pipe", "dp", None),
        P("pipe", None),
        P("pipe", None, "dp", "tensor"),
        P("pipe", "dp", "tensor"),
        P("pipe", "dp", "tensor"),
        P("dp", "tensor"),
        P("dp"),
        P("pipe", None, "dp", "tensor"),
    )
    return jax.shard_map(
        on_device,
        mesh=mesh,
        in_specs=placed,
        out_specs=(P("pipe", "dp", "tensor"), P("pipe", None, "dp", "tensor")),
        check_vma=False,
    )
```

profile of v0, /device:TPU:16, one launch (start us, length us, event | category | flops | bytes accessed | tf_op | source)
XLA Modules:
  0.0 680.4 jit_solution(699949194490273766)
XLA Ops:
  11.0 54.0 %all-gather.5.cloned.1.call-done = bf16[1,2,8192,256]{3,2,1,0:T(8,128)(2,1)} async-done(((bf16[1,2,1024,256]{3,2,1,0:T(8,128)(2,1)}), bf16[1,2,8192,256]{3,2,1,0:T(8,128)(2,1)}) %all-gather.5.cloned.1.call-update) | async-done | bytes 8388624 | tf_op jit(solution)/shard_map/all_gather | solution.py:80
  64.9 2.9 fusion.25
  67.9 3.0 fusion.24
  72.1 2.9 convolution_bitcast_fusion.2
  77.2 3.2 fusion.23
  86.7 3.7 fusion.7
  90.4 5.1 convolution_add_fusion
  97.0 2.7 convolution_add_fusion.1
  99.9 5.6 convolution_convert_fusion
  105.7 2.4 fusion.2
  108.1 110.7 %all-reduce.5.cloned.1.call-done = (f32[64,8192]{1,0:T(8,128)}, f32[64,8192]{1,0:T(8,128)}) async-done(((f32[64,8192]{1,0:T(8,128)}, f32[64,8192]{1,0:T(8,128)}), (f32[64,8192]{1,0:T(8,128)}, f32[64,8192]{1,0:T(8,128)})) %all-reduce.5.cloned.1.call-update) | async-done | bytes 4194320 | tf_op jit(solution)/shard_map/psum | solution.py:66
  218.8 4.4 multiply_reduce_fusion.1
  227.0 3.9 broadcast_in_dim.31
  230.9 3.9 reshape.194
  234.7 44.0 %reduce-scatter.2.cloned.1.call-done = bf16[1024,512]{1,0:T(8,128)(2,1)} async-done(((bf16[8192,512]{1,0:T(8,128)(2,1)}), bf16[1024,512]{1,0:T(8,128)(2,1)}) %reduce-scatter.2.cloned.1.call-update) | async-done | bytes 1048592 | tf_op jit(solution)/shard_map/reduce_scatter | solution.py:135
  283.0 350.6 %all-gather.7.cloned.1.call-done = f32[2048,4096]{1,0:T(8,128)} async-done(((f32[128,4096]{1,0:T(8,128)}), f32[2048,4096]{1,0:T(8,128)}) %all-gather.7.cloned.1.call-update) | async-done | bytes 33554448 | tf_op jit(solution)/shard_map/all_gather | solution.py:16
  633.6 37.4 %while.16 = (s32[]{:T(128)}, f32[128,4096]{1,0:T(8,128)S(1)}, s32[]{:T(128)}, f32[16,128,4096]{2,1,0:T(8,128)}, s32[]{:T(128)}, /*index=5*/s32[]{:T(128)}, s32[]{:T(128)}, s32[]{:T(128)}) while((s32[]{:T(128)}, f32[128,4096]{1,0:T(8,128)S(1)}, s32[]{:T(128)}, f32[16,128,4096]{2,1,0:T(8,128)}, s32[]{:T(128)}, ...), condition=%wide.region_12.13_spmd.clone, body=%wide.region_11.12_spmd.clone.sunk | while | flops 1572872 | bytes 6291619 | solution.py:25
  636.0 2.3 add_select_fusion.2
  638.3 2.3 add_select_fusion.2
  640.6 2.3 add_select_fusion.2
  643.0 2.3 add_select_fusion.2
  647.6 2.3 add_select_fusion.2
  650.0 2.3 add_select_fusion.2
  652.3 2.3 add_select_fusion.2
  654.7 2.3 add_select_fusion.2
  657.0 2.3 add_select_fusion.2
  659.3 2.3 add_select_fusion.2
  661.7 2.3 add_select_fusion.2
  664.0 2.3 add_select_fusion.2
  666.4 2.3 add_select_fusion.2
  668.7 2.3 add_select_fusion.2
  671.0 2.8 fusion.28
  (79 shorter events, 27.6 us)
Async XLA Ops:
  7.2 2.1 copy-start.6
  7.2 2.1 copy-start.3
  7.2 57.7 %all-gather.5.cloned.1.call-start = ((), (), s32[]{:S(2)}) async-start(), calls=%async_computation.2 | async-start | bytes 9437184 | tf_op jit(solution)/shard_map/all_gather | solution.py:80
  7.9 2.3 copy-start
  7.9 210.9 %all-reduce.5.cloned.1.call-start = ((), (), s32[]{:S(2)}) async-start(), calls=%async_computation.4 | async-start | bytes 8388608 | tf_op jit(solution)/shard_map/psum | solution.py:66
  9.3 1.4 copy-start.7
  67.9 3.0 copy-start.4
  70.9 6.3 copy-start.5
  77.2 3.4 slice-start.2
  77.2 3.4 slice-start.3
  86.7 8.9 %slice-start = ((s8[8388608]{0:T(1024)(128)(4,1)}), s8[4194304]{0:T(1024)(128)(4,1)S(1)}, s32[]{:S(2)}) async-start(s8[8388608]{0:T(1024)(128)(4,1)} %bitcast.160), calls=%async_computation.5 | async-start | bytes 8388608
  90.4 5.1 slice-start.1
  99.7 179.0 %reduce-scatter.2.cloned.1.call-start = ((), (), s32[]{:S(2)}) async-start(), calls=%async_computation.1 | async-start | bytes 9437184 | tf_op jit(solution)/shard_map/reduce_scatter | solution.py:135
  105.6 528.0 %all-gather.7.cloned.1.call-start = ((), (), s32[]{:S(2)}) async-start(), calls=%async_computation.3 | async-start | bytes 35651584 | tf_op jit(solution)/shard_map/all_gather | solution.py:16
  223.7 1.0 copy-start.1
  226.1 0.7 copy-start.8
  280.2 1.6 copy-start.2
Sparse Core Ops, SparseCore 0:
  9.9 55.0 all-gather.4
  99.8 118.9 all-reduce.4
  221.5 57.1 reduce-scatter.1
  280.5 353.1 all-gather.6
where the time goes:
time: 683 us; the launch traced here: 680 us
  waiting for transfers between devices  560 us (82%)
  other arithmetic  51.9 us (8%)
  matrix products  39.7 us (6%)
  between operations  14.2 us (2%)
  local copies, waits for them, and re-layouts  13.9 us (2%)
    all_gather x1, waiting for transfers between devices, carried_in(): everything = lax.all_gather(array, axis)  351 us
    psum x1, waiting for transfers between devices, finish(): full_sum = lax.psum(d_normed, 'tensor')  111 us
    all_gather x1, waiting for transfers between devices, on_device(): weights = lax.all_gather(kv_weight[0], 'dp', axis=1, tiled=True)  54 us
    reduce_scatter x1, waiting for transfers between devices, on_device(): lax.psum_scatter(jnp.einsum('tr,tc->rc', normed, grads_b, preferred_eleme...  44 us
    select_n x16, other arithmetic, turn(): return jnp.where(reached, new, before)  36.9 us
  transfers between devices with their start and end apart: 4, of which 4 were waited for; matrix products, arithmetic and copies ran while one was open for 4% of the time, Pallas kernels for 0%

commit v1 on v0

v1 whole, which is shorter than its diff:
```python
import jax
import jax.numpy as jnp
from jax import lax
from jax.experimental import pallas as pl
from jax.experimental.pallas import tpu as pltpu
from jax.sharding import PartitionSpec as P

HD = 128
BLOCK = 128
EPS = 1e-05


def attend(query, grad_out, key_rows, value_rows, segments):
    count = query.shape[0]
    kv_local = key_rows.shape[1] // HD
    group_size = query.shape[1] // key_rows.shape[1]
    score_scale = HD ** (-0.5)
    query_h = query.reshape(count, kv_local, group_size, HD)
    grad_h = grad_out.reshape(count, kv_local, group_size, HD)
    key_h = key_rows.reshape(count, kv_local, HD)
    value_h = value_rows.reshape(count, kv_local, HD)
    scores = (
        jnp.einsum("qkgd,mkd->kgqm", query_h, key_h, preferred_element_type=jnp.float32)
        * score_scale
    )
    pos = jnp.arange(count, dtype=jnp.int32)
    allowed = (pos[None, :] <= pos[:, None]) & (segments[None, :] == segments[:, None])
    scores = jnp.where(allowed, scores, jnp.float32(-1e30))
    row_max = jnp.max(scores, -1, keepdims=True)
    probability = jnp.exp(scores - row_max)
    probability = probability / jnp.sum(probability, -1, keepdims=True)
    dprob = jnp.einsum("qkgd,mkd->kgqm", grad_h, value_h, preferred_element_type=jnp.float32)
    delta = jnp.sum(probability * dprob, -1, keepdims=True)
    dscore_b = (probability * (dprob - delta)).astype(jnp.bfloat16)
    prob_b = probability.astype(jnp.bfloat16)
    value_grad = jnp.einsum("kgqm,qkgd->mkd", prob_b, grad_h, preferred_element_type=jnp.float32)
    key_grad = (
        jnp.einsum("kgqm,qkgd->mkd", dscore_b, query_h, preferred_element_type=jnp.float32)
        * score_scale
    )
    return (
        key_grad.reshape(count, kv_local * HD).astype(jnp.bfloat16),
        value_grad.reshape(count, kv_local * HD).astype(jnp.bfloat16),
    )


def suffix_kernel(parts_ref, top_ref, out_ref):
    layers = parts_ref.shape[0]
    running = top_ref[...].astype(jnp.float32)
    for layer in reversed(range(layers)):
        running = running + parts_ref[layer].astype(jnp.float32)
        out_ref[layer] = running.astype(jnp.bfloat16)


def suffix_sum(parts, top):
    layers, rows, width = parts.shape
    tile = min(width, 1024)
    return pl.pallas_call(
        suffix_kernel,
        grid=(width // tile,),
        in_specs=[
            pl.BlockSpec((layers, rows, tile), lambda i: (0, 0, i)),
            pl.BlockSpec((rows, tile), lambda i: (0, i)),
        ],
        out_specs=pl.BlockSpec((layers, rows, tile), lambda i: (0, 0, i)),
        out_shape=jax.ShapeDtypeStruct(parts.shape, jnp.bfloat16),
        cost_estimate=pl.CostEstimate(
            flops=parts.size, bytes_accessed=4 * parts.size, transcendentals=0
        ),
    )(parts, top)


def on_device(
    layer_input, norm_gain, kv_weight, queries, out_grad, top_grad, segment_ids, scale_exp
):
    inputs = layer_input[0]
    weights = lax.all_gather(kv_weight[0], "dp", axis=1, tiled=True)
    token_count, feature_count = inputs.shape
    kv_width = weights.shape[2]
    half_width = feature_count // lax.axis_size("tensor")
    tensor_pos = lax.axis_index("tensor")
    pipe_count = lax.axis_size("pipe")
    pipe_pos = lax.axis_index("pipe")
    x_float = inputs.astype(jnp.float32)
    inv_rms = lax.rsqrt(jnp.mean(x_float * x_float, -1, keepdims=True) + EPS)
    x_hat = x_float * inv_rms
    gain_f = norm_gain[0].astype(jnp.float32)
    normed = (x_hat * gain_f).astype(jnp.bfloat16)
    key_f = jnp.dot(normed, weights[0], preferred_element_type=jnp.float32)
    value_f = jnp.dot(normed, weights[1], preferred_element_type=jnp.float32)
    key_b, value_b = attend(
        queries[0],
        out_grad[0],
        key_f.astype(jnp.bfloat16),
        value_f.astype(jnp.bfloat16),
        segment_ids,
    )
    inner = (
        jnp.sum(
            key_b.astype(jnp.float32) * key_f + value_b.astype(jnp.float32) * value_f,
            -1,
            keepdims=True,
        )
        / feature_count
    )

    def partial_branch(start):
        rows_k = lax.dynamic_slice_in_dim(weights[0], start, half_width, 0)
        rows_v = lax.dynamic_slice_in_dim(weights[1], start, half_width, 0)
        d_normed = jnp.einsum("tc,dc->td", key_b, rows_k, preferred_element_type=jnp.float32)
        d_normed = d_normed + jnp.einsum(
            "tc,dc->td", value_b, rows_v, preferred_element_type=jnp.float32
        )
        x_rows = lax.dynamic_slice_in_dim(inputs, start, half_width, 1).astype(jnp.float32)
        gains = lax.dynamic_slice_in_dim(gain_f, start, half_width, 0)
        return inv_rms * (gains * d_normed - (x_rows * inv_rms) * inner)

    theirs = partial_branch((1 - tensor_pos) * half_width).astype(jnp.bfloat16)
    arrived = lax.ppermute(theirs, "tensor", [(0, 1), (1, 0)])
    mine = partial_branch(tensor_pos * half_width)
    branch = (mine + arrived.astype(jnp.float32)).astype(jnp.bfloat16)
    parts = lax.all_to_all(branch, "pipe", 0, 0, tiled=True)
    rows = token_count // pipe_count
    top_rows = lax.dynamic_slice_in_dim(top_grad, pipe_pos * rows, rows, 0)
    sums = suffix_sum(parts.reshape(pipe_count, rows, half_width), top_rows)
    input_grad = lax.all_to_all(sums.reshape(token_count, half_width), "pipe", 0, 0, tiled=True)

    grads_b = jnp.concatenate([key_b, value_b], 1)
    summed = lax.psum_scatter(
        jnp.einsum("tr,tc->rc", normed, grads_b, preferred_element_type=jnp.float32).astype(
            jnp.bfloat16
        ),
        "dp",
        scatter_dimension=0,
        tiled=True,
    ).astype(jnp.float32)
    factor = jnp.exp2(-scale_exp[0].astype(jnp.float32))
    factor = jnp.repeat(jnp.repeat(factor, BLOCK, 1), HD, 2)
    both_grads = jnp.stack([summed[:, :kv_width], summed[:, kv_width:]])
    weight_grad = (both_grads * factor).astype(jnp.bfloat16)[None]
    return (input_grad[None], weight_grad)


def solution(mesh):
    placed = (
        P("pipe", "dp", None),
        P("pipe", None),
        P("pipe", None, "dp", "tensor"),
        P("pipe", "dp", "tensor"),
        P("pipe", "dp", "tensor"),
        P("dp", "tensor"),
        P("dp"),
        P("pipe", None, "dp", "tensor"),
    )
    return jax.shard_map(
        on_device,
        mesh=mesh,
        in_specs=placed,
        out_specs=(P("pipe", "dp", "tensor"), P("pipe", None, "dp", "tensor")),
        check_vma=False,
    )
```

time: 683 us -> 207 us (0.30)
  waiting for transfers between devices: 560 us -> 123 us
  other arithmetic: 51.9 us -> 5.27 us
  starting transfers between devices: 0.34 us -> 13.5 us
  matrix products: 39.7 us -> 27 us
    all_gather x1 -> x0, waiting for transfers between devices: 351 us -> none  [carried_in(): everything = lax.all_gather(array, axis)]
    psum x1 -> x0, waiting for transfers between devices: 111 us -> none  [finish(): full_sum = lax.psum(d_normed, 'tensor')]
    all_to_all x0 -> x2, waiting for transfers between devices: none -> 45.7 us  [the longest x1 25.4 us: on_device(): parts = lax.all_to_all(branch, 'pipe', 0, 0, tiled=True)]
    reduce_scatter x1, waiting for transfers between devices: 44 us -> 0.01 us  [on_device(): lax.psum_scatter(jnp.einsum('tr,tc->rc', normed, grads_b, preferred_eleme...]
    select_n x16 -> x0, other arithmetic: 36.9 us -> none  [turn(): return jnp.where(reached, new, before)]
    ppermute x0 -> x1, waiting for transfers between devices: none -> 25.5 us  [on_device(): arrived = lax.ppermute(theirs, 'tensor', [(0, 1), (1, 0)])]
    all_to_all x0 -> x2, starting transfers between devices: none -> 12.9 us  [the longest x1 7.75 us: on_device(): parts = lax.all_to_all(branch, 'pipe', 0, 0, tiled=True)]
  transfers between devices with their start and end apart: 4 -> 5, of which waited for: 4 -> 4; matrix products, arithmetic and copies ran while one was open for 4% -> 11% of each run, Pallas kernels for 0% -> 2%
where the time goes in v1:
time: 207 us; the launch traced here: 206 us
  waiting for transfers between devices  123 us (59%)
  matrix products  27 us (13%)
  local copies, waits for them, and re-layouts  19.1 us (9%)
  between operations  14.2 us (7%)
  starting transfers between devices  13.5 us (7%)
  other arithmetic  5.27 us (3%)
  Pallas kernels  3.42 us (2%)
    all_gather x1, waiting for transfers between devices, on_device(): weights = lax.all_gather(kv_weight[0], 'dp', axis=1, tiled=True)  51.5 us
    ppermute x1, waiting for transfers between devices, on_device(): arrived = lax.ppermute(theirs, 'tensor', [(0, 1), (1, 0)])  25.5 us
    all_to_all x1, waiting for transfers between devices, on_device(): parts = lax.all_to_all(branch, 'pipe', 0, 0, tiled=True)  25.4 us
    all_to_all x1, waiting for transfers between devices, on_device(): lax.all_to_all(sums.reshape(token_count, half_width), 'pipe', 0, 0, tiled...  20.4 us
    all_to_all x1, starting transfers between devices, on_device(): parts = lax.all_to_all(branch, 'pipe', 0, 0, tiled=True)  7.75 us
    dot_general x1, matrix products, on_device(): jnp.einsum('tr,tc->rc', normed, grads_b, preferred_element_type=jnp.float32)  5.69 us
    all_to_all x1, starting transfers between devices, on_device(): lax.all_to_all(sums.reshape(token_count, half_width), 'pipe', 0, 0, tiled...  5.1 us
  transfers between devices with their start and end apart: 5, of which 4 were waited for; matrix products, arithmetic and copies ran while one was open for 11% of the time, Pallas kernels for 2%

profile of v1, /device:TPU:16, one launch (start us, length us, event | category | flops | bytes accessed | tf_op | source)
XLA Modules:
  0.0 205.9 jit_solution(4624163111145990272)
XLA Ops:
  7.2 0.7 all-gather.3.cloned.1.call-update
  8.0 0.8 convert_element_type.109
  8.8 2.0 copy.33
  10.8 2.0 copy.34
  13.5 51.5 %all-gather.3.cloned.1.call-done = bf16[1,2,8192,256]{3,2,1,0:T(8,128)(2,1)} async-done(((bf16[1,2,1024,256]{3,2,1,0:T(8,128)(2,1)}), bf16[1,2,8192,256]{3,2,1,0:T(8,128)(2,1)}) %all-gather.3.cloned.1.call-update) | async-done | bytes 8388624 | tf_op jit(solution)/shard_map/all_gather | solution.py:77
  64.9 3.6 %fusion.79 = (bf16[128,256]{1,0:T(8,128)(2,1)S(1)}, f32[128,256]{1,0:T(8,128)}) fusion(bf16[1,2,8192,256]{3,2,1,0:T(8,128)(2,1)} %all-gather.3.cloned.1.call-done, bf16[1,128,8192]{2,1,0:T(8,128)(2,1)S(1)} %copy-done.1, f32[8192]{0:T(1024)S(1)} %bitcast.130, f32[128]{0:T(128)S(1)} %add_rsqrt_fusion), kind=kOutput, calls=%fused_computation.88 | convolution fusion | flops 541097984 | bytes 6521344 | tf_op jit(solution)/shard_map/dot_general | solution.py:90
  68.5 3.6 %fusion.80 = (bf16[128,256]{1,0:T(8,128)(2,1)S(1)}, f32[128,256]{1,0:T(8,128)}) fusion(bf16[1,2,8192,256]{3,2,1,0:T(8,128)(2,1)} %all-gather.3.cloned.1.call-done, bf16[1,128,8192]{2,1,0:T(8,128)(2,1)S(1)} %copy-done.1, f32[8192]{0:T(1024)S(1)} %bitcast.131, f32[128]{0:T(128)S(1)} %add_rsqrt_fusion), kind=kOutput, calls=%fused_computation.89 | convolution fusion | flops 541097984 | bytes 6521344 | tf_op jit(solution)/shard_map/dot_general | solution.py:89
  72.2 2.5 %fusion.81 = (f32[2,8,128]{2,1,0:T(8,128)S(1)}, f32[2,8,128,128]{2,3,1,0:T(8,128)}) fusion(bf16[128,2,8,128]{0,3,2,1:T(8,128)(2,1)} %bitcast.125, pred[128,128]{0,1:T(8,128)(4,1)S(1)} %fusion.55, bf16[128,2,128,1]{2,1,0,3:T(2,128)(2,1)S(1)} %bitcast.135), kind=kOutput, calls=%fused_computation.90 | convolution fusion | flops 68157568 | bytes 1662976 | tf_op jit(solution)/shard_map/sub | solution.py:30
  74.6 1.9 fusion.42
  76.5 2.7 %multiply_reduce_fusion = (f32[2,8,128]{2,1,0:T(8,128)S(1)}, f32[2,8,128,128]{2,3,1,0:T(8,128)}) fusion(f32[2,8,128,128]{2,3,1,0:T(8,128)} %get-tuple-element.13, f32[2,8,128]{2,1,0:T(8,128)S(1)} %get-tuple-element.12, bf16[128,2,8,128]{0,3,2,1:T(8,128)(2,1)} %bitcast.129, bf16[128,2,128,1]{2,1,0,3:T(2,128)(2,1)S(1)} %bitcast.138), kind=kOutput, calls=%fused_computation.59 | convolution fusion | flops 67893248 | bytes 2703360 | tf_op jit(solution)/shard_map/qkgd,mkd->kgqm/dot_general | solution.py:32
  79.1 2.2 %fusion.41 = bf16[2,128,128]{1,2,0:T(8,128)(2,1)S(1)} fusion(bf16[128,2,8,128]{0,3,2,1:T(8,128)(2,1)} %bitcast.127, f32[2,8,128,128]{2,3,1,0:T(8,128)} %get-tuple-element.15, f32[2,8,128]{2,1,0:T(8,128)S(1)} %get-tuple-element.14, f32[2,8,128]{2,1,0:T(8,128)S(1)} %get-tuple-element.12, pred[128,128]{0,1:T(8,128)(4,1)S(1)} %fusion.55, ...), kind=kOutput, calls=%fused_computation.53 | convolution fusion | flops 136120448 | bytes 1736704 | tf_op jit(solution)/shard_map/kgqm,qkgd->mkd/dot_general | solution.py:38
  81.6 5.7 %convolution_convert_fusion = bf16[8192,512]{1,0:T(8,128)(2,1)} fusion(bf16[1,128,8192]{2,1,0:T(8,128)(2,1)S(1)} %copy-done.1, f32[8192]{0:T(1024)S(1)} %bitcast.132, f32[128]{0:T(128)S(1)} %add_rsqrt_fusion, bf16[128,256]{1,0:T(8,128)(2,1)S(1)} %copy.32, bf16[128,256]{1,0:T(8,128)(2,1)S(1)} %copy.31), kind=kOutput, calls=%fused_computation.1 | convolution fusion | flops 1082392576 | bytes 10650112 | tf_op jit(solution)/shard_map/tr,tc->rc/dot_general | solution.py:130
  87.3 1.1 add_reduce_fusion
  88.4 3.8 %fusion.78 = (bf16[1,1,8192,256]{3,2,1,0:T(8,128)(2,1)S(1)}, bf16[1,1,8192,256]{3,2,1,0:T(8,128)(2,1)S(1)}) fusion(bf16[1,2,8192,256]{3,2,1,0:T(8,128)(2,1)} %all-gather.3.cloned.1.call-done), kind=kLoop, calls=%fused_computation.87 | loop fusion | bytes 16777216 | tf_op jit(solution)/shard_map/slice | solution.py:90
  92.2 0.8 fusion.25
  93.0 1.1 fusion.9
  94.1 0.6 collective-permute-start
  94.7 0.8 fusion.28
  95.5 25.5 %collective-permute-done = bf16[128,4096]{1,0:T(8,128)(2,1)S(1)} collective-permute-done((bf16[128,4096]{1,0:T(8,128)(2,1)S(1)}, bf16[128,4096]{1,0:T(8,128)(2,1)S(1)}, u32[]{:S(2)}, u32[]{:S(2)}) %collective-permute-start) | collective-permute-done | bytes 1048608 | tf_op jit(solution)/shard_map/ppermute | solution.py:119
  121.0 2.2 %fusion.43 = bf16[16,8,4096]{2,1,0:T(8,128)(2,1)} fusion(bf16[128,4096]{1,0:T(8,128)(2,1)S(1)} %collective-permute-done, f32[128,4096]{1,0:T(8,128)S(1)} %fusion.28, bf16[128,256]{0,1:T(8,128)(2,1)S(1)} %bitcast.121, bf16[1,1,8192,256]{3,2,1,0:T(8,128)(2,1)S(1)} %get-tuple-element.2, s32[]{:T(128)S(6)} %select_n.10, f32[128]{0:T(128)S(1)} %broadcast_multiply_fusion, ...), kind=kOutput, calls=%fused_computation.55 | convolution fusion | flops 273678336 | bytes 7424000 | tf_op jit(solution)/shard_map/tc,dc->td/dot_general | solution.py:111
  123.2 7.8 %all-to-all-start = ((bf16[16,8,4096]{2,1,0:T(8,128)(2,1)}), bf16[16,8,4096]{2,1,0:T(8,128)(2,1)S(1)}, u32[]{:S(2)}, u32[]{:S(2)}) async-start(bf16[16,8,4096]{2,1,0:T(8,128)(2,1)} %fusion.43), calls=%async_computation | async-start | bytes 2097152 | tf_op jit(solution)/shard_map/all_to_all | solution.py:122
  131.0 0.6 constant_dynamic-slice_fusion.top_ref
  131.6 25.4 %all-to-all-done.parts_ref = bf16[16,8,4096]{2,1,0:T(8,128)(2,1)S(1)} async-done(((bf16[16,8,4096]{2,1,0:T(8,128)(2,1)}), bf16[16,8,4096]{2,1,0:T(8,128)(2,1)S(1)}, u32[]{:S(2)}, u32[]{:S(2)}) %all-to-all-start) | async-done | bytes 1048608 | tf_op jit(solution)/shard_map/all_to_all | solution.py:122
  157.0 1.0 copy-done.2
  158.0 3.4 %shard_map.95 = bf16[16,8,4096]{2,1,0:T(8,128)(2,1)} custom-call(bf16[16,8,4096]{2,1,0:T(8,128)(2,1)} %copy-done.2, bf16[8,4096]{1,0:T(8,128)(2,1)} %constant_dynamic-slice_fusion.top_ref), custom_call_target="tpu_custom_call" | custom-call | flops 524288 | bytes 2097152 | tf_op jit(solution)/shard_map/pallas_call | solution.py:58
  161.4 5.1 %all-to-all-start.1 = ((bf16[16,8,4096]{2,1,0:T(8,128)(2,1)}), bf16[16,8,4096]{2,1,0:T(8,128)(2,1)}, u32[]{:S(2)}, u32[]{:S(2)}) async-start(bf16[16,8,4096]{2,1,0:T(8,128)(2,1)} %shard_map.95), calls=%async_computation.1 | async-start | bytes 2097152 | tf_op jit(solution)/shard_map/all_to_all | solution.py:126
  166.7 3.8 %broadcast_in_dim.18 = f32[2,1024,2,128]{3,2,1,0:T(2,128)} broadcast(f32[2,1024,2]{2,1,0:T(8,128)S(1)} %bitcast.118), dimensions={0,1,2} | broadcast | bytes 2113536 | tf_op jit(solution)/shard_map/broadcast_in_dim | solution.py:138
  170.5 2.9 %reshape.145 = f32[1,2,1024,256]{3,2,1,0:T(8,128)S(1)} reshape(f32[2,1024,2,128]{3,2,1,0:T(2,128)} %broadcast_in_dim.18) | data formatting | bytes 4194304 | tf_op jit(solution)/shard_map/reshape | solution.py:138
  173.5 20.4 %all-to-all-done.1 = bf16[16,8,4096]{2,1,0:T(8,128)(2,1)} async-done(((bf16[16,8,4096]{2,1,0:T(8,128)(2,1)}), bf16[16,8,4096]{2,1,0:T(8,128)(2,1)}, u32[]{:S(2)}, u32[]{:S(2)}) %all-to-all-start.1) | async-done | bytes 1048608 | tf_op jit(solution)/shard_map/all_to_all | solution.py:126
  193.8 1.5 convert_element_type.134
  195.5 1.3 fusion.21
  196.8 2.3 %copy.56 = bf16[1,128,4096]{2,1,0:T(8,128)(2,1)} copy(bf16[1,128,4096]{2,1,0:T(8,128)(2,1)} %bitcast.28) | data formatting | bytes 2097152
  (26 shorter events, 1.3 us)
Async XLA Ops:
  7.2 123.8 %copy-start = (bf16[128,4096]{1,0:T(8,128)(2,1)S(1)}, bf16[128,4096]{1,0:T(8,128)(2,1)}, u32[]{:S(2)}) copy-start(bf16[128,4096]{1,0:T(8,128)(2,1)} %param.13) | copy-start | bytes 3145732
  7.2 5.7 %copy-start.1 = (bf16[1,128,8192]{2,1,0:T(8,128)(2,1)S(1)}, bf16[1,128,8192]{2,1,0:T(8,128)(2,1)}, u32[]{:S(2)}) copy-start(bf16[1,128,8192]{2,1,0:T(8,128)(2,1)} %param.8) | copy-start | bytes 6291460
  7.2 57.7 %all-gather.3.cloned.1.call-start = ((), (), s32[]{:S(2)}) async-start(), calls=%async_computation.4 | async-start | bytes 9437184 | tf_op jit(solution)/shard_map/all_gather | solution.py:77
  7.9 185.9 %reduce-scatter.2.cloned.1.call-start = ((), (), s32[]{:S(2)}) async-start(), calls=%async_computation.3 | async-start | bytes 9437184 | tf_op jit(solution)/shard_map/reduce_scatter | solution.py:129
  8.8 4.6 %copy-start.3 = (s32[128]{0:T(128)S(1)}, s32[128]{0:T(128)}, u32[]{:S(2)}) copy-start(s32[128]{0:T(128)} %param.14) | copy-start | bytes 1540
  94.1 26.9 %collective-permute-start = (bf16[128,4096]{1,0:T(8,128)(2,1)S(1)}, bf16[128,4096]{1,0:T(8,128)(2,1)S(1)}, u32[]{:S(2)}, u32[]{:S(2)}) collective-permute-start(bf16[128,4096]{1,0:T(8,128)(2,1)S(1)} %fusion.9), channel_id=1, source_target_pairs={{0,1},{1,0},{2,3},{3,2},{4,5},{5,4},{6,7},{7,6},{8,9},{9,8},{10,11... | collective-permute-start | bytes 3145736 | tf_op jit(solution)/shard_map/ppermute | solution.py:119
  123.2 33.8 %all-to-all-start = ((bf16[16,8,4096]{2,1,0:T(8,128)(2,1)}), bf16[16,8,4096]{2,1,0:T(8,128)(2,1)S(1)}, u32[]{:S(2)}, u32[]{:S(2)}) async-start(bf16[16,8,4096]{2,1,0:T(8,128)(2,1)} %fusion.43), calls=%async_computation | async-start | bytes 2097152 | tf_op jit(solution)/shard_map/all_to_all | solution.py:122
  131.6 34.9 %copy-start.4 = (s32[1,2,8,2]{2,3,1,0:T(2,128)S(1)}, s32[1,2,8,2]{2,3,1,0:T(2,128)}, u32[]{:S(2)}) copy-start(s32[1,2,8,2]{2,3,1,0:T(2,128)} %param.15) | copy-start | bytes 388
  157.0 1.0 copy-start.2
  161.4 32.4 %all-to-all-start.1 = ((bf16[16,8,4096]{2,1,0:T(8,128)(2,1)}), bf16[16,8,4096]{2,1,0:T(8,128)(2,1)}, u32[]{:S(2)}, u32[]{:S(2)}) async-start(bf16[16,8,4096]{2,1,0:T(8,128)(2,1)} %shard_map.95), calls=%async_computation.1 | async-start | bytes 2097152 | tf_op jit(solution)/shard_map/all_to_all | solution.py:126
Sparse Core Ops, SparseCore 0:
  9.9 55.0 all-gather.2
  87.4 55.1 reduce-scatter.1

commit v2 on v1

v2 whole, which is shorter than its diff:
```python
import jax
import jax.numpy as jnp
from jax import lax
from jax.experimental import pallas as pl
from jax.experimental.pallas import tpu as pltpu
from jax.sharding import PartitionSpec as P

HD = 128
BLOCK = 128
EPS = 1e-05
MIB = 1024 * 1024
TILE = 1024
HALF_TILES = 4
THEIRS, MINE, STAGE = 16, 17, 18

NT = (((1,), (1,)), ((), ()))
NN = (((1,), (0,)), ((), ()))
TN = (((0,), (0,)), ((), ()))


def dot(a, b, dims):
    return lax.dot_general(a, b, dims, preferred_element_type=jnp.float32)


def cost(flops, nbytes, transcendentals=0):
    return pl.CostEstimate(
        flops=int(flops), bytes_accessed=int(nbytes), transcendentals=int(transcendentals)
    )


def stacked(ref, group, count):
    base = group * count
    return jnp.concatenate([ref[:, (base + h) * HD : (base + h + 1) * HD] for h in range(count)], 0)


def add_rows(shards_ref, normed_ref, pieces, whole_ref, sems, first, total):
    depth = pieces[0].shape[0]
    copies = []
    for i, piece in enumerate(pieces):
        rows = pl.ds(pl.multiple_of(shards_ref[first + i] * depth, depth), depth)
        copy = pltpu.make_async_copy(piece, whole_ref.at[rows, :], sems.at[i])
        copy.start()
        copies.append(copy)
    for i, piece in enumerate(pieces):
        columns = pl.ds(pl.multiple_of(shards_ref[first + i] * depth, depth), depth)
        part = dot(normed_ref[:, columns], piece[...], NN)
        total = part if total is None else total + part
    return total, copies


def in_vmem(count):
    return [pl.BlockSpec(memory_space=pltpu.VMEM)] * count


IN_SMEM = pl.BlockSpec(memory_space=pltpu.SMEM)
ANYWHERE = pl.BlockSpec(memory_space=pl.ANY)


def places_kernel(out_ref):
    me = lax.axis_index("dp")
    tensor_pos = lax.axis_index("tensor")
    before, after, across = lax.rem(me + 6, 8), lax.rem(me + 2, 8), lax.rem(me + 4, 8)
    order = (me, before, me, after, after, across, before, across)
    for i, shard in enumerate(order):
        out_ref[2 * i] = shard
        out_ref[2 * i + 1] = shard + 1 - 2 * lax.rem(shard, 2)
    out_ref[THEIRS] = (1 - tensor_pos) * HALF_TILES
    out_ref[MINE] = tensor_pos * HALF_TILES
    out_ref[STAGE] = lax.axis_index("pipe")


def all_places():
    return pl.pallas_call(
        places_kernel,
        out_specs=IN_SMEM,
        out_shape=jax.ShapeDtypeStruct((32,), jnp.int32),
        compiler_params=pltpu.CompilerParams(vmem_limit_bytes=MIB),
        cost_estimate=cost(0, 0),
    )()


def normed_kernel(x_ref, gain_ref, normed_ref, rms_ref):
    x = x_ref[...].astype(jnp.float32)
    rms = lax.rsqrt(jnp.mean(x * x, -1, keepdims=True) + EPS)
    rms_ref[...] = rms
    normed_ref[...] = ((x * rms) * gain_ref[...].astype(jnp.float32)).astype(jnp.bfloat16)


def norm(x, gain):
    tokens, features = x.shape
    rows = min(tokens, 32)
    return pl.pallas_call(
        normed_kernel,
        grid=(tokens // rows,),
        in_specs=[
            pl.BlockSpec((rows, features), lambda i: (i, 0)),
            pl.BlockSpec((1, features), lambda i: (0, 0)),
        ],
        out_specs=[
            pl.BlockSpec((rows, features), lambda i: (i, 0)),
            pl.BlockSpec((rows, 1), lambda i: (i, 0)),
        ],
        out_shape=(
            jax.ShapeDtypeStruct(x.shape, jnp.bfloat16),
            jax.ShapeDtypeStruct((tokens, 1), jnp.float32),
        ),
        compiler_params=pltpu.CompilerParams(vmem_limit_bytes=12 * MIB),
        cost_estimate=cost(4 * x.size, 4 * x.size),
    )(x, gain)


def early_kernel(shards_ref, normed_ref, both_ref, *refs, count):
    key_pieces, value_pieces = list(refs[: count - 1]), list(refs[count - 1 : 2 * count - 2])
    key_pieces.insert(1, both_ref.at[0])
    value_pieces.insert(1, both_ref.at[1])
    key_ref, value_ref, key_w_ref, value_w_ref, key_sems, value_sems = refs[2 * count - 2 :]
    key_f, copies = add_rows(shards_ref, normed_ref, key_pieces, key_w_ref, key_sems, 0, None)
    value_f, more = add_rows(
        shards_ref, normed_ref, value_pieces, value_w_ref, value_sems, count, None
    )
    key_ref[...] = key_f
    value_ref[...] = value_f
    for copy in copies + more:
        copy.wait()


def early_rows(shards, normed, both, key_pieces, value_pieces):
    tokens, features = normed.shape
    depth, width = key_pieces[0].shape
    count = len(key_pieces) + 1
    rows = jax.ShapeDtypeStruct((tokens, width), jnp.float32)
    whole = jax.ShapeDtypeStruct((features, width), jnp.bfloat16)
    return pl.pallas_call(
        lambda *refs: early_kernel(*refs, count=count),
        in_specs=[IN_SMEM] + in_vmem(2 * count),
        out_specs=in_vmem(2) + [ANYWHERE] * 2,
        out_shape=(rows, rows, whole, whole),
        scratch_shapes=[pltpu.SemaphoreType.DMA((count,))] * 2,
        compiler_params=pltpu.CompilerParams(vmem_limit_bytes=16 * MIB),
        cost_estimate=cost(4 * tokens * depth * width * count, 8 * depth * width * count),
    )(shards, normed, both, *key_pieces, *value_pieces)


def attention_kernel(shards_ref, normed_ref, *refs, count, first, features):
    key_pieces, value_pieces = refs[:count], refs[count : 2 * count]
    key_part_ref, value_part_ref, _, _, query_ref, grad_ref, seg_ref = refs[
        2 * count : 2 * count + 7
    ]
    key_w_ref, value_w_ref, key_grad_ref, value_grad_ref, inner_ref, key_sems, value_sems = refs[
        2 * count + 7 :
    ]
    key_f, copies = add_rows(
        shards_ref, normed_ref, key_pieces, key_w_ref, key_sems, first, key_part_ref[...]
    )
    value_f, more = add_rows(
        shards_ref, normed_ref, value_pieces, value_w_ref, value_sems, first + count, value_part_ref[...]
    )
    tokens = query_ref.shape[0]
    width = key_f.shape[1]
    group_size = query_ref.shape[1] // width
    key_pos = lax.broadcasted_iota(jnp.int32, (tokens, tokens), 0)
    query_pos = lax.broadcasted_iota(jnp.int32, (tokens, tokens), 1)
    by_query = jnp.broadcast_to(seg_ref[...].astype(jnp.float32), (tokens, tokens))
    allowed = (key_pos <= query_pos) & (by_query.T == by_query)
    allowed = jnp.concatenate([jnp.where(allowed, 1.0, 0.0)] * group_size, 1) > 0.5
    total = jnp.zeros(inner_ref.shape, jnp.float32)
    for j in range(width // HD):
        at = slice(j * HD, (j + 1) * HD)
        key_j, value_j = key_f[:, at], value_f[:, at]
        query_j = stacked(query_ref, j, group_size)
        grad_j = stacked(grad_ref, j, group_size)
        scores = dot(key_j.astype(jnp.bfloat16), query_j, NT) * (HD ** (-0.5))
        scores = jnp.where(allowed, scores, jnp.float32(-1e30))
        weight = jnp.exp(scores - jnp.max(scores, 0, keepdims=True))
        probability = weight / jnp.sum(weight, 0, keepdims=True)
        value_grad = dot(probability.astype(jnp.bfloat16), grad_j, NN).astype(jnp.bfloat16)
        dprob = dot(value_j.astype(jnp.bfloat16), grad_j, NT)
        delta = jnp.sum(probability * dprob, 0, keepdims=True)
        dscore_b = (probability * (dprob - delta)).astype(jnp.bfloat16)
        key_grad = (dot(dscore_b, query_j, NN) * (HD ** (-0.5))).astype(jnp.bfloat16)
        key_grad_ref[:, at] = key_grad
        value_grad_ref[:, at] = value_grad
        total = total + jnp.sum(
            key_grad.astype(jnp.float32) * key_j + value_grad.astype(jnp.float32) * value_j,
            1,
            keepdims=True,
        )
    inner_ref[...] = total / features
    for copy in copies + more:
        copy.wait()


def attention_grads(shards, first, normed, key_pieces, value_pieces, early, query, grad_out, segments):
    tokens, features = normed.shape
    depth, width = key_pieces[0].shape
    count = len(key_pieces)
    whole = jax.ShapeDtypeStruct((features, width), jnp.bfloat16)
    grads = jax.ShapeDtypeStruct((tokens, width), jnp.bfloat16)
    at = 2 * count + 4
    return pl.pallas_call(
        lambda *refs: attention_kernel(*refs, count=count, first=first, features=features),
        in_specs=[IN_SMEM] + in_vmem(2 * count + 3) + [ANYWHERE] * 2 + in_vmem(3),
        out_specs=[ANYWHERE] * 2 + in_vmem(3),
        out_shape=(whole, whole, grads, grads, jax.ShapeDtypeStruct((tokens, 1), jnp.float32)),
        input_output_aliases={at: 0, at + 1: 1},
        scratch_shapes=[pltpu.SemaphoreType.DMA((count,))] * 2,
        compiler_params=pltpu.CompilerParams(vmem_limit_bytes=20 * MIB),
        cost_estimate=cost(
            4 * tokens * depth * width * count + 8 * tokens * query.size,
            8 * depth * width * count + 4 * query.size,
            tokens * query.size // HD,
        ),
    )(shards, normed, *key_pieces, *value_pieces, *early, query, grad_out, segments)


def ordered_kernel(*refs):
    del refs


def ordered(arrays, after):
    count = len(arrays)
    return pl.pallas_call(
        ordered_kernel,
        in_specs=[ANYWHERE] * (count + 1),
        out_specs=[ANYWHERE] * count,
        out_shape=[jax.ShapeDtypeStruct(a.shape, a.dtype) for a in arrays],
        input_output_aliases={i: i for i in range(count)},
        compiler_params=pltpu.CompilerParams(vmem_limit_bytes=MIB),
        cost_estimate=cost(0, 0),
    )(*arrays, after)


def branch_kernel(
    at_ref, key_grad_ref, value_grad_ref, key_w_ref, value_w_ref, x_ref, gain_ref, rms_ref, inner_ref, out_ref
):
    d_normed = dot(key_grad_ref[...], key_w_ref[...], NT)
    d_normed = d_normed + dot(value_grad_ref[...], value_w_ref[...], NT)
    rms = rms_ref[...]
    x_hat = x_ref[...].astype(jnp.float32) * rms
    gated = gain_ref[...].astype(jnp.float32) * d_normed
    out_ref[...] = (rms * (gated - x_hat * inner_ref[...])).astype(out_ref.dtype)


def partial_branch(places, half, kind, key_grad, value_grad, key_w, value_w, x, gain, inv_rms, inner):
    tokens, columns = key_grad.shape
    tile, width = TILE, TILE * HALF_TILES
    whole = lambda i, at: (0, 0)
    rows = lambda i, at: (at[half] + i, 0)
    lanes = lambda i, at: (0, at[half] + i)
    return pl.pallas_call(
        branch_kernel,
        grid_spec=pltpu.PrefetchScalarGridSpec(
            num_scalar_prefetch=1,
            grid=(width // tile,),
            in_specs=[
                pl.BlockSpec((tokens, columns), whole),
                pl.BlockSpec((tokens, columns), whole),
                pl.BlockSpec((tile, columns), rows),
                pl.BlockSpec((tile, columns), rows),
                pl.BlockSpec((tokens, tile), lanes),
                pl.BlockSpec((1, tile), lanes),
                pl.BlockSpec((tokens, 1), whole),
                pl.BlockSpec((tokens, 1), whole),
            ],
            out_specs=pl.BlockSpec((tokens, tile), lambda i, at: (0, i)),
        ),
        out_shape=jax.ShapeDtypeStruct((tokens, width), kind),
        compiler_params=pltpu.CompilerParams(vmem_limit_bytes=8 * MIB),
        cost_estimate=cost(
            4 * tokens * width * columns, 4 * width * columns + 2 * width * tokens
        ),
    )(places, key_grad, value_grad, key_w, value_w, x, gain, inv_rms, inner)


def weight_part_kernel(normed_ref, key_grad_ref, value_grad_ref, after_ref, out_ref, token_ref):
    columns = key_grad_ref.shape[1]
    normed = normed_ref[...]
    out_ref[:, :columns] = dot(normed, key_grad_ref[...], TN).astype(out_ref.dtype)
    out_ref[:, columns:] = dot(normed, value_grad_ref[...], TN).astype(out_ref.dtype)
    token_ref[...] = jnp.zeros_like(token_ref)


def weight_part(normed, key_grad, value_grad, after):
    tokens, features = normed.shape
    columns = key_grad.shape[1]
    return pl.pallas_call(
        weight_part_kernel,
        grid=(features // TILE,),
        in_specs=[
            pl.BlockSpec((tokens, TILE), lambda i: (0, i)),
            pl.BlockSpec((tokens, columns), lambda i: (0, 0)),
            pl.BlockSpec((tokens, columns), lambda i: (0, 0)),
            ANYWHERE,
        ],
        out_specs=[
            pl.BlockSpec((TILE, 2 * columns), lambda i: (i, 0)),
            pl.BlockSpec((8, 128), lambda i: (0, 0)),
        ],
        out_shape=(
            jax.ShapeDtypeStruct((features, 2 * columns), jnp.bfloat16),
            jax.ShapeDtypeStruct((8, 128), jnp.float32),
        ),
        compiler_params=pltpu.CompilerParams(vmem_limit_bytes=8 * MIB),
        cost_estimate=cost(4 * tokens * features * columns, 4 * features * columns),
    )(normed, key_grad, value_grad, after)


def add_kernel(mine_ref, arrived_ref, token_ref, out_ref):
    out_ref[...] = (mine_ref[...] + arrived_ref[...].astype(jnp.float32)).astype(out_ref.dtype)


def add_halves(mine, arrived, token):
    tokens, width = mine.shape
    spec = pl.BlockSpec((tokens, TILE), lambda i: (0, i))
    return pl.pallas_call(
        add_kernel,
        grid=(width // TILE,),
        in_specs=[spec, spec, ANYWHERE],
        out_specs=spec,
        out_shape=jax.ShapeDtypeStruct(mine.shape, jnp.bfloat16),
        compiler_params=pltpu.CompilerParams(vmem_limit_bytes=8 * MIB),
        cost_estimate=cost(mine.size, 8 * mine.size),
    )(mine, arrived, token)


def copy_kernel(at_ref, in_ref, out_ref):
    out_ref[...] = in_ref[...]


def take_rows(places, array, rows):
    width = array.shape[1]
    return pl.pallas_call(
        copy_kernel,
        grid_spec=pltpu.PrefetchScalarGridSpec(
            num_scalar_prefetch=1,
            grid=(1,),
            in_specs=[pl.BlockSpec((rows, width), lambda i, at: (at[STAGE], 0))],
            out_specs=pl.BlockSpec((rows, width), lambda i, at: (0, 0)),
        ),
        out_shape=jax.ShapeDtypeStruct((rows, width), array.dtype),
        compiler_params=pltpu.CompilerParams(vmem_limit_bytes=MIB),
        cost_estimate=cost(0, 0),
    )(places, array)


def suffix_kernel(parts_ref, top_ref, out_ref):
    running = top_ref[...].astype(jnp.float32)
    for layer in reversed(range(parts_ref.shape[0])):
        running = running + parts_ref[layer].astype(jnp.float32)
        out_ref[layer] = running.astype(jnp.bfloat16)


def suffix_sum(parts, top):
    layers, rows, width = parts.shape
    tile = min(width, 1024)
    return pl.pallas_call(
        suffix_kernel,
        grid=(width // tile,),
        in_specs=[
            pl.BlockSpec((layers, rows, tile), lambda i: (0, 0, i)),
            pl.BlockSpec((rows, tile), lambda i: (0, i)),
        ],
        out_specs=pl.BlockSpec((layers, rows, tile), lambda i: (0, 0, i)),
        out_shape=jax.ShapeDtypeStruct(parts.shape, jnp.bfloat16),
        compiler_params=pltpu.CompilerParams(vmem_limit_bytes=8 * MIB),
        cost_estimate=cost(1e15, 1e12),
    )(parts, top)


def scale_kernel(factor_ref, summed_ref, out_ref):
    p = pl.program_id(0)
    for i in range(out_ref.shape[1] // BLOCK):
        for c in range(out_ref.shape[2] // HD):
            block = summed_ref[i * BLOCK : (i + 1) * BLOCK, c * HD : (c + 1) * HD]
            scaled = block.astype(jnp.float32) * factor_ref[p, i, c]
            out_ref[0, i * BLOCK : (i + 1) * BLOCK, c * HD : (c + 1) * HD] = scaled.astype(jnp.bfloat16)


def scaled_grad(summed, factor):
    rows = summed.shape[0]
    columns = summed.shape[1] // 2
    return pl.pallas_call(
        scale_kernel,
        grid=(2,),
        in_specs=[
            pl.BlockSpec(memory_space=pltpu.SMEM),
            pl.BlockSpec((rows, columns), lambda p: (0, p)),
        ],
        out_specs=pl.BlockSpec((1, rows, columns), lambda p: (p, 0, 0)),
        out_shape=jax.ShapeDtypeStruct((2, rows, columns), jnp.bfloat16),
        compiler_params=pltpu.CompilerParams(vmem_limit_bytes=8 * MIB),
        cost_estimate=cost(summed.size, 4 * summed.size),
    )(factor, summed)


def ring_pairs(count):
    right = [(i, (i + 2) % count) for i in range(count)]
    left = [(i, (i - 2) % count) for i in range(count)]
    other = [(i, i ^ 1) for i in range(count)]
    return right, left, other


def on_device(
    layer_input, norm_gain, kv_weight, queries, out_grad, top_grad, segment_ids, scale_exp
):
    inputs = layer_input[0]
    token_count, feature_count = inputs.shape
    pipe_count = lax.axis_size("pipe")
    right, left, other = ring_pairs(lax.axis_size("dp"))
    send = lambda piece, pairs: lax.ppermute(piece, "dp", pairs)
    key_own, value_own = kv_weight[0, 0], kv_weight[0, 1]
    key_l = send(key_own, right)
    value_r = send(value_own, left)
    both = send(kv_weight[0], other)
    key_r = send(key_own, left)
    value_l = send(value_own, right)
    key_2 = send(key_l, right)
    value_2 = send(value_r, left)

    places = all_places()
    normed, inv_rms = norm(inputs, norm_gain)
    early = early_rows(
        places,
        normed,
        both,
        [key_own, key_l, send(key_l, other)],
        [value_own, value_r, send(value_r, other)],
    )
    key_r, value_l = ordered((key_r, value_l), early[0])
    key_w, value_w, key_grad, value_grad, inner = attention_grads(
        places,
        8,
        normed,
        [key_r, send(key_r, other), key_2, send(key_2, other)],
        [value_l, send(value_l, other), value_2, send(value_2, other)],
        early,
        queries[0],
        out_grad[0],
        segment_ids[None, :],
    )

    def share(half, kind):
        return partial_branch(
            places, half, kind, key_grad, value_grad, key_w, value_w, inputs, norm_gain, inv_rms, inner
        )

    arrived = lax.ppermute(share(THEIRS, jnp.bfloat16), "tensor", [(0, 1), (1, 0)])
    mine = share(MINE, jnp.float32)
    part, token = weight_part(normed, key_grad, value_grad, mine)
    branch = add_halves(mine, arrived, token)
    parts = lax.all_to_all(branch, "pipe", 0, 0, tiled=True)
    rows = token_count // pipe_count
    sums = suffix_sum(
        parts.reshape(pipe_count, rows, branch.shape[1]), take_rows(places, top_grad, rows)
    )
    input_grad = lax.all_to_all(
        sums.reshape(token_count, branch.shape[1]), "pipe", 0, 0, tiled=True
    )

    summed = lax.psum_scatter(part, "dp", scatter_dimension=0, tiled=True)
    weight_grad = scaled_grad(summed, jnp.exp2(-scale_exp[0].astype(jnp.float32)))
    return (input_grad[None], weight_grad[None])


def solution(mesh):
    placed = (
        P("pipe", "dp", None),
        P("pipe", None),
        P("pipe", None, "dp", "tensor"),
        P("pipe", "dp", "tensor"),
        P("pipe", "dp", "tensor"),
        P("dp", "tensor"),
        P("dp"),
        P("pipe", None, "dp", "tensor"),
    )
    return jax.shard_map(
        on_device,
        mesh=mesh,
        in_specs=placed,
        out_specs=(P("pipe", "dp", "tensor"), P("pipe", None, "dp", "tensor")),
        check_vma=False,
    )
```

time: 207 us -> 170 us (0.82)
  matrix products: 27 us -> 0 us
  waiting for transfers between devices: 123 us -> 98.2 us
  Pallas kernels: 3.42 us -> 23 us
  starting transfers between devices: 13.5 us -> 24.9 us
  local copies, waits for them, and re-layouts: 19.1 us -> 9.2 us
  other arithmetic: 5.27 us -> 0.01 us
    all_gather x1 -> x0, waiting for transfers between devices: 51.5 us -> none  [on_device(): weights = lax.all_gather(kv_weight[0], 'dp', axis=1, tiled=True)]
    dot_general x10 -> x0, matrix products: 24.5 us -> none  [the longest x1 5.69 us: on_device(): jnp.einsum('tr,tc->rc', normed, grads_b, preferred_element_type=jnp.float32)]
    pallas_call x0 -> x11, Pallas kernels: none -> 21.3 us  [the longest x2 5.51 us: partial_branch(): pl.pallas_call(branch_kernel, grid_spec=pltpu.PrefetchScalarGridSpec(num_...]
    ppermute x1 -> x14, waiting for transfers between devices: 25.5 us -> 46 us  [the longest x13 29.5 us: on_device(): send = lambda piece, pairs: lax.ppermute(piece, 'dp', pairs)]
    ppermute x1 -> x14, starting transfers between devices: 0.61 us -> 10.3 us  [the longest x13 10 us: on_device(): send = lambda piece, pairs: lax.ppermute(piece, 'dp', pairs)]
    all_to_all x1, waiting for transfers between devices: 20.4 us -> 27.2 us  [on_device(): lax.all_to_all(sums.reshape(token_count, branch.shape[1]), 'pipe', 0, 0,...]
    unnamed x11 -> x23, local copies, waits for them, and re-layouts: 3.28 us -> 7.84 us
    another operation x3 -> x0, local copies, waits for them, and re-layouts: 4.22 us -> none  [the longest x1 2.05 us: attend(): query_h = query.reshape(count, kv_local, group_size, HD)]
  transfers between devices with their start and end apart: 5 -> 17, of which waited for: 4 -> 9; matrix products, arithmetic and copies ran while one was open for 11% -> 0% of each run, Pallas kernels for 2% -> 8%
where the time goes in v2:
time: 170 us
  waiting for transfers between devices  98.2 us (58%)
  starting transfers between devices  24.9 us (15%)
  Pallas kernels  23 us (14%)
  between operations  14.2 us (8%)
  local copies, waits for them, and re-layouts  9.2 us (5%)
    ppermute x13, waiting for transfers between devices, on_device(): send = lambda piece, pairs: lax.ppermute(piece, 'dp', pairs)  29.5 us
    all_to_all x1, waiting for transfers between devices, on_device(): lax.all_to_all(sums.reshape(token_count, branch.shape[1]), 'pipe', 0, 0,...  27.2 us
    all_to_all x1, waiting for transfers between devices, on_device(): parts = lax.all_to_all(branch, 'pipe', 0, 0, tiled=True)  25 us
    ppermute x1, waiting for transfers between devices, on_device(): lax.ppermute(share(THEIRS, jnp.bfloat16), 'tensor', [(0, 1), (1, 0)])  16.5 us
    ppermute x13, starting transfers between devices, on_device(): send = lambda piece, pairs: lax.ppermute(piece, 'dp', pairs)  10 us
    all_to_all x1, starting transfers between devices, on_device(): parts = lax.all_to_all(branch, 'pipe', 0, 0, tiled=True)  9.29 us
    unnamed x23, local copies, waits for them, and re-layouts  7.84 us
    pallas_call x2, Pallas kernels, partial_branch(): pl.pallas_call(branch_kernel, grid_spec=pltpu.PrefetchScalarGridSpec(num_...  5.51 us
  transfers between devices with their start and end apart: 17, of which 9 were waited for; matrix products, arithmetic and copies ran while one was open for 0% of the time, Pallas kernels for 8%

profile of v2, /device:TPU:16, one launch (start us, length us, event | category | flops | bytes accessed | tf_op | source)
XLA Modules:
  0.0 169.6 jit_solution(4306249928598895931)
XLA Ops:
  7.2 1.3 slice_bitcast_fusion
  8.4 1.6 collective-permute-start.3
  10.0 1.7 %collective-permute-start.5 = (bf16[1024,256]{1,0:T(8,128)(2,1)S(1)}, bf16[1024,256]{1,0:T(8,128)(2,1)S(1)}, u32[]{:S(2)}, u32[]{:S(2)}) collective-permute-start(bf16[1024,256]{1,0:T(8,128)(2,1)S(1)} %get-tuple-element.32.refs_6_), channel_id=1, source_target_pairs={{0,12},{2,14},{4,0},{6,2},{8,4},{10,6},{12,8},{14,10},{1,13},{3,15... | collective-permute-start | bytes 1572872 | tf_op jit(solution)/shard_map/ppermute | solution.py:410
  11.8 11.6 %collective-permute-done.3.refs_4_ = bf16[1024,256]{1,0:T(8,128)(2,1)S(1)} collective-permute-done((bf16[1024,256]{1,0:T(8,128)(2,1)S(1)}, bf16[1024,256]{1,0:T(8,128)(2,1)S(1)}, u32[]{:S(2)}, u32[]{:S(2)}) %collective-permute-start.3) | collective-permute-done | bytes 524320 | tf_op jit(solution)/shard_map/ppermute | solution.py:410
  23.9 2.4 %collective-permute-start = (bf16[1024,256]{1,0:T(8,128)(2,1)S(1)}, bf16[1024,256]{1,0:T(8,128)(2,1)S(1)}, u32[]{:S(2)}, u32[]{:S(2)}) collective-permute-start(bf16[1024,256]{1,0:T(8,128)(2,1)S(1)} %get-tuple-element.33.refs_3_), channel_id=1, source_target_pairs={{0,12},{2,14},{4,0},{6,2},{8,4},{10,6},{12,8},{14,10},{1,13},{3,15... | collective-permute-start | bytes 1572872 | tf_op jit(solution)/shard_map/ppermute | solution.py:410
  26.4 3.2 %collective-permute-start.11 = (bf16[1024,256]{1,0:T(8,128)(2,1)S(1)}, bf16[1024,256]{1,0:T(8,128)(2,1)S(1)}, u32[]{:S(2)}, u32[]{:S(2)}) collective-permute-start(bf16[1024,256]{1,0:T(8,128)(2,1)S(1)} %collective-permute-done.5.refs_7_), channel_id=1, source_target_pairs={{0,12},{2,14},{4,0},{6,2},{8,4},{10,6},{12,8},{14,10},{1,13},{3,15... | collective-permute-start | bytes 1572872 | tf_op jit(solution)/shard_map/ppermute | solution.py:410
  29.6 0.6 shard_map.95.refs_0_.at_ref
  30.2 1.6 copy-done
  31.8 0.8 copy-done.7
  32.6 1.5 shard_map.96
  34.1 2.3 %shard_map.97 = (f32[128,256]{1,0:T(8,128)S(1)}, f32[128,256]{1,0:T(8,128)S(1)}, bf16[8192,256]{1,0:T(8,128)(2,1)S(1)}, bf16[8192,256]{1,0:T(8,128)(2,1)S(1)}) custom-call(s32[32]{0:T(128)S(1)} %shard_map.95.refs_0_.at_ref, bf16[128,8192]{1,0:T(8,128)(2,1)S(1)} %get-tuple-element.17.refs_1_.normed_ref, ...), custom_call_target="tpu_custom_call" | custom-call | flops 536870912 | bytes 8388608 | tf_op jit(solution)/shard_map/pallas_call | solution.py:133
  36.4 2.3 %collective-permute-done.refs_0_ = bf16[1024,256]{1,0:T(8,128)(2,1)S(1)} collective-permute-done((bf16[1024,256]{1,0:T(8,128)(2,1)S(1)}, bf16[1024,256]{1,0:T(8,128)(2,1)S(1)}, u32[]{:S(2)}, u32[]{:S(2)}) %collective-permute-start) | collective-permute-done | bytes 524320 | tf_op jit(solution)/shard_map/ppermute | solution.py:410
  38.7 3.6 %collective-permute-done.1.refs_1_ = bf16[1024,256]{1,0:T(8,128)(2,1)S(1)} collective-permute-done((bf16[1024,256]{1,0:T(8,128)(2,1)S(1)}, bf16[1024,256]{1,0:T(8,128)(2,1)S(1)}, u32[]{:S(2)}, u32[]{:S(2)}) %collective-permute-start.1) | collective-permute-done | bytes 524320 | tf_op jit(solution)/shard_map/ppermute | solution.py:410
  42.8 6.6 %collective-permute-done.11.refs_8_ = bf16[1024,256]{1,0:T(8,128)(2,1)S(1)} collective-permute-done((bf16[1024,256]{1,0:T(8,128)(2,1)S(1)}, bf16[1024,256]{1,0:T(8,128)(2,1)S(1)}, u32[]{:S(2)}, u32[]{:S(2)}) %collective-permute-start.11) | collective-permute-done | bytes 524320 | tf_op jit(solution)/shard_map/ppermute | solution.py:410
  49.4 3.4 %collective-permute-done.8.refs_4_ = bf16[1024,256]{1,0:T(8,128)(2,1)S(1)} collective-permute-done((bf16[1024,256]{1,0:T(8,128)(2,1)S(1)}, bf16[1024,256]{1,0:T(8,128)(2,1)S(1)}, u32[]{:S(2)}, u32[]{:S(2)}) %collective-permute-start.8) | collective-permute-done | bytes 524320 | tf_op jit(solution)/shard_map/ppermute | solution.py:410
  52.9 1.9 %collective-permute-done.9.refs_5_ = bf16[1024,256]{1,0:T(8,128)(2,1)S(1)} collective-permute-done((bf16[1024,256]{1,0:T(8,128)(2,1)S(1)}, bf16[1024,256]{1,0:T(8,128)(2,1)S(1)}, u32[]{:S(2)}, u32[]{:S(2)}) %collective-permute-start.9) | collective-permute-done | bytes 524320 | tf_op jit(solution)/shard_map/ppermute | solution.py:410
  54.8 3.5 %shard_map.99 = (bf16[8192,256]{1,0:T(8,128)(2,1)S(1)}, bf16[8192,256]{1,0:T(8,128)(2,1)S(1)}, bf16[128,256]{1,0:T(8,128)(2,1)S(1)}, bf16[128,256]{1,0:T(8,128)(2,1)S(1)}, f32[128,1]{1,0:T(8,128)S(1)}) custom-call(s32[32]{0:T(128)S(1)} %shard_map.95.refs_0_.at_ref, ...), custom_call_target="tpu_custom_call", output_to_operand_aliasing={{0}: (12, {}), {1}: (13, {})} | custom-call | flops 805306368 | bytes 9437184 | tf_op jit(solution)/shard_map/pallas_call | solution.py:200
  58.3 2.7 %shard_map.101 = bf16[128,4096]{1,0:T(8,128)(2,1)S(1)} custom-call(s32[32]{0:T(128)S(1)} %shard_map.95.refs_0_.at_ref, bf16[128,256]{1,0:T(8,128)(2,1)S(1)} %get-tuple-element.24.key_grad_ref, bf16[128,256]{1,0:T(8,128)(2,1)S(1)} %get-tuple-element.25.value_grad_ref, bf16[8192,256]{1,0:T(8,128)(2,1)S(1)} %get-tuple-element.26.key_w_ref, ...), custom_call_target="tpu_custom_call" | custom-call | flops 536870912 | bytes 5242880 | tf_op jit(solution)/shard_map/pallas_call | solution.py:250
  61.3 2.8 %shard_map.100.after_ref.mine_ref = f32[128,4096]{1,0:T(8,128)S(1)} custom-call(s32[32]{0:T(128)S(1)} %shard_map.95.refs_0_.at_ref, bf16[128,256]{1,0:T(8,128)(2,1)S(1)} %get-tuple-element.24.key_grad_ref, bf16[128,256]{1,0:T(8,128)(2,1)S(1)} %get-tuple-element.25.value_grad_ref, bf16[8192,256]{1,0:T(8,128)(2,1)S(1)} %get-tuple-element.26.key_w_ref, ...), custom_call_target="tpu_custom_call" | custom-call | flops 536870912 | bytes 5242880 | tf_op jit(solution)/shard_map/pallas_call | solution.py:250
  64.1 3.9 %shard_map.102 = (bf16[8192,512]{1,0:T(8,128)(2,1)S(1)}, f32[8,128]{1,0:T(8,128)S(1)}) custom-call(bf16[128,8192]{1,0:T(8,128)(2,1)S(1)} %get-tuple-element.17.refs_1_.normed_ref, bf16[128,256]{1,0:T(8,128)(2,1)S(1)} %get-tuple-element.24.key_grad_ref, bf16[128,256]{1,0:T(8,128)(2,1)S(1)} %get-tuple-element.25.value_grad_ref, ...), custom_call_target="tpu_custom_call" | custom-call | flops 1073741824 | bytes 8388608 | tf_op jit(solution)/shard_map/pallas_call | solution.py:286
  68.0 3.3 %copy-done.2 = bf16[8192,512]{1,0:T(8,128)(2,1)} copy-done((bf16[8192,512]{1,0:T(8,128)(2,1)}, bf16[8192,512]{1,0:T(8,128)(2,1)S(1)}, u32[]{:S(2)}) %copy-start.2) | copy-done | bytes 8388632
  71.3 16.5 %collective-permute-done.13.arrived_ref = bf16[128,4096]{1,0:T(8,128)(2,1)S(1)} collective-permute-done((bf16[128,4096]{1,0:T(8,128)(2,1)S(1)}, bf16[128,4096]{1,0:T(8,128)(2,1)S(1)}, u32[]{:S(2)}, u32[]{:S(2)}) %collective-permute-start.13) | collective-permute-done | bytes 1048608 | tf_op jit(solution)/shard_map/ppermute | solution.py:447
  87.8 1.8 %shard_map.103 = bf16[128,4096]{1,0:T(8,128)(2,1)} custom-call(f32[128,4096]{1,0:T(8,128)S(1)} %shard_map.100.after_ref.mine_ref, bf16[128,4096]{1,0:T(8,128)(2,1)S(1)} %collective-permute-done.13.arrived_ref, f32[8,128]{1,0:T(8,128)S(1)} %get-tuple-element.30.token_ref), custom_call_target="tpu_custom_call" | custom-call | flops 524288 | bytes 4194304 | tf_op jit(solution)/shard_map/pallas_call | solution.py:315
  89.6 9.3 %all-to-all-start = ((bf16[16,8,4096]{2,1,0:T(8,128)(2,1)}), bf16[16,8,4096]{2,1,0:T(8,128)(2,1)S(1)}, u32[]{:S(2)}, u32[]{:S(2)}) async-start(bf16[16,8,4096]{2,1,0:T(8,128)(2,1)} %bitcast.7), calls=%async_computation | async-start | bytes 2097152 | tf_op jit(solution)/shard_map/all_to_all | solution.py:451
  98.9 0.6 shard_map.104.top_ref
  99.6 25.0 %all-to-all-done.parts_ref = bf16[16,8,4096]{2,1,0:T(8,128)(2,1)S(1)} async-done(((bf16[16,8,4096]{2,1,0:T(8,128)(2,1)}), bf16[16,8,4096]{2,1,0:T(8,128)(2,1)S(1)}, u32[]{:S(2)}, u32[]{:S(2)}) %all-to-all-start) | async-done | bytes 1048608 | tf_op jit(solution)/shard_map/all_to_all | solution.py:451
  124.6 1.7 shard_map.105
  126.2 5.2 %all-to-all-start.1 = ((bf16[16,8,4096]{2,1,0:T(8,128)(2,1)}), bf16[16,8,4096]{2,1,0:T(8,128)(2,1)S(1)}, u32[]{:S(2)}, u32[]{:S(2)}) async-start(bf16[16,8,4096]{2,1,0:T(8,128)(2,1)} %shard_map.105), calls=%async_computation.1 | async-start | bytes 2097152 | tf_op jit(solution)/shard_map/all_to_all | solution.py:456
  131.6 27.2 %all-to-all-done.1 = bf16[16,8,4096]{2,1,0:T(8,128)(2,1)S(1)} async-done(((bf16[16,8,4096]{2,1,0:T(8,128)(2,1)}), bf16[16,8,4096]{2,1,0:T(8,128)(2,1)S(1)}, u32[]{:S(2)}, u32[]{:S(2)}) %all-to-all-start.1) | async-done | bytes 1048608 | tf_op jit(solution)/shard_map/all_to_all | solution.py:456
  158.8 1.2 copy-done.4
  160.0 1.8 %shard_map.106 = bf16[2,1024,256]{2,1,0:T(8,128)(2,1)} custom-call(f32[2,8,2]{2,1,0:T(8,128)S(1)} %copy.14.factor_ref, bf16[1024,512]{1,0:T(8,128)(2,1)S(1)} %copy-done.4), custom_call_target="tpu_custom_call" | custom-call | flops 524288 | bytes 2097152 | tf_op jit(solution)/shard_map/pallas_call | solution.py:382
  161.8 1.0 copy.20
  (41 shorter events, 1.7 us)
Async XLA Ops:
  8.4 15.0 %collective-permute-start.3 = (bf16[1024,256]{1,0:T(8,128)(2,1)S(1)}, bf16[1024,256]{1,0:T(8,128)(2,1)S(1)}, u32[]{:S(2)}, u32[]{:S(2)}) collective-permute-start(bf16[1024,256]{1,0:T(8,128)(2,1)S(1)} %get-tuple-element.33.refs_3_), channel_id=1, source_target_pairs={{0,4},{2,6},{4,8},{6,10},{8,12},{10,14},{12,0},{14,2},{1,5},{3,7},... | collective-permute-start | bytes 1572872 | tf_op jit(solution)/shard_map/ppermute | solution.py:410
  10.0 13.4 %collective-permute-start.5 = (bf16[1024,256]{1,0:T(8,128)(2,1)S(1)}, bf16[1024,256]{1,0:T(8,128)(2,1)S(1)}, u32[]{:S(2)}, u32[]{:S(2)}) collective-permute-start(bf16[1024,256]{1,0:T(8,128)(2,1)S(1)} %get-tuple-element.32.refs_6_), channel_id=1, source_target_pairs={{0,12},{2,14},{4,0},{6,2},{8,4},{10,6},{12,8},{14,10},{1,13},{3,15... | collective-permute-start | bytes 1572872 | tf_op jit(solution)/shard_map/ppermute | solution.py:410
  11.8 22.3 %collective-permute-start.2 = (bf16[2,1024,256]{2,1,0:T(8,128)(2,1)}, bf16[2,1024,256]{2,1,0:T(8,128)(2,1)S(1)}, u32[]{:S(2)}, u32[]{:S(2)}) collective-permute-start(bf16[2,1024,256]{2,1,0:T(8,128)(2,1)} %bitcast.21), channel_id=1, source_target_pairs={{0,2},{2,0},{4,6},{6,4},{8,10},{10,8},{12,14},{14,12},{1,3},{3,1},... | collective-permute-start | bytes 3145736 | tf_op jit(solution)/shard_map/ppermute | solution.py:410
  23.4 3.0 %collective-permute-start.4 = (bf16[1024,256]{1,0:T(8,128)(2,1)S(1)}, bf16[1024,256]{1,0:T(8,128)(2,1)S(1)}, u32[]{:S(2)}, u32[]{:S(2)}) collective-permute-start(bf16[1024,256]{1,0:T(8,128)(2,1)S(1)} %collective-permute-done.3.refs_4_), channel_id=1, source_target_pairs={{0,2},{2,0},{4,6},{6,4},{8,10},{10,8},{12,14},{14,12},{1,3},{3,1},... | collective-permute-start | bytes 1572872 | tf_op jit(solution)/shard_map/ppermute | solution.py:410
  23.4 6.2 %collective-permute-start.6 = (bf16[1024,256]{1,0:T(8,128)(2,1)S(1)}, bf16[1024,256]{1,0:T(8,128)(2,1)S(1)}, u32[]{:S(2)}, u32[]{:S(2)}) collective-permute-start(bf16[1024,256]{1,0:T(8,128)(2,1)S(1)} %collective-permute-done.5.refs_7_), channel_id=1, source_target_pairs={{0,2},{2,0},{4,6},{6,4},{8,10},{10,8},{12,14},{14,12},{1,3},{3,1},... | collective-permute-start | bytes 1572872 | tf_op jit(solution)/shard_map/ppermute | solution.py:410
  23.9 14.8 %collective-permute-start = (bf16[1024,256]{1,0:T(8,128)(2,1)S(1)}, bf16[1024,256]{1,0:T(8,128)(2,1)S(1)}, u32[]{:S(2)}, u32[]{:S(2)}) collective-permute-start(bf16[1024,256]{1,0:T(8,128)(2,1)S(1)} %get-tuple-element.33.refs_3_), channel_id=1, source_target_pairs={{0,12},{2,14},{4,0},{6,2},{8,4},{10,6},{12,8},{14,10},{1,13},{3,15... | collective-permute-start | bytes 1572872 | tf_op jit(solution)/shard_map/ppermute | solution.py:410
  26.4 16.0 %collective-permute-start.1 = (bf16[1024,256]{1,0:T(8,128)(2,1)S(1)}, bf16[1024,256]{1,0:T(8,128)(2,1)S(1)}, u32[]{:S(2)}, u32[]{:S(2)}) collective-permute-start(bf16[1024,256]{1,0:T(8,128)(2,1)S(1)} %get-tuple-element.32.refs_6_), channel_id=1, source_target_pairs={{0,4},{2,6},{4,8},{6,10},{8,12},{10,14},{12,0},{14,2},{1,5},{3,7},... | collective-permute-start | bytes 1572872 | tf_op jit(solution)/shard_map/ppermute | solution.py:410
  26.4 23.1 %collective-permute-start.11 = (bf16[1024,256]{1,0:T(8,128)(2,1)S(1)}, bf16[1024,256]{1,0:T(8,128)(2,1)S(1)}, u32[]{:S(2)}, u32[]{:S(2)}) collective-permute-start(bf16[1024,256]{1,0:T(8,128)(2,1)S(1)} %collective-permute-done.5.refs_7_), channel_id=1, source_target_pairs={{0,12},{2,14},{4,0},{6,2},{8,4},{10,6},{12,8},{14,10},{1,13},{3,15... | collective-permute-start | bytes 1572872 | tf_op jit(solution)/shard_map/ppermute | solution.py:410
  29.6 23.3 %collective-permute-start.8 = (bf16[1024,256]{1,0:T(8,128)(2,1)S(1)}, bf16[1024,256]{1,0:T(8,128)(2,1)S(1)}, u32[]{:S(2)}, u32[]{:S(2)}) collective-permute-start(bf16[1024,256]{1,0:T(8,128)(2,1)S(1)} %collective-permute-done.3.refs_4_), channel_id=1, source_target_pairs={{0,4},{2,6},{4,8},{6,10},{8,12},{10,14},{12,0},{14,2},{1,5},{3,7},... | collective-permute-start | bytes 1572872 | tf_op jit(solution)/shard_map/ppermute | solution.py:410
  30.2 1.6 copy-start
  31.8 0.8 copy-start.7
  34.0 20.7 %copy-start.5 = (bf16[1,128,2048]{2,1,0:T(8,128)(2,1)S(1)}, bf16[1,128,2048]{2,1,0:T(8,128)(2,1)}, u32[]{:S(2)}) copy-start(bf16[1,128,2048]{2,1,0:T(8,128)(2,1)} %param.11) | copy-start | bytes 1572868
  34.1 20.7 %copy-start.6 = (bf16[1,128,2048]{2,1,0:T(8,128)(2,1)S(1)}, bf16[1,128,2048]{2,1,0:T(8,128)(2,1)}, u32[]{:S(2)}) copy-start(bf16[1,128,2048]{2,1,0:T(8,128)(2,1)} %param.12) | copy-start | bytes 1572868
  34.1 20.7 %copy-start.9 = (s32[128]{0:T(128)S(1)}, s32[128]{0:T(128)}, u32[]{:S(2)}) copy-start(s32[128]{0:T(128)} %param.14) | copy-start | bytes 1540
  42.3 10.5 %collective-permute-start.10 = (bf16[1024,256]{1,0:T(8,128)(2,1)S(1)}, bf16[1024,256]{1,0:T(8,128)(2,1)S(1)}, u32[]{:S(2)}, u32[]{:S(2)}) collective-permute-start(bf16[1024,256]{1,0:T(8,128)(2,1)S(1)} %get-tuple-element.20.refs_6_), channel_id=1, source_target_pairs={{0,2},{2,0},{4,6},{6,4},{8,10},{10,8},{12,14},{14,12},{1,3},{3,1},... | collective-permute-start | bytes 1572872 | tf_op jit(solution)/shard_map/ppermute | solution.py:410
  42.3 10.5 %collective-permute-start.7 = (bf16[1024,256]{1,0:T(8,128)(2,1)S(1)}, bf16[1024,256]{1,0:T(8,128)(2,1)S(1)}, u32[]{:S(2)}, u32[]{:S(2)}) collective-permute-start(bf16[1024,256]{1,0:T(8,128)(2,1)S(1)} %get-tuple-element.19.refs_2_), channel_id=1, source_target_pairs={{0,2},{2,0},{4,6},{6,4},{8,10},{10,8},{12,14},{14,12},{1,3},{3,1},... | collective-permute-start | bytes 1572872 | tf_op jit(solution)/shard_map/ppermute | solution.py:410
  49.4 3.4 %collective-permute-start.12 = (bf16[1024,256]{1,0:T(8,128)(2,1)S(1)}, bf16[1024,256]{1,0:T(8,128)(2,1)S(1)}, u32[]{:S(2)}, u32[]{:S(2)}) collective-permute-start(bf16[1024,256]{1,0:T(8,128)(2,1)S(1)} %collective-permute-done.11.refs_8_), channel_id=1, source_target_pairs={{0,2},{2,0},{4,6},{6,4},{8,10},{10,8},{12,14},{14,12},{1,3},{3,1},... | collective-permute-start | bytes 1572872 | tf_op jit(solution)/shard_map/ppermute | solution.py:410
  52.9 1.9 %collective-permute-start.9 = (bf16[1024,256]{1,0:T(8,128)(2,1)S(1)}, bf16[1024,256]{1,0:T(8,128)(2,1)S(1)}, u32[]{:S(2)}, u32[]{:S(2)}) collective-permute-start(bf16[1024,256]{1,0:T(8,128)(2,1)S(1)} %collective-permute-done.8.refs_4_), channel_id=1, source_target_pairs={{0,2},{2,0},{4,6},{6,4},{8,10},{10,8},{12,14},{14,12},{1,3},{3,1},... | collective-permute-start | bytes 1572872 | tf_op jit(solution)/shard_map/ppermute | solution.py:410
  54.8 3.5 %copy-start.1 = (bf16[1,128,8192]{2,1,0:T(8,128)(2,1)S(1)}, bf16[1,128,8192]{2,1,0:T(8,128)(2,1)}, u32[]{:S(2)}) copy-start(bf16[1,128,8192]{2,1,0:T(8,128)(2,1)} %param.8) | copy-start | bytes 6291460
  54.8 3.5 %copy-start.8 = (bf16[1,8192]{1,0:T(2,128)(2,1)S(1)}, bf16[1,8192]{1,0:T(2,128)(2,1)}, u32[]{:S(2)}) copy-start(bf16[1,8192]{1,0:T(2,128)(2,1)} %gain_ref.5) | copy-start | bytes 49156
  61.0 26.8 %collective-permute-start.13 = (bf16[128,4096]{1,0:T(8,128)(2,1)S(1)}, bf16[128,4096]{1,0:T(8,128)(2,1)S(1)}, u32[]{:S(2)}, u32[]{:S(2)}) collective-permute-start(bf16[128,4096]{1,0:T(8,128)(2,1)S(1)} %shard_map.101), channel_id=1, source_target_pairs={{0,1},{1,0},{2,3},{3,2},{4,5},{5,4},{6,7},{7,6},{8,9},{9,8},{10,11... | collective-permute-start | bytes 3145736 | tf_op jit(solution)/shard_map/ppermute | solution.py:447
  68.0 3.3 %copy-start.2 = (bf16[8192,512]{1,0:T(8,128)(2,1)}, bf16[8192,512]{1,0:T(8,128)(2,1)S(1)}, u32[]{:S(2)}) copy-start(bf16[8192,512]{1,0:T(8,128)(2,1)S(1)} %get-tuple-element.31) | copy-start | bytes 25165828
  71.3 27.6 %copy-start.3 = (bf16[128,4096]{1,0:T(8,128)(2,1)S(1)}, bf16[128,4096]{1,0:T(8,128)(2,1)}, u32[]{:S(2)}) copy-start(bf16[128,4096]{1,0:T(8,128)(2,1)} %in_ref.1) | copy-start | bytes 3145732
  89.6 35.0 %all-to-all-start = ((bf16[16,8,4096]{2,1,0:T(8,128)(2,1)}), bf16[16,8,4096]{2,1,0:T(8,128)(2,1)S(1)}, u32[]{:S(2)}, u32[]{:S(2)}) async-start(bf16[16,8,4096]{2,1,0:T(8,128)(2,1)} %bitcast.7), calls=%async_computation | async-start | bytes 2097152 | tf_op jit(solution)/shard_map/all_to_all | solution.py:451
  98.9 59.9 %reduce-scatter.2.cloned.1.call-start = ((), (), s32[]{:S(2)}) async-start(), calls=%async_computation.3 | async-start | bytes 9437184 | tf_op jit(solution)/shard_map/reduce_scatter | solution.py:460
  124.6 6.9 %copy-start.10 = (s32[1,2,8,2]{2,3,1,0:T(2,128)S(1)}, s32[1,2,8,2]{2,3,1,0:T(2,128)}, u32[]{:S(2)}) copy-start(s32[1,2,8,2]{2,3,1,0:T(2,128)} %param.15) | copy-start | bytes 388
  126.2 32.5 %all-to-all-start.1 = ((bf16[16,8,4096]{2,1,0:T(8,128)(2,1)}), bf16[16,8,4096]{2,1,0:T(8,128)(2,1)S(1)}, u32[]{:S(2)}, u32[]{:S(2)}) async-start(bf16[16,8,4096]{2,1,0:T(8,128)(2,1)} %shard_map.105), calls=%async_computation.1 | async-start | bytes 2097152 | tf_op jit(solution)/shard_map/all_to_all | solution.py:456
  158.8 1.2 copy-start.4
Sparse Core Ops, SparseCore 0:
  102.2 54.3 reduce-scatter.1

commit v3 on v2

--- a/solution.py
+++ b/solution.py
@@ -11,7 +11,7 @@
 MIB = 1024 * 1024
 TILE = 1024
 HALF_TILES = 4
-THEIRS, MINE, STAGE = 16, 17, 18
+THEIRS, MINE, STAGE, CORE, CHIP = 16, 17, 18, 19, 20
 
 NT = (((1,), (1,)), ((), ()))
 NN = (((1,), (0,)), ((), ()))
@@ -60,10 +60,15 @@
     me = lax.axis_index("dp")
     tensor_pos = lax.axis_index("tensor")
     before, after, across = lax.rem(me + 6, 8), lax.rem(me + 2, 8), lax.rem(me + 4, 8)
-    order = (me, before, me, after, after, across, before, across)
+    sibling = lambda shard: shard + 1 - 2 * lax.rem(shard, 2)
+    order = (me, sibling(me), before, sibling(before), after)
+    order += (me, sibling(me), after, sibling(after), before)
+    order += (sibling(after), across, sibling(across))
+    order += (sibling(before), across, sibling(across))
     for i, shard in enumerate(order):
-        out_ref[2 * i] = shard
-        out_ref[2 * i + 1] = shard + 1 - 2 * lax.rem(shard, 2)
+        out_ref[i] = shard
+    out_ref[CORE] = lax.rem(me, 2)
+    out_ref[CHIP] = me // 2
     out_ref[THEIRS] = (1 - tensor_pos) * HALF_TILES
     out_ref[MINE] = tensor_pos * HALF_TILES
     out_ref[STAGE] = lax.axis_index("pipe")
@@ -79,34 +84,44 @@
     )()
 
 
-def normed_kernel(x_ref, gain_ref, normed_ref, rms_ref):
+def normed_kernel(at_ref, x_ref, gain_ref, normed_ref, rms_ref, other_ref):
     x = x_ref[...].astype(jnp.float32)
     rms = lax.rsqrt(jnp.mean(x * x, -1, keepdims=True) + EPS)
     rms_ref[...] = rms
     normed_ref[...] = ((x * rms) * gain_ref[...].astype(jnp.float32)).astype(jnp.bfloat16)
-
-
-def norm(x, gain):
+    for k in range(other_ref.shape[1] // TILE):
+        shard = 2 * k + 1 - at_ref[CORE]
+        columns = pl.ds(pl.multiple_of(shard * TILE, TILE), TILE)
+        other_ref[:, k * TILE : (k + 1) * TILE] = normed_ref[:, columns]
+
+
+def norm(places, x, gain):
     tokens, features = x.shape
     rows = min(tokens, 32)
+    by_rows = lambda i, at: (i, 0)
     return pl.pallas_call(
         normed_kernel,
-        grid=(tokens // rows,),
-        in_specs=[
-            pl.BlockSpec((rows, features), lambda i: (i, 0)),
-            pl.BlockSpec((1, features), lambda i: (0, 0)),
-        ],
-        out_specs=[
-            pl.BlockSpec((rows, features), lambda i: (i, 0)),
-            pl.BlockSpec((rows, 1), lambda i: (i, 0)),
-        ],
+        grid_spec=pltpu.PrefetchScalarGridSpec(
+            num_scalar_prefetch=1,
+            grid=(tokens // rows,),
+            in_specs=[
+                pl.BlockSpec((rows, features), by_rows),
+                pl.BlockSpec((1, features), lambda i, at: (0, 0)),
+            ],
+            out_specs=[
+                pl.BlockSpec((rows, features), by_rows),
+                pl.BlockSpec((rows, 1), by_rows),
+                pl.BlockSpec((rows, features // 2), by_rows),
+            ],
+        ),
         out_shape=(
             jax.ShapeDtypeStruct(x.shape, jnp.bfloat16),
             jax.ShapeDtypeStruct((tokens, 1), jnp.float32),
+            jax.ShapeDtypeStruct((tokens, features // 2), jnp.bfloat16),
         ),
         compiler_params=pltpu.CompilerParams(vmem_limit_bytes=12 * MIB),
-        cost_estimate=cost(4 * x.size, 4 * x.size),
-    )(x, gain)
+        cost_estimate=cost(0, 0),
+    )(places, x, gain)
 
 
 def early_kernel(shards_ref, normed_ref, both_ref, *refs, count):
@@ -137,7 +152,7 @@
         out_shape=(rows, rows, whole, whole),
         scratch_shapes=[pltpu.SemaphoreType.DMA((count,))] * 2,
         compiler_params=pltpu.CompilerParams(vmem_limit_bytes=16 * MIB),
-        cost_estimate=cost(4 * tokens * depth * width * count, 8 * depth * width * count),
+        cost_estimate=cost(0, 0),
     )(shards, normed, both, *key_pieces, *value_pieces)
 
 
@@ -146,7 +161,7 @@
     key_part_ref, value_part_ref, _, _, query_ref, grad_ref, seg_ref = refs[
         2 * count : 2 * count + 7
     ]
-    key_w_ref, value_w_ref, key_grad_ref, value_grad_ref, inner_ref, key_sems, value_sems = refs[
+    key_w_ref, value_w_ref, grads_ref, inner_ref, key_sems, value_sems = refs[
         2 * count + 7 :
     ]
     key_f, copies = add_rows(
@@ -178,8 +193,8 @@
         delta = jnp.sum(probability * dprob, 0, keepdims=True)
         dscore_b = (probability * (dprob - delta)).astype(jnp.bfloat16)
         key_grad = (dot(dscore_b, query_j, NN) * (HD ** (-0.5))).astype(jnp.bfloat16)
-        key_grad_ref[:, at] = key_grad
-        value_grad_ref[:, at] = value_grad
+        grads_ref[:, at] = key_grad
+        grads_ref[:, width + j * HD : width + (j + 1) * HD] = value_grad
         total = total + jnp.sum(
             key_grad.astype(jnp.float32) * key_j + value_grad.astype(jnp.float32) * value_j,
             1,
@@ -195,13 +210,13 @@
     depth, width = key_pieces[0].shape
     count = len(key_pieces)
     whole = jax.ShapeDtypeStruct((features, width), jnp.bfloat16)
-    grads = jax.ShapeDtypeStruct((tokens, width), jnp.bfloat16)
+    grads = jax.ShapeDtypeStruct((tokens, 2 * width), jnp.bfloat16)
     at = 2 * count + 4
     return pl.pallas_call(
         lambda *refs: attention_kernel(*refs, count=count, first=first, features=features),
         in_specs=[IN_SMEM] + in_vmem(2 * count + 3) + [ANYWHERE] * 2 + in_vmem(3),
-        out_specs=[ANYWHERE] * 2 + in_vmem(3),
-        out_shape=(whole, whole, grads, grads, jax.ShapeDtypeStruct((tokens, 1), jnp.float32)),
+        out_specs=[ANYWHERE] * 2 + in_vmem(2),
+        out_shape=(whole, whole, grads, jax.ShapeDtypeStruct((tokens, 1), jnp.float32)),
         input_output_aliases={at: 0, at + 1: 1},
         scratch_shapes=[pltpu.SemaphoreType.DMA((count,))] * 2,
         compiler_params=pltpu.CompilerParams(vmem_limit_bytes=20 * MIB),
@@ -230,20 +245,20 @@
     )(*arrays, after)
 
 
-def branch_kernel(
-    at_ref, key_grad_ref, value_grad_ref, key_w_ref, value_w_ref, x_ref, gain_ref, rms_ref, inner_ref, out_ref
-):
-    d_normed = dot(key_grad_ref[...], key_w_ref[...], NT)
-    d_normed = d_normed + dot(value_grad_ref[...], value_w_ref[...], NT)
+def branch_kernel(at_ref, grads_ref, key_w_ref, value_w_ref, x_ref, gain_ref, rms_ref, inner_ref, out_ref):
+    columns = key_w_ref.shape[1]
+    d_normed = dot(grads_ref[:, :columns], key_w_ref[...], NT)
+    d_normed = d_normed + dot(grads_ref[:, columns:], value_w_ref[...], NT)
     rms = rms_ref[...]
     x_hat = x_ref[...].astype(jnp.float32) * rms
     gated = gain_ref[...].astype(jnp.float32) * d_normed
     out_ref[...] = (rms * (gated - x_hat * inner_ref[...])).astype(out_ref.dtype)
 
 
-def partial_branch(places, half, kind, key_grad, value_grad, key_w, value_w, x, gain, inv_rms, inner):
-    tokens, columns = key_grad.shape
-    tile, width = TILE, TILE * HALF_TILES
+def partial_branch(places, half, kind, grads, key_w, value_w, x, gain, inv_rms, inner):
+    tokens = grads.shape[0]
+    columns = key_w.shape[1]
+    width = TILE * HALF_TILES
     whole = lambda i, at: (0, 0)
     rows = lambda i, at: (at[half] + i, 0)
     lanes = lambda i, at: (0, at[half] + i)
@@ -251,58 +266,81 @@
         branch_kernel,
         grid_spec=pltpu.PrefetchScalarGridSpec(
             num_scalar_prefetch=1,
-            grid=(width // tile,),
+            grid=(HALF_TILES,),
             in_specs=[
-                pl.BlockSpec((tokens, columns), whole),
-                pl.BlockSpec((tokens, columns), whole),
-                pl.BlockSpec((tile, columns), rows),
-                pl.BlockSpec((tile, columns), rows),
-                pl.BlockSpec((tokens, tile), lanes),
-                pl.BlockSpec((1, tile), lanes),
+                pl.BlockSpec((tokens, 2 * columns), whole),
+                pl.BlockSpec((TILE, columns), rows),
+                pl.BlockSpec((TILE, columns), rows),
+                pl.BlockSpec((tokens, TILE), lanes),
+                pl.BlockSpec((1, TILE), lanes),
                 pl.BlockSpec((tokens, 1), whole),
                 pl.BlockSpec((tokens, 1), whole),
             ],
-            out_specs=pl.BlockSpec((tokens, tile), lambda i, at: (0, i)),
+            out_specs=pl.BlockSpec((tokens, TILE), lambda i, at: (0, i)),
         ),
         out_shape=jax.ShapeDtypeStruct((tokens, width), kind),
         compiler_params=pltpu.CompilerParams(vmem_limit_bytes=8 * MIB),
         cost_estimate=cost(
             4 * tokens * width * columns, 4 * width * columns + 2 * width * tokens
         ),
-    )(places, key_grad, value_grad, key_w, value_w, x, gain, inv_rms, inner)
-
-
-def weight_part_kernel(normed_ref, key_grad_ref, value_grad_ref, after_ref, out_ref, token_ref):
-    columns = key_grad_ref.shape[1]
-    normed = normed_ref[...]
-    out_ref[:, :columns] = dot(normed, key_grad_ref[...], TN).astype(out_ref.dtype)
-    out_ref[:, columns:] = dot(normed, value_grad_ref[...], TN).astype(out_ref.dtype)
+    )(places, grads, key_w, value_w, x, gain, inv_rms, inner)
+
+
+def weight_part_kernel(
+    at_ref, normed_ref, normed_sib_ref, grads_ref, grads_sib_ref, after_ref,
+    own_ref, right_ref, left_ref, far_right_ref, far_left_ref,
+):
+    grads = jnp.concatenate([grads_ref[...], grads_sib_ref[...]], 0)
+    half = far_right_ref.shape[0]
+
+    def part(step):
+        k = lax.rem(at_ref[CHIP] + step, 4)
+        own = pl.ds(pl.multiple_of((2 * k + at_ref[CORE]) * TILE, TILE), TILE)
+        sib = pl.ds(pl.multiple_of(k * TILE, TILE), TILE)
+        rows = jnp.concatenate([normed_ref[:, own], normed_sib_ref[:, sib]], 0)
+        return dot(rows, grads, TN).astype(own_ref.dtype)
+
+    far = part(2)
+    far_right_ref[...] = far[:half]
+    far_left_ref[...] = far[half:]
+    own_ref[...] = part(0)
+    right_ref[...] = part(1)
+    left_ref[...] = part(3)
+
+
+def weight_parts(places, normed, normed_sib, grads, grads_sib, after):
+    part = jax.ShapeDtypeStruct((TILE, grads.shape[1]), jnp.bfloat16)
+    half = jax.ShapeDtypeStruct((TILE // 2, grads.shape[1]), jnp.bfloat16)
+    return pl.pallas_call(
+        weight_part_kernel,
+        in_specs=[IN_SMEM] + in_vmem(4) + [ANYWHERE],
+        out_specs=in_vmem(5),
+        out_shape=[part] * 3 + [half] * 2,
+        compiler_params=pltpu.CompilerParams(vmem_limit_bytes=20 * MIB),
+        cost_estimate=cost(4 * normed.size * grads.shape[1], 4 * normed.size),
+    )(places, normed, normed_sib, grads, grads_sib, after)
+
+
+def join_kernel(right_ref, left_ref, far_right_ref, far_left_ref, to_right_ref, to_left_ref, token_ref):
+    half = far_right_ref.shape[0]
+    join = lambda a, b: (a.astype(jnp.float32) + b.astype(jnp.float32)).astype(jnp.bfloat16)
+    to_right_ref[:half] = join(right_ref[:half], far_right_ref[...])
+    to_right_ref[half:] = right_ref[half:]
+    to_left_ref[:half] = left_ref[:half]
+    to_left_ref[half:] = join(left_ref[half:], far_left_ref[...])
     token_ref[...] = jnp.zeros_like(token_ref)
 
 
-def weight_part(normed, key_grad, value_grad, after):
-    tokens, features = normed.shape
-    columns = key_grad.shape[1]
-    return pl.pallas_call(
-        weight_part_kernel,
-        grid=(features // TILE,),
-        in_specs=[
-            pl.BlockSpec((tokens, TILE), lambda i: (0, i)),
-            pl.BlockSpec((tokens, columns), lambda i: (0, 0)),
-            pl.BlockSpec((tokens, columns), lambda i: (0, 0)),
-            ANYWHERE,
-        ],
-        out_specs=[
-            pl.BlockSpec((TILE, 2 * columns), lambda i: (i, 0)),
-            pl.BlockSpec((8, 128), lambda i: (0, 0)),
-        ],
-        out_shape=(
-            jax.ShapeDtypeStruct((features, 2 * columns), jnp.bfloat16),
-            jax.ShapeDtypeStruct((8, 128), jnp.float32),
-        ),
-        compiler_params=pltpu.CompilerParams(vmem_limit_bytes=8 * MIB),
-        cost_estimate=cost(4 * tokens * features * columns, 4 * features * columns),
-    )(normed, key_grad, value_grad, after)
+def join_parts(right, left, far_right, far_left):
+    part = jax.ShapeDtypeStruct(right.shape, right.dtype)
+    return pl.pallas_call(
+        join_kernel,
+        in_specs=in_vmem(4),
+        out_specs=in_vmem(3),
+        out_shape=[part, part, jax.ShapeDtypeStruct((8, 128), jnp.float32)],
+        compiler_params=pltpu.CompilerParams(vmem_limit_bytes=12 * MIB),
+        cost_estimate=cost(right.size, 8 * right.size),
+    )(right, left, far_right, far_left)
 
 
 def add_kernel(mine_ref, arrived_ref, token_ref, out_ref):
@@ -319,7 +357,7 @@
         out_specs=spec,
         out_shape=jax.ShapeDtypeStruct(mine.shape, jnp.bfloat16),
         compiler_params=pltpu.CompilerParams(vmem_limit_bytes=8 * MIB),
-        cost_estimate=cost(mine.size, 8 * mine.size),
+        cost_estimate=cost(1e15, 1e12),
     )(mine, arrived, token)
 
 
@@ -363,34 +401,34 @@
         out_specs=pl.BlockSpec((layers, rows, tile), lambda i: (0, 0, i)),
         out_shape=jax.ShapeDtypeStruct(parts.shape, jnp.bfloat16),
         compiler_params=pltpu.CompilerParams(vmem_limit_bytes=8 * MIB),
-        cost_estimate=cost(1e15, 1e12),
+        cost_estimate=cost(parts.size, 4 * parts.size),
     )(parts, top)
 
 
-def scale_kernel(factor_ref, summed_ref, out_ref):
+def scale_kernel(factor_ref, *refs):
+    *part_refs, out_ref = refs
     p = pl.program_id(0)
     for i in range(out_ref.shape[1] // BLOCK):
         for c in range(out_ref.shape[2] // HD):
-            block = summed_ref[i * BLOCK : (i + 1) * BLOCK, c * HD : (c + 1) * HD]
-            scaled = block.astype(jnp.float32) * factor_ref[p, i, c]
-            out_ref[0, i * BLOCK : (i + 1) * BLOCK, c * HD : (c + 1) * HD] = scaled.astype(jnp.bfloat16)
-
-
-def scaled_grad(summed, factor):
-    rows = summed.shape[0]
-    columns = summed.shape[1] // 2
+            at = (slice(i * BLOCK, (i + 1) * BLOCK), slice(c * HD, (c + 1) * HD))
+            total = part_refs[0][at].astype(jnp.float32)
+            for ref in part_refs[1:]:
+                total = total + ref[at].astype(jnp.float32)
+            out_ref[(0, *at)] = (total * factor_ref[p, i, c]).astype(jnp.bfloat16)
+
+
+def scaled_grad(parts, factor):
+    rows = parts[0].shape[0]
+    columns = parts[0].shape[1] // 2
     return pl.pallas_call(
         scale_kernel,
         grid=(2,),
-        in_specs=[
-            pl.BlockSpec(memory_space=pltpu.SMEM),
-            pl.BlockSpec((rows, columns), lambda p: (0, p)),
-        ],
+        in_specs=[IN_SMEM] + [pl.BlockSpec((rows, columns), lambda p: (0, p))] * len(parts),
         out_specs=pl.BlockSpec((1, rows, columns), lambda p: (p, 0, 0)),
         out_shape=jax.ShapeDtypeStruct((2, rows, columns), jnp.bfloat16),
-        compiler_params=pltpu.CompilerParams(vmem_limit_bytes=8 * MIB),
-        cost_estimate=cost(summed.size, 4 * summed.size),
-    )(factor, summed)
+        compiler_params=pltpu.CompilerParams(vmem_limit_bytes=12 * MIB),
+        cost_estimate=cost(parts[0].size, 10 * parts[0].size),
+    )(factor, *parts)
 
 
 def ring_pairs(count):
@@ -418,21 +456,22 @@
     value_2 = send(value_r, left)
 
     places = all_places()
-    normed, inv_rms = norm(inputs, norm_gain)
+    normed, inv_rms, normed_other = norm(places, inputs, norm_gain)
+    normed_sib = send(normed_other, other)
     early = early_rows(
         places,
         normed,
         both,
-        [key_own, key_l, send(key_l, other)],
-        [value_own, value_r, send(value_r, other)],
+        [key_own, key_l, send(key_l, other), key_r],
+        [value_own, value_r, send(value_r, other), value_l],
     )
     key_r, value_l = ordered((key_r, value_l), early[0])
-    key_w, value_w, key_grad, value_grad, inner = attention_grads(
+    key_w, value_w, grads, inner = attention_grads(
         places,
-        8,
+        10,
         normed,
-        [key_r, send(key_r, other), key_2, send(key_2, other)],
-        [value_l, send(value_l, other), value_2, send(value_2, other)],
+        [send(key_r, other), key_2, send(key_2, other)],
+        [send(value_l, other), value_2, send(value_2, other)],
         early,
         queries[0],
         out_grad[0],
@@ -441,12 +480,18 @@
 
     def share(half, kind):
         return partial_branch(
-            places, half, kind, key_grad, value_grad, key_w, value_w, inputs, norm_gain, inv_rms, inner
+            places, half, kind, grads, key_w, value_w, inputs, norm_gain, inv_rms, inner
         )
 
     arrived = lax.ppermute(share(THEIRS, jnp.bfloat16), "tensor", [(0, 1), (1, 0)])
     mine = share(MINE, jnp.float32)
-    part, token = weight_part(normed, key_grad, value_grad, mine)
+    own, to_right, to_left, far_right, far_left = weight_parts(
+        places, normed, normed_sib, grads, send(grads, other), mine
+    )
+    to_right, to_left, token = join_parts(
+        to_right, to_left, send(far_right, right), send(far_left, left)
+    )
+    received = [send(to_right, right), send(to_left, left)]
     branch = add_halves(mine, arrived, token)
     parts = lax.all_to_all(branch, "pipe", 0, 0, tiled=True)
     rows = token_count // pipe_count
@@ -456,9 +501,7 @@
     input_grad = lax.all_to_all(
         sums.reshape(token_count, branch.shape[1]), "pipe", 0, 0, tiled=True
     )
-
-    summed = lax.psum_scatter(part, "dp", scatter_dimension=0, tiled=True)
-    weight_grad = scaled_grad(summed, jnp.exp2(-scale_exp[0].astype(jnp.float32)))
+    weight_grad = scaled_grad([own, *received], jnp.exp2(-scale_exp[0].astype(jnp.float32)))
     return (input_grad[None], weight_grad[None])
 
 

time: 170 us -> 154 us (0.906)
  between operations: 14.2 us -> 0.91 us
  starting transfers between devices: 24.9 us -> 30.9 us
  waiting for transfers between devices: 98.2 us -> 92.6 us
  local copies, waits for them, and re-layouts: 9.2 us -> 6.04 us
    ppermute x13 -> x19, waiting for transfers between devices: 29.5 us -> 62.4 us  [on_device(): send = lambda piece, pairs: lax.ppermute(piece, 'dp', pairs)]
    all_to_all x1, waiting for transfers between devices: 27.2 us -> 0.01 us  [on_device(): lax.all_to_all(sums.reshape(token_count, branch.shape[1]), 'pipe', 0, 0,...]
    ppermute x1, waiting for transfers between devices: 16.5 us -> 5.1 us  [on_device(): lax.ppermute(share(THEIRS, jnp.bfloat16), 'tensor', [(0, 1), (1, 0)])]
    ppermute x13 -> x19, starting transfers between devices: 10 us -> 16.1 us  [on_device(): send = lambda piece, pairs: lax.ppermute(piece, 'dp', pairs)]
    unnamed x23, local copies, waits for them, and re-layouts: 7.84 us -> 4.68 us
    pallas_call x3 -> x4, Pallas kernels: 7.14 us -> 7.23 us  [the longest x1 2.11 us: norm(): pl.pallas_call(normed_kernel, grid_spec=pltpu.PrefetchScalarGridSpec(num_...]
  transfers between devices with their start and end apart: 17 -> 22, of which waited for: 9 -> 10; matrix products, arithmetic and copies ran while one was open for 0% -> 0% of each run, Pallas kernels for 8% -> 13%
where the time goes in v3:
time: 154 us
  waiting for transfers between devices  92.6 us (60%)
  starting transfers between devices  30.9 us (20%)
  Pallas kernels  23.1 us (15%)
  local copies, waits for them, and re-layouts  6.04 us (4%)
    ppermute x19, waiting for transfers between devices, on_device(): send = lambda piece, pairs: lax.ppermute(piece, 'dp', pairs)  62.4 us
    all_to_all x1, waiting for transfers between devices, on_device(): parts = lax.all_to_all(branch, 'pipe', 0, 0, tiled=True)  25.1 us
    ppermute x19, starting transfers between devices, on_device(): send = lambda piece, pairs: lax.ppermute(piece, 'dp', pairs)  16.1 us
    all_to_all x1, starting transfers between devices, on_device(): parts = lax.all_to_all(branch, 'pipe', 0, 0, tiled=True)  9.43 us
    pallas_call x2, Pallas kernels, partial_branch(): pl.pallas_call(branch_kernel, grid_spec=pltpu.PrefetchScalarGridSpec(num_...  5.51 us
    all_to_all x1, starting transfers between devices, on_device(): lax.all_to_all(sums.reshape(token_count, branch.shape[1]), 'pipe', 0, 0,...  5.27 us
    ppermute x1, waiting for transfers between devices, on_device(): lax.ppermute(share(THEIRS, jnp.bfloat16), 'tensor', [(0, 1), (1, 0)])  5.1 us
    unnamed x23, local copies, waits for them, and re-layouts  4.68 us
  transfers between devices with their start and end apart: 22, of which 10 were waited for; matrix products, arithmetic and copies ran while one was open for 0% of the time, Pallas kernels for 13%

profile of v3, /device:TPU:16, one launch (start us, length us, event | category | flops | bytes accessed | tf_op | source)
XLA Modules:
  0.0 153.6 jit_solution(14207061553457641489)
XLA Ops:
  0.6 1.3 slice_bitcast_fusion
  1.9 1.6 %collective-permute-start.3 = (bf16[1024,256]{1,0:T(8,128)(2,1)S(1)}, bf16[1024,256]{1,0:T(8,128)(2,1)S(1)}, u32[]{:S(2)}, u32[]{:S(2)}) collective-permute-start(bf16[1024,256]{1,0:T(8,128)(2,1)S(1)} %get-tuple-element.45.refs_3_), channel_id=1, source_target_pairs={{0,4},{2,6},{4,8},{6,10},{8,12},{10,14},{12,0},{14,2},{1,5},{3,7},... | collective-permute-start | bytes 1572872 | tf_op jit(solution)/shard_map/ppermute | solution.py:448
  3.5 1.7 %collective-permute-start.5 = (bf16[1024,256]{1,0:T(8,128)(2,1)S(1)}, bf16[1024,256]{1,0:T(8,128)(2,1)S(1)}, u32[]{:S(2)}, u32[]{:S(2)}) collective-permute-start(bf16[1024,256]{1,0:T(8,128)(2,1)S(1)} %get-tuple-element.44.refs_7_), channel_id=1, source_target_pairs={{0,12},{2,14},{4,0},{6,2},{8,4},{10,6},{12,8},{14,10},{1,13},{3,15... | collective-permute-start | bytes 1572872 | tf_op jit(solution)/shard_map/ppermute | solution.py:448
  5.2 1.5 %collective-permute-start = (bf16[1024,256]{1,0:T(8,128)(2,1)S(1)}, bf16[1024,256]{1,0:T(8,128)(2,1)S(1)}, u32[]{:S(2)}, u32[]{:S(2)}) collective-permute-start(bf16[1024,256]{1,0:T(8,128)(2,1)S(1)} %get-tuple-element.45.refs_3_), channel_id=1, source_target_pairs={{0,12},{2,14},{4,0},{6,2},{8,4},{10,6},{12,8},{14,10},{1,13},{3,15... | collective-permute-start | bytes 1572872 | tf_op jit(solution)/shard_map/ppermute | solution.py:448
  7.2 10.8 %collective-permute-done.3.refs_4_ = bf16[1024,256]{1,0:T(8,128)(2,1)S(1)} collective-permute-done((bf16[1024,256]{1,0:T(8,128)(2,1)S(1)}, bf16[1024,256]{1,0:T(8,128)(2,1)S(1)}, u32[]{:S(2)}, u32[]{:S(2)}) %collective-permute-start.3) | collective-permute-done | bytes 524320 | tf_op jit(solution)/shard_map/ppermute | solution.py:448
  18.5 9.6 %collective-permute-done.refs_6_.refs_0_ = bf16[1024,256]{1,0:T(8,128)(2,1)S(1)} collective-permute-done((bf16[1024,256]{1,0:T(8,128)(2,1)S(1)}, bf16[1024,256]{1,0:T(8,128)(2,1)S(1)}, u32[]{:S(2)}, u32[]{:S(2)}) %collective-permute-start) | collective-permute-done | bytes 524320 | tf_op jit(solution)/shard_map/ppermute | solution.py:448
  28.1 3.0 %collective-permute-start.11 = (bf16[1024,256]{1,0:T(8,128)(2,1)S(1)}, bf16[1024,256]{1,0:T(8,128)(2,1)S(1)}, u32[]{:S(2)}, u32[]{:S(2)}) collective-permute-start(bf16[1024,256]{1,0:T(8,128)(2,1)S(1)} %collective-permute-done.5.refs_8_), channel_id=1, source_target_pairs={{0,12},{2,14},{4,0},{6,2},{8,4},{10,6},{12,8},{14,10},{1,13},{3,15... | collective-permute-start | bytes 1572872 | tf_op jit(solution)/shard_map/ppermute | solution.py:448
  31.1 0.6 shard_map.95.at_ref.refs_0_
  31.7 1.6 %copy-done = bf16[1,128,8192]{2,1,0:T(8,128)(2,1)S(1)} copy-done((bf16[1,128,8192]{2,1,0:T(8,128)(2,1)S(1)}, bf16[1,128,8192]{2,1,0:T(8,128)(2,1)}, u32[]{:S(2)}) %copy-start) | copy-done | bytes 2097176
  33.3 0.8 copy-done.5
  34.0 2.1 %shard_map.96 = (bf16[128,8192]{1,0:T(8,128)(2,1)S(1)}, f32[128,1]{1,0:T(8,128)S(1)}, bf16[128,4096]{1,0:T(8,128)(2,1)S(1)}) custom-call(s32[32]{0:T(128)S(1)} %shard_map.95.at_ref.refs_0_, bf16[128,8192]{1,0:T(8,128)(2,1)S(1)} %bitcast.14, bf16[1,8192]{1,0:T(2,128)(2,1)S(1)} %copy-done.5), custom_call_target="tpu_custom_call" | custom-call | tf_op jit(solution)/shard_map/pallas_call | solution.py:102
  36.3 2.7 %shard_map.97 = (f32[128,256]{1,0:T(8,128)S(1)}, f32[128,256]{1,0:T(8,128)S(1)}, bf16[8192,256]{1,0:T(8,128)(2,1)S(1)}, bf16[8192,256]{1,0:T(8,128)(2,1)S(1)}) custom-call(s32[32]{0:T(128)S(1)} %shard_map.95.at_ref.refs_0_, bf16[128,8192]{1,0:T(8,128)(2,1)S(1)} %get-tuple-element.23.refs_1_.normed_ref, ...), custom_call_target="tpu_custom_call" | custom-call | tf_op jit(solution)/shard_map/pallas_call | solution.py:148
  39.7 1.4 collective-permute-done.11.refs_6_
  41.0 3.4 %collective-permute-done.8.refs_3_ = bf16[1024,256]{1,0:T(8,128)(2,1)S(1)} collective-permute-done((bf16[1024,256]{1,0:T(8,128)(2,1)S(1)}, bf16[1024,256]{1,0:T(8,128)(2,1)S(1)}, u32[]{:S(2)}, u32[]{:S(2)}) %collective-permute-start.8) | collective-permute-done | bytes 524320 | tf_op jit(solution)/shard_map/ppermute | solution.py:448
  44.5 1.9 %collective-permute-done.9.refs_4_ = bf16[1024,256]{1,0:T(8,128)(2,1)S(1)} collective-permute-done((bf16[1024,256]{1,0:T(8,128)(2,1)S(1)}, bf16[1024,256]{1,0:T(8,128)(2,1)S(1)}, u32[]{:S(2)}, u32[]{:S(2)}) %collective-permute-start.9) | collective-permute-done | bytes 524320 | tf_op jit(solution)/shard_map/ppermute | solution.py:448
  46.4 3.1 %shard_map.99 = (bf16[8192,256]{1,0:T(8,128)(2,1)S(1)}, bf16[8192,256]{1,0:T(8,128)(2,1)S(1)}, bf16[128,512]{1,0:T(8,128)(2,1)S(1)}, f32[128,1]{1,0:T(8,128)S(1)}) custom-call(s32[32]{0:T(128)S(1)} %shard_map.95.at_ref.refs_0_, bf16[128,8192]{1,0:T(8,128)(2,1)S(1)} %get-tuple-element.23.refs_1_.normed_ref, ...), custom_call_target="tpu_custom_call", output_to_operand_aliasing={{0}: (10, {}), {1}: (11, {})} | custom-call | flops 671088640 | bytes 7340032 | tf_op jit(solution)/shard_map/pallas_call | solution.py:215
  49.5 2.7 %shard_map.101 = bf16[128,4096]{1,0:T(8,128)(2,1)S(1)} custom-call(s32[32]{0:T(128)S(1)} %shard_map.95.at_ref.refs_0_, bf16[128,512]{1,0:T(8,128)(2,1)S(1)} %get-tuple-element.30.grads_ref, bf16[8192,256]{1,0:T(8,128)(2,1)S(1)} %get-tuple-element.31.key_w_ref, bf16[8192,256]{1,0:T(8,128)(2,1)S(1)} %get-tuple-element.32.value_w_ref, ...), custom_call_target="tpu_custom_call" | custom-call | flops 536870912 | bytes 5242880 | tf_op jit(solution)/shard_map/pallas_call | solution.py:265
  52.6 2.8 %shard_map.100.after_ref.mine_ref = f32[128,4096]{1,0:T(8,128)S(1)} custom-call(s32[32]{0:T(128)S(1)} %shard_map.95.at_ref.refs_0_, bf16[128,512]{1,0:T(8,128)(2,1)S(1)} %get-tuple-element.30.grads_ref, bf16[8192,256]{1,0:T(8,128)(2,1)S(1)} %get-tuple-element.31.key_w_ref, bf16[8192,256]{1,0:T(8,128)(2,1)S(1)} %get-tuple-element.32.value_w_ref, ...), custom_call_target="tpu_custom_call" | custom-call | flops 536870912 | bytes 5242880 | tf_op jit(solution)/shard_map/pallas_call | solution.py:265
  55.4 1.8 %shard_map.102 = (bf16[1024,512]{1,0:T(8,128)(2,1)S(1)}, bf16[1024,512]{1,0:T(8,128)(2,1)S(1)}, bf16[1024,512]{1,0:T(8,128)(2,1)S(1)}, bf16[512,512]{1,0:T(8,128)(2,1)S(1)}, bf16[512,512]{1,0:T(8,128)(2,1)S(1)}) custom-call(s32[32]{0:T(128)S(1)} %shard_map.95.at_ref.refs_0_, bf16[128,8192]{1,0:T(8,128)(2,1)S(1)} %get-tuple-element.23.refs_1_.normed_ref, ...), custom_call_target="tpu_custom_call" | custom-call | flops 2147483648 | bytes 4194304 | tf_op jit(solution)/shard_map/pallas_call | solution.py:314
  57.3 3.2 %collective-permute-start.17 = (bf16[512,512]{1,0:T(8,128)(2,1)S(1)}, bf16[512,512]{1,0:T(8,128)(2,1)S(1)}, u32[]{:S(2)}, u32[]{:S(2)}) collective-permute-start(bf16[512,512]{1,0:T(8,128)(2,1)S(1)} %get-tuple-element.39), channel_id=1, source_target_pairs={{0,12},{2,14},{4,0},{6,2},{8,4},{10,6},{12,8},{14,10},{1,13},{3,15... | collective-permute-start | bytes 1572872 | tf_op jit(solution)/shard_map/ppermute | solution.py:448
  60.6 12.2 %collective-permute-done.16.far_right_ref = bf16[512,512]{1,0:T(8,128)(2,1)S(1)} collective-permute-done((bf16[512,512]{1,0:T(8,128)(2,1)S(1)}, bf16[512,512]{1,0:T(8,128)(2,1)S(1)}, u32[]{:S(2)}, u32[]{:S(2)}) %collective-permute-start.16) | collective-permute-done | bytes 524320 | tf_op jit(solution)/shard_map/ppermute | solution.py:448
  72.7 1.2 shard_map.103
  73.9 5.1 %collective-permute-done.13.arrived_ref = bf16[128,4096]{1,0:T(8,128)(2,1)S(1)} collective-permute-done((bf16[128,4096]{1,0:T(8,128)(2,1)S(1)}, bf16[128,4096]{1,0:T(8,128)(2,1)S(1)}, u32[]{:S(2)}, u32[]{:S(2)}) %collective-permute-start.13) | collective-permute-done | bytes 1048608 | tf_op jit(solution)/shard_map/ppermute | solution.py:486
  79.0 1.8 %shard_map.104 = bf16[128,4096]{1,0:T(8,128)(2,1)} custom-call(f32[128,4096]{1,0:T(8,128)S(1)} %shard_map.100.after_ref.mine_ref, bf16[128,4096]{1,0:T(8,128)(2,1)S(1)} %collective-permute-done.13.arrived_ref, f32[8,128]{1,0:T(8,128)S(1)} %get-tuple-element.40.token_ref), custom_call_target="tpu_custom_call" | custom-call | flops 999999986991104 | bytes 999999995904 | tf_op jit(solution)/shard_map/pallas_call | solution.py:353
  80.8 9.4 %all-to-all-start = ((bf16[16,8,4096]{2,1,0:T(8,128)(2,1)}), bf16[16,8,4096]{2,1,0:T(8,128)(2,1)S(1)}, u32[]{:S(2)}, u32[]{:S(2)}) async-start(bf16[16,8,4096]{2,1,0:T(8,128)(2,1)} %bitcast.7), calls=%async_computation | async-start | bytes 2097152 | tf_op jit(solution)/shard_map/all_to_all | solution.py:496
  90.8 25.1 %all-to-all-done.parts_ref = bf16[16,8,4096]{2,1,0:T(8,128)(2,1)S(1)} async-done(((bf16[16,8,4096]{2,1,0:T(8,128)(2,1)}), bf16[16,8,4096]{2,1,0:T(8,128)(2,1)S(1)}, u32[]{:S(2)}, u32[]{:S(2)}) %all-to-all-start) | async-done | bytes 1048608 | tf_op jit(solution)/shard_map/all_to_all | solution.py:496
  116.0 1.7 %shard_map.106 = bf16[16,8,4096]{2,1,0:T(8,128)(2,1)} custom-call(bf16[16,8,4096]{2,1,0:T(8,128)(2,1)S(1)} %all-to-all-done.parts_ref, bf16[8,4096]{1,0:T(8,128)(2,1)S(1)} %shard_map.105.top_ref), custom_call_target="tpu_custom_call" | custom-call | flops 524288 | bytes 2097152 | tf_op jit(solution)/shard_map/pallas_call | solution.py:394
  117.6 5.3 %all-to-all-start.1 = ((bf16[16,8,4096]{2,1,0:T(8,128)(2,1)}), bf16[16,8,4096]{2,1,0:T(8,128)(2,1)}, u32[]{:S(2)}, u32[]{:S(2)}) async-start(bf16[16,8,4096]{2,1,0:T(8,128)(2,1)} %shard_map.106), calls=%async_computation.1 | async-start | bytes 2097152 | tf_op jit(solution)/shard_map/all_to_all | solution.py:501
  123.0 3.2 %collective-permute-start.19 = (bf16[1024,512]{1,0:T(8,128)(2,1)}, bf16[1024,512]{1,0:T(8,128)(2,1)S(1)}, u32[]{:S(2)}, u32[]{:S(2)}) collective-permute-start(bf16[1024,512]{1,0:T(8,128)(2,1)} %copy-done.9), channel_id=1, source_target_pairs={{0,12},{2,14},{4,0},{6,2},{8,4},{10,6},{12,8},{14,10},{1,13},{3,15... | collective-permute-start | bytes 3145736 | tf_op jit(solution)/shard_map/ppermute | solution.py:448
  126.3 22.9 %collective-permute-done.18.refs_1_ = bf16[1024,512]{1,0:T(8,128)(2,1)S(1)} collective-permute-done((bf16[1024,512]{1,0:T(8,128)(2,1)}, bf16[1024,512]{1,0:T(8,128)(2,1)S(1)}, u32[]{:S(2)}, u32[]{:S(2)}) %collective-permute-start.18) | collective-permute-done | bytes 1048608 | tf_op jit(solution)/shard_map/ppermute | solution.py:448
  149.2 2.1 %shard_map.107 = bf16[2,1024,256]{2,1,0:T(8,128)(2,1)} custom-call(f32[2,8,2]{2,1,0:T(8,128)S(1)} %copy.14.factor_ref, bf16[1024,512]{1,0:T(8,128)(2,1)S(1)} %get-tuple-element.41.refs_0_, bf16[1024,512]{1,0:T(8,128)(2,1)S(1)} %collective-permute-done.18.refs_1_, bf16[1024,512]{1,0:T(8,128)(2,1)S(1)} %collective-permute-done.19.refs_2_), custom_call_target="tpu_custom_call" | custom-call | flops 524288 | bytes 5242880 | tf_op jit(solution)/shard_map/pallas_call | solution.py:423
  151.3 2.3 %copy.20 = bf16[1,128,4096]{2,1,0:T(8,128)(2,1)} copy(bf16[1,128,4096]{2,1,0:T(8,128)(2,1)} %bitcast.8) | data formatting | bytes 2097152
  (51 shorter events, 3.0 us)
Async XLA Ops:
  1.9 16.1 %collective-permute-start.3 = (bf16[1024,256]{1,0:T(8,128)(2,1)S(1)}, bf16[1024,256]{1,0:T(8,128)(2,1)S(1)}, u32[]{:S(2)}, u32[]{:S(2)}) collective-permute-start(bf16[1024,256]{1,0:T(8,128)(2,1)S(1)} %get-tuple-element.45.refs_3_), channel_id=1, source_target_pairs={{0,4},{2,6},{4,8},{6,10},{8,12},{10,14},{12,0},{14,2},{1,5},{3,7},... | collective-permute-start | bytes 1572872 | tf_op jit(solution)/shard_map/ppermute | solution.py:448
  3.5 14.8 %collective-permute-start.5 = (bf16[1024,256]{1,0:T(8,128)(2,1)S(1)}, bf16[1024,256]{1,0:T(8,128)(2,1)S(1)}, u32[]{:S(2)}, u32[]{:S(2)}) collective-permute-start(bf16[1024,256]{1,0:T(8,128)(2,1)S(1)} %get-tuple-element.44.refs_7_), channel_id=1, source_target_pairs={{0,12},{2,14},{4,0},{6,2},{8,4},{10,6},{12,8},{14,10},{1,13},{3,15... | collective-permute-start | bytes 1572872 | tf_op jit(solution)/shard_map/ppermute | solution.py:448
  5.2 31.0 %collective-permute-start.2 = (bf16[2,1024,256]{2,1,0:T(8,128)(2,1)}, bf16[2,1024,256]{2,1,0:T(8,128)(2,1)S(1)}, u32[]{:S(2)}, u32[]{:S(2)}) collective-permute-start(bf16[2,1024,256]{2,1,0:T(8,128)(2,1)} %bitcast.20), channel_id=1, source_target_pairs={{0,2},{2,0},{4,6},{6,4},{8,10},{10,8},{12,14},{14,12},{1,3},{3,1},... | collective-permute-start | bytes 3145736 | tf_op jit(solution)/shard_map/ppermute | solution.py:448
  5.2 22.9 %collective-permute-start = (bf16[1024,256]{1,0:T(8,128)(2,1)S(1)}, bf16[1024,256]{1,0:T(8,128)(2,1)S(1)}, u32[]{:S(2)}, u32[]{:S(2)}) collective-permute-start(bf16[1024,256]{1,0:T(8,128)(2,1)S(1)} %get-tuple-element.45.refs_3_), channel_id=1, source_target_pairs={{0,12},{2,14},{4,0},{6,2},{8,4},{10,6},{12,8},{14,10},{1,13},{3,15... | collective-permute-start | bytes 1572872 | tf_op jit(solution)/shard_map/ppermute | solution.py:448
  6.8 24.3 %collective-permute-start.1 = (bf16[1024,256]{1,0:T(8,128)(2,1)S(1)}, bf16[1024,256]{1,0:T(8,128)(2,1)S(1)}, u32[]{:S(2)}, u32[]{:S(2)}) collective-permute-start(bf16[1024,256]{1,0:T(8,128)(2,1)S(1)} %get-tuple-element.44.refs_7_), channel_id=1, source_target_pairs={{0,4},{2,6},{4,8},{6,10},{8,12},{10,14},{12,0},{14,2},{1,5},{3,7},... | collective-permute-start | bytes 1572872 | tf_op jit(solution)/shard_map/ppermute | solution.py:448
  18.0 18.1 %collective-permute-start.4 = (bf16[1024,256]{1,0:T(8,128)(2,1)S(1)}, bf16[1024,256]{1,0:T(8,128)(2,1)S(1)}, u32[]{:S(2)}, u32[]{:S(2)}) collective-permute-start(bf16[1024,256]{1,0:T(8,128)(2,1)S(1)} %collective-permute-done.3.refs_4_), channel_id=1, source_target_pairs={{0,2},{2,0},{4,6},{6,4},{8,10},{10,8},{12,14},{14,12},{1,3},{3,1},... | collective-permute-start | bytes 1572872 | tf_op jit(solution)/shard_map/ppermute | solution.py:448
  18.3 17.9 %collective-permute-start.6 = (bf16[1024,256]{1,0:T(8,128)(2,1)S(1)}, bf16[1024,256]{1,0:T(8,128)(2,1)S(1)}, u32[]{:S(2)}, u32[]{:S(2)}) collective-permute-start(bf16[1024,256]{1,0:T(8,128)(2,1)S(1)} %collective-permute-done.5.refs_8_), channel_id=1, source_target_pairs={{0,2},{2,0},{4,6},{6,4},{8,10},{10,8},{12,14},{14,12},{1,3},{3,1},... | collective-permute-start | bytes 1572872 | tf_op jit(solution)/shard_map/ppermute | solution.py:448
  28.1 12.9 %collective-permute-start.11 = (bf16[1024,256]{1,0:T(8,128)(2,1)S(1)}, bf16[1024,256]{1,0:T(8,128)(2,1)S(1)}, u32[]{:S(2)}, u32[]{:S(2)}) collective-permute-start(bf16[1024,256]{1,0:T(8,128)(2,1)S(1)} %collective-permute-done.5.refs_8_), channel_id=1, source_target_pairs={{0,12},{2,14},{4,0},{6,2},{8,4},{10,6},{12,8},{14,10},{1,13},{3,15... | collective-permute-start | bytes 1572872 | tf_op jit(solution)/shard_map/ppermute | solution.py:448
  31.1 13.4 %collective-permute-start.8 = (bf16[1024,256]{1,0:T(8,128)(2,1)S(1)}, bf16[1024,256]{1,0:T(8,128)(2,1)S(1)}, u32[]{:S(2)}, u32[]{:S(2)}) collective-permute-start(bf16[1024,256]{1,0:T(8,128)(2,1)S(1)} %collective-permute-done.3.refs_4_), channel_id=1, source_target_pairs={{0,4},{2,6},{4,8},{6,10},{8,12},{10,14},{12,0},{14,2},{1,5},{3,7},... | collective-permute-start | bytes 1572872 | tf_op jit(solution)/shard_map/ppermute | solution.py:448
  31.7 23.7 %copy-start.6 = (s32[32]{0:T(128)}, s32[32]{0:T(128)S(1)}, u32[]{:S(2)}) copy-start(s32[32]{0:T(128)S(1)} %shard_map.95.at_ref.refs_0_) | copy-start | bytes 388
  31.7 1.6 %copy-start = (bf16[1,128,8192]{2,1,0:T(8,128)(2,1)S(1)}, bf16[1,128,8192]{2,1,0:T(8,128)(2,1)}, u32[]{:S(2)}) copy-start(bf16[1,128,8192]{2,1,0:T(8,128)(2,1)} %param.8) | copy-start | bytes 6291460
  36.1 19.2 %collective-permute-start.14 = (bf16[128,4096]{1,0:T(8,128)(2,1)S(1)}, bf16[128,4096]{1,0:T(8,128)(2,1)S(1)}, u32[]{:S(2)}, u32[]{:S(2)}) collective-permute-start(bf16[128,4096]{1,0:T(8,128)(2,1)S(1)} %get-tuple-element.35), channel_id=1, source_target_pairs={{0,2},{2,0},{4,6},{6,4},{8,10},{10,8},{12,14},{14,12},{1,3},{3,1},... | collective-permute-start | bytes 3145736 | tf_op jit(solution)/shard_map/ppermute | solution.py:448
  36.3 10.1 %copy-start.3 = (bf16[1,128,2048]{2,1,0:T(8,128)(2,1)S(1)}, bf16[1,128,2048]{2,1,0:T(8,128)(2,1)}, u32[]{:S(2)}) copy-start(bf16[1,128,2048]{2,1,0:T(8,128)(2,1)} %param.11) | copy-start | bytes 1572868
  36.3 10.1 %copy-start.4 = (bf16[1,128,2048]{2,1,0:T(8,128)(2,1)S(1)}, bf16[1,128,2048]{2,1,0:T(8,128)(2,1)}, u32[]{:S(2)}) copy-start(bf16[1,128,2048]{2,1,0:T(8,128)(2,1)} %param.12) | copy-start | bytes 1572868
  36.3 10.1 %copy-start.8 = (s32[128]{0:T(128)S(1)}, s32[128]{0:T(128)}, u32[]{:S(2)}) copy-start(s32[128]{0:T(128)} %param.14) | copy-start | bytes 1540
  39.0 5.5 %collective-permute-start.10 = (bf16[1024,256]{1,0:T(8,128)(2,1)S(1)}, bf16[1024,256]{1,0:T(8,128)(2,1)S(1)}, u32[]{:S(2)}, u32[]{:S(2)}) collective-permute-start(bf16[1024,256]{1,0:T(8,128)(2,1)S(1)} %get-tuple-element.26), channel_id=1, source_target_pairs={{0,2},{2,0},{4,6},{6,4},{8,10},{10,8},{12,14},{14,12},{1,3},{3,1},... | collective-permute-start | bytes 1572872 | tf_op jit(solution)/shard_map/ppermute | solution.py:448
  39.6 4.9 %collective-permute-start.7 = (bf16[1024,256]{1,0:T(8,128)(2,1)S(1)}, bf16[1024,256]{1,0:T(8,128)(2,1)S(1)}, u32[]{:S(2)}, u32[]{:S(2)}) collective-permute-start(bf16[1024,256]{1,0:T(8,128)(2,1)S(1)} %get-tuple-element.25), channel_id=1, source_target_pairs={{0,2},{2,0},{4,6},{6,4},{8,10},{10,8},{12,14},{14,12},{1,3},{3,1},... | collective-permute-start | bytes 1572872 | tf_op jit(solution)/shard_map/ppermute | solution.py:448
  41.0 3.4 %collective-permute-start.12 = (bf16[1024,256]{1,0:T(8,128)(2,1)S(1)}, bf16[1024,256]{1,0:T(8,128)(2,1)S(1)}, u32[]{:S(2)}, u32[]{:S(2)}) collective-permute-start(bf16[1024,256]{1,0:T(8,128)(2,1)S(1)} %collective-permute-done.11.refs_6_), channel_id=1, source_target_pairs={{0,2},{2,0},{4,6},{6,4},{8,10},{10,8},{12,14},{14,12},{1,3},{3,1},... | collective-permute-start | bytes 1572872 | tf_op jit(solution)/shard_map/ppermute | solution.py:448
  44.5 1.9 %collective-permute-start.9 = (bf16[1024,256]{1,0:T(8,128)(2,1)S(1)}, bf16[1024,256]{1,0:T(8,128)(2,1)S(1)}, u32[]{:S(2)}, u32[]{:S(2)}) collective-permute-start(bf16[1024,256]{1,0:T(8,128)(2,1)S(1)} %collective-permute-done.8.refs_3_), channel_id=1, source_target_pairs={{0,2},{2,0},{4,6},{6,4},{8,10},{10,8},{12,14},{14,12},{1,3},{3,1},... | collective-permute-start | bytes 1572872 | tf_op jit(solution)/shard_map/ppermute | solution.py:448
  46.4 3.1 %copy-start.1 = (bf16[1,128,8192]{2,1,0:T(8,128)(2,1)S(1)}, bf16[1,128,8192]{2,1,0:T(8,128)(2,1)}, u32[]{:S(2)}) copy-start(bf16[1,128,8192]{2,1,0:T(8,128)(2,1)} %param.8) | copy-start | bytes 6291460
  52.2 26.8 %collective-permute-start.13 = (bf16[128,4096]{1,0:T(8,128)(2,1)S(1)}, bf16[128,4096]{1,0:T(8,128)(2,1)S(1)}, u32[]{:S(2)}, u32[]{:S(2)}) collective-permute-start(bf16[128,4096]{1,0:T(8,128)(2,1)S(1)} %shard_map.101), channel_id=1, source_target_pairs={{0,1},{1,0},{2,3},{3,2},{4,5},{5,4},{6,7},{7,6},{8,9},{9,8},{10,11... | collective-permute-start | bytes 3145736 | tf_op jit(solution)/shard_map/ppermute | solution.py:486
  52.3 3.0 %collective-permute-start.15 = (bf16[128,512]{1,0:T(8,128)(2,1)S(1)}, bf16[128,512]{1,0:T(8,128)(2,1)S(1)}, u32[]{:S(2)}, u32[]{:S(2)}) collective-permute-start(bf16[128,512]{1,0:T(8,128)(2,1)S(1)} %get-tuple-element.30.grads_ref), channel_id=1, source_target_pairs={{0,2},{2,0},{4,6},{6,4},{8,10},{10,8},{12,14},{14,12},{1,3},{3,1},... | collective-permute-start | bytes 393224 | tf_op jit(solution)/shard_map/ppermute | solution.py:448
  57.3 15.5 %collective-permute-start.16 = (bf16[512,512]{1,0:T(8,128)(2,1)S(1)}, bf16[512,512]{1,0:T(8,128)(2,1)S(1)}, u32[]{:S(2)}, u32[]{:S(2)}) collective-permute-start(bf16[512,512]{1,0:T(8,128)(2,1)S(1)} %get-tuple-element.38), channel_id=1, source_target_pairs={{0,4},{2,6},{4,8},{6,10},{8,12},{10,14},{12,0},{14,2},{1,5},{3,7},... | collective-permute-start | bytes 1572872 | tf_op jit(solution)/shard_map/ppermute | solution.py:448
  57.3 15.4 %collective-permute-start.17 = (bf16[512,512]{1,0:T(8,128)(2,1)S(1)}, bf16[512,512]{1,0:T(8,128)(2,1)S(1)}, u32[]{:S(2)}, u32[]{:S(2)}) collective-permute-start(bf16[512,512]{1,0:T(8,128)(2,1)S(1)} %get-tuple-element.39), channel_id=1, source_target_pairs={{0,12},{2,14},{4,0},{6,2},{8,4},{10,6},{12,8},{14,10},{1,13},{3,15... | collective-permute-start | bytes 1572872 | tf_op jit(solution)/shard_map/ppermute | solution.py:448
  73.9 6.9 %copy-start.9 = (bf16[1024,512]{1,0:T(8,128)(2,1)}, bf16[1024,512]{1,0:T(8,128)(2,1)S(1)}, u32[]{:S(2)}) copy-start(bf16[1024,512]{1,0:T(8,128)(2,1)S(1)} %get-tuple-element.43) | copy-start | bytes 3145732
  79.0 11.2 %copy-start.2 = (bf16[128,4096]{1,0:T(8,128)(2,1)S(1)}, bf16[128,4096]{1,0:T(8,128)(2,1)}, u32[]{:S(2)}) copy-start(bf16[128,4096]{1,0:T(8,128)(2,1)} %in_ref.1) | copy-start | bytes 3145732
  79.0 11.2 %copy-start.7 = (s32[32]{0:T(128)S(1)}, s32[32]{0:T(128)}, u32[]{:S(2)}) copy-start(s32[32]{0:T(128)} %copy-done.6) | copy-start | bytes 388
  80.8 45.4 %copy-start.10 = (s32[1,2,8,2]{2,3,1,0:T(2,128)S(1)}, s32[1,2,8,2]{2,3,1,0:T(2,128)}, u32[]{:S(2)}) copy-start(s32[1,2,8,2]{2,3,1,0:T(2,128)} %param.15) | copy-start | bytes 388
  80.8 35.2 %all-to-all-start = ((bf16[16,8,4096]{2,1,0:T(8,128)(2,1)}), bf16[16,8,4096]{2,1,0:T(8,128)(2,1)S(1)}, u32[]{:S(2)}, u32[]{:S(2)}) async-start(bf16[16,8,4096]{2,1,0:T(8,128)(2,1)} %bitcast.7), calls=%async_computation | async-start | bytes 2097152 | tf_op jit(solution)/shard_map/all_to_all | solution.py:496
  117.6 33.7 %all-to-all-start.1 = ((bf16[16,8,4096]{2,1,0:T(8,128)(2,1)}), bf16[16,8,4096]{2,1,0:T(8,128)(2,1)}, u32[]{:S(2)}, u32[]{:S(2)}) async-start(bf16[16,8,4096]{2,1,0:T(8,128)(2,1)} %shard_map.106), calls=%async_computation.1 | async-start | bytes 2097152 | tf_op jit(solution)/shard_map/all_to_all | solution.py:501
  122.9 26.3 %collective-permute-start.18 = (bf16[1024,512]{1,0:T(8,128)(2,1)}, bf16[1024,512]{1,0:T(8,128)(2,1)S(1)}, u32[]{:S(2)}, u32[]{:S(2)}) collective-permute-start(bf16[1024,512]{1,0:T(8,128)(2,1)} %get-tuple-element.42), channel_id=1, source_target_pairs={{0,4},{2,6},{4,8},{6,10},{8,12},{10,14},{12,0},{14,2},{1,5},{3,7},... | collective-permute-start | bytes 3145736 | tf_op jit(solution)/shard_map/ppermute | solution.py:448
  123.0 26.2 %collective-permute-start.19 = (bf16[1024,512]{1,0:T(8,128)(2,1)}, bf16[1024,512]{1,0:T(8,128)(2,1)S(1)}, u32[]{:S(2)}, u32[]{:S(2)}) collective-permute-start(bf16[1024,512]{1,0:T(8,128)(2,1)} %copy-done.9), channel_id=1, source_target_pairs={{0,12},{2,14},{4,0},{6,2},{8,4},{10,6},{12,8},{14,10},{1,13},{3,15... | collective-permute-start | bytes 3145736 | tf_op jit(solution)/shard_map/ppermute | solution.py:448
  (1 other events, 0.8 us)

commit v4 on v3

--- a/solution.py
+++ b/solution.py
@@ -80,7 +80,7 @@
         out_specs=IN_SMEM,
         out_shape=jax.ShapeDtypeStruct((32,), jnp.int32),
         compiler_params=pltpu.CompilerParams(vmem_limit_bytes=MIB),
-        cost_estimate=cost(0, 0),
+        cost_estimate=cost(1, 1),
     )()
 
 
@@ -120,7 +120,7 @@
             jax.ShapeDtypeStruct((tokens, features // 2), jnp.bfloat16),
         ),
         compiler_params=pltpu.CompilerParams(vmem_limit_bytes=12 * MIB),
-        cost_estimate=cost(0, 0),
+        cost_estimate=cost(1, 1),
     )(places, x, gain)
 
 
@@ -152,7 +152,7 @@
         out_shape=(rows, rows, whole, whole),
         scratch_shapes=[pltpu.SemaphoreType.DMA((count,))] * 2,
         compiler_params=pltpu.CompilerParams(vmem_limit_bytes=16 * MIB),
-        cost_estimate=cost(0, 0),
+        cost_estimate=cost(1, 1),
     )(shards, normed, both, *key_pieces, *value_pieces)
 
 
@@ -241,7 +241,7 @@
         out_shape=[jax.ShapeDtypeStruct(a.shape, a.dtype) for a in arrays],
         input_output_aliases={i: i for i in range(count)},
         compiler_params=pltpu.CompilerParams(vmem_limit_bytes=MIB),
-        cost_estimate=cost(0, 0),
+        cost_estimate=cost(1, 1),
     )(*arrays, after)
 
 
@@ -377,7 +377,7 @@
         ),
         out_shape=jax.ShapeDtypeStruct((rows, width), array.dtype),
         compiler_params=pltpu.CompilerParams(vmem_limit_bytes=MIB),
-        cost_estimate=cost(0, 0),
+        cost_estimate=cost(1, 1),
     )(places, array)
 
 
@@ -427,7 +427,7 @@
         out_specs=pl.BlockSpec((1, rows, columns), lambda p: (p, 0, 0)),
         out_shape=jax.ShapeDtypeStruct((2, rows, columns), jnp.bfloat16),
         compiler_params=pltpu.CompilerParams(vmem_limit_bytes=12 * MIB),
-        cost_estimate=cost(parts[0].size, 10 * parts[0].size),
+        cost_estimate=cost(1e15, 1e12),
     )(factor, *parts)
 
 
@@ -447,16 +447,16 @@
     right, left, other = ring_pairs(lax.axis_size("dp"))
     send = lambda piece, pairs: lax.ppermute(piece, "dp", pairs)
     key_own, value_own = kv_weight[0, 0], kv_weight[0, 1]
+    both = send(kv_weight[0], other)
     key_l = send(key_own, right)
     value_r = send(value_own, left)
-    both = send(kv_weight[0], other)
     key_r = send(key_own, left)
     value_l = send(value_own, right)
+    places = all_places()
+    normed, inv_rms, normed_other = norm(places, inputs, norm_gain)
+    key_l, value_r = ordered((key_l, value_r), inv_rms)
     key_2 = send(key_l, right)
     value_2 = send(value_r, left)
-
-    places = all_places()
-    normed, inv_rms, normed_other = norm(places, inputs, norm_gain)
     normed_sib = send(normed_other, other)
     early = early_rows(
         places,

time: 154 us -> 153 us (level)
  waiting for transfers between devices: 92.6 us -> 89.5 us
  local copies, waits for them, and re-layouts: 6.04 us -> 8.23 us
    all_to_all x1, waiting for transfers between devices: 0.01 us -> 23.5 us  [on_device(): lax.all_to_all(sums.reshape(token_count, branch.shape[1]), 'pipe', 0, 0,...]
    ppermute x19, waiting for transfers between devices: 62.4 us -> 39.2 us  [on_device(): send = lambda piece, pairs: lax.ppermute(piece, 'dp', pairs)]
    all_to_all x1, waiting for transfers between devices: 25.1 us -> 21.7 us  [on_device(): parts = lax.all_to_all(branch, 'pipe', 0, 0, tiled=True)]
    unnamed x23 -> x27, local copies, waits for them, and re-layouts: 4.68 us -> 6.87 us
  transfers between devices with their start and end apart: 22 -> 22, of which waited for: 10 -> 10; matrix products, arithmetic and copies ran while one was open for 0% -> 0% of each run, Pallas kernels for 13% -> 14%
where the time goes in v4:
time: 153 us; the launch traced here: 152 us
  waiting for transfers between devices  89.5 us (58%)
  starting transfers between devices  31 us (20%)
  Pallas kernels  22.7 us (15%)
  local copies, waits for them, and re-layouts  8.23 us (5%)
    ppermute x19, waiting for transfers between devices, on_device(): send = lambda piece, pairs: lax.ppermute(piece, 'dp', pairs)  39.2 us
    all_to_all x1, waiting for transfers between devices, on_device(): lax.all_to_all(sums.reshape(token_count, branch.shape[1]), 'pipe', 0, 0,...  23.5 us
    all_to_all x1, waiting for transfers between devices, on_device(): parts = lax.all_to_all(branch, 'pipe', 0, 0, tiled=True)  21.7 us
    ppermute x19, starting transfers between devices, on_device(): send = lambda piece, pairs: lax.ppermute(piece, 'dp', pairs)  16.3 us
    all_to_all x1, starting transfers between devices, on_device(): parts = lax.all_to_all(branch, 'pipe', 0, 0, tiled=True)  9.29 us
    unnamed x27, local copies, waits for them, and re-layouts  6.87 us
    pallas_call x2, Pallas kernels, partial_branch(): pl.pallas_call(branch_kernel, grid_spec=pltpu.PrefetchScalarGridSpec(num_...  5.51 us
    all_to_all x1, starting transfers between devices, on_device(): lax.all_to_all(sums.reshape(token_count, branch.shape[1]), 'pipe', 0, 0,...  5.27 us
  transfers between devices with their start and end apart: 22, of which 10 were waited for; matrix products, arithmetic and copies ran while one was open for 0% of the time, Pallas kernels for 14%

profile of v4, /device:TPU:16, one launch (start us, length us, event | category | flops | bytes accessed | tf_op | source)
XLA Modules:
  0.0 152.4 jit_solution(7908317478799386854)
XLA Ops:
  0.6 1.3 slice_bitcast_fusion
  1.9 1.6 %collective-permute-start.3 = (bf16[1024,256]{1,0:T(8,128)(2,1)S(1)}, bf16[1024,256]{1,0:T(8,128)(2,1)S(1)}, u32[]{:S(2)}, u32[]{:S(2)}) collective-permute-start(bf16[1024,256]{1,0:T(8,128)(2,1)S(1)} %get-tuple-element.49.refs_3_), channel_id=1, source_target_pairs={{0,4},{2,6},{4,8},{6,10},{8,12},{10,14},{12,0},{14,2},{1,5},{3,7},... | collective-permute-start | bytes 1572872 | tf_op jit(solution)/shard_map/ppermute | solution.py:448
  3.5 1.7 %collective-permute-start.4 = (bf16[1024,256]{1,0:T(8,128)(2,1)S(1)}, bf16[1024,256]{1,0:T(8,128)(2,1)S(1)}, u32[]{:S(2)}, u32[]{:S(2)}) collective-permute-start(bf16[1024,256]{1,0:T(8,128)(2,1)S(1)} %get-tuple-element.48.refs_7_), channel_id=1, source_target_pairs={{0,12},{2,14},{4,0},{6,2},{8,4},{10,6},{12,8},{14,10},{1,13},{3,15... | collective-permute-start | bytes 1572872 | tf_op jit(solution)/shard_map/ppermute | solution.py:448
  5.2 1.5 %collective-permute-start = (bf16[1024,256]{1,0:T(8,128)(2,1)S(1)}, bf16[1024,256]{1,0:T(8,128)(2,1)S(1)}, u32[]{:S(2)}, u32[]{:S(2)}) collective-permute-start(bf16[1024,256]{1,0:T(8,128)(2,1)S(1)} %get-tuple-element.49.refs_3_), channel_id=1, source_target_pairs={{0,12},{2,14},{4,0},{6,2},{8,4},{10,6},{12,8},{14,10},{1,13},{3,15... | collective-permute-start | bytes 1572872 | tf_op jit(solution)/shard_map/ppermute | solution.py:448
  7.9 1.6 %copy-done = bf16[1,128,8192]{2,1,0:T(8,128)(2,1)S(1)} copy-done((bf16[1,128,8192]{2,1,0:T(8,128)(2,1)S(1)}, bf16[1,128,8192]{2,1,0:T(8,128)(2,1)}, u32[]{:S(2)}) %copy-start) | copy-done | bytes 2097176
  9.5 0.8 copy-done.5
  10.2 2.1 %shard_map.96 = (bf16[128,8192]{1,0:T(8,128)(2,1)S(1)}, f32[128,1]{1,0:T(8,128)S(1)}, bf16[128,4096]{1,0:T(8,128)(2,1)S(1)}) custom-call(s32[32]{0:T(128)S(1)} %shard_map.95.at_ref.refs_0_, bf16[128,8192]{1,0:T(8,128)(2,1)S(1)} %bitcast.14, bf16[1,8192]{1,0:T(2,128)(2,1)S(1)} %copy-done.5), custom_call_target="tpu_custom_call" | custom-call | flops 1 | bytes 1 | tf_op jit(solution)/shard_map/pallas_call | solution.py:102
  12.3 5.7 %collective-permute-done.3.refs_0_ = bf16[1024,256]{1,0:T(8,128)(2,1)S(1)} collective-permute-done((bf16[1024,256]{1,0:T(8,128)(2,1)S(1)}, bf16[1024,256]{1,0:T(8,128)(2,1)S(1)}, u32[]{:S(2)}, u32[]{:S(2)}) %collective-permute-start.3) | collective-permute-done | bytes 524320 | tf_op jit(solution)/shard_map/ppermute | solution.py:448
  18.8 9.3 %collective-permute-done.refs_6_.refs_0_ = bf16[1024,256]{1,0:T(8,128)(2,1)S(1)} collective-permute-done((bf16[1024,256]{1,0:T(8,128)(2,1)S(1)}, bf16[1024,256]{1,0:T(8,128)(2,1)S(1)}, u32[]{:S(2)}, u32[]{:S(2)}) %collective-permute-start) | collective-permute-done | bytes 524320 | tf_op jit(solution)/shard_map/ppermute | solution.py:448
  28.1 3.0 %collective-permute-start.11 = (bf16[1024,256]{1,0:T(8,128)(2,1)S(1)}, bf16[1024,256]{1,0:T(8,128)(2,1)S(1)}, u32[]{:S(2)}, u32[]{:S(2)}) collective-permute-start(bf16[1024,256]{1,0:T(8,128)(2,1)S(1)} %get-tuple-element.28.refs_8_), channel_id=1, source_target_pairs={{0,12},{2,14},{4,0},{6,2},{8,4},{10,6},{12,8},{14,10},{1,13},{3,15... | collective-permute-start | bytes 1572872 | tf_op jit(solution)/shard_map/ppermute | solution.py:448
  31.2 2.7 %shard_map.98 = (f32[128,256]{1,0:T(8,128)S(1)}, f32[128,256]{1,0:T(8,128)S(1)}, bf16[8192,256]{1,0:T(8,128)(2,1)S(1)}, bf16[8192,256]{1,0:T(8,128)(2,1)S(1)}) custom-call(s32[32]{0:T(128)S(1)} %shard_map.95.at_ref.refs_0_, bf16[128,8192]{1,0:T(8,128)(2,1)S(1)} %get-tuple-element.25.refs_1_.normed_ref, ...), custom_call_target="tpu_custom_call" | custom-call | flops 1 | bytes 1 | tf_op jit(solution)/shard_map/pallas_call | solution.py:148
  34.6 6.5 %collective-permute-done.11.refs_6_ = bf16[1024,256]{1,0:T(8,128)(2,1)S(1)} collective-permute-done((bf16[1024,256]{1,0:T(8,128)(2,1)S(1)}, bf16[1024,256]{1,0:T(8,128)(2,1)S(1)}, u32[]{:S(2)}, u32[]{:S(2)}) %collective-permute-start.11) | collective-permute-done | bytes 524320 | tf_op jit(solution)/shard_map/ppermute | solution.py:448
  41.0 3.4 %collective-permute-done.8.refs_3_ = bf16[1024,256]{1,0:T(8,128)(2,1)S(1)} collective-permute-done((bf16[1024,256]{1,0:T(8,128)(2,1)S(1)}, bf16[1024,256]{1,0:T(8,128)(2,1)S(1)}, u32[]{:S(2)}, u32[]{:S(2)}) %collective-permute-start.8) | collective-permute-done | bytes 524320 | tf_op jit(solution)/shard_map/ppermute | solution.py:448
  44.5 1.9 %collective-permute-done.9.refs_4_ = bf16[1024,256]{1,0:T(8,128)(2,1)S(1)} collective-permute-done((bf16[1024,256]{1,0:T(8,128)(2,1)S(1)}, bf16[1024,256]{1,0:T(8,128)(2,1)S(1)}, u32[]{:S(2)}, u32[]{:S(2)}) %collective-permute-start.9) | collective-permute-done | bytes 524320 | tf_op jit(solution)/shard_map/ppermute | solution.py:448
  46.4 3.1 %shard_map.100 = (bf16[8192,256]{1,0:T(8,128)(2,1)S(1)}, bf16[8192,256]{1,0:T(8,128)(2,1)S(1)}, bf16[128,512]{1,0:T(8,128)(2,1)S(1)}, f32[128,1]{1,0:T(8,128)S(1)}) custom-call(s32[32]{0:T(128)S(1)} %shard_map.95.at_ref.refs_0_, bf16[128,8192]{1,0:T(8,128)(2,1)S(1)} %get-tuple-element.25.refs_1_.normed_ref, ...), custom_call_target="tpu_custom_call", output_to_operand_aliasing={{0}: (10, {}), {1}: (11, {})} | custom-call | flops 671088640 | bytes 7340032 | tf_op jit(solution)/shard_map/pallas_call | solution.py:215
  49.5 2.7 %shard_map.102 = bf16[128,4096]{1,0:T(8,128)(2,1)S(1)} custom-call(s32[32]{0:T(128)S(1)} %shard_map.95.at_ref.refs_0_, bf16[128,512]{1,0:T(8,128)(2,1)S(1)} %get-tuple-element.35.grads_ref, bf16[8192,256]{1,0:T(8,128)(2,1)S(1)} %get-tuple-element.36.key_w_ref, bf16[8192,256]{1,0:T(8,128)(2,1)S(1)} %get-tuple-element.37.value_w_ref, ...), custom_call_target="tpu_custom_call" | custom-call | flops 536870912 | bytes 5242880 | tf_op jit(solution)/shard_map/pallas_call | solution.py:265
  52.6 2.8 %shard_map.101.after_ref.mine_ref = f32[128,4096]{1,0:T(8,128)S(1)} custom-call(s32[32]{0:T(128)S(1)} %shard_map.95.at_ref.refs_0_, bf16[128,512]{1,0:T(8,128)(2,1)S(1)} %get-tuple-element.35.grads_ref, bf16[8192,256]{1,0:T(8,128)(2,1)S(1)} %get-tuple-element.36.key_w_ref, bf16[8192,256]{1,0:T(8,128)(2,1)S(1)} %get-tuple-element.37.value_w_ref, ...), custom_call_target="tpu_custom_call" | custom-call | flops 536870912 | bytes 5242880 | tf_op jit(solution)/shard_map/pallas_call | solution.py:265
  55.4 1.8 %shard_map.103 = (bf16[1024,512]{1,0:T(8,128)(2,1)S(1)}, bf16[1024,512]{1,0:T(8,128)(2,1)S(1)}, bf16[1024,512]{1,0:T(8,128)(2,1)S(1)}, bf16[512,512]{1,0:T(8,128)(2,1)S(1)}, bf16[512,512]{1,0:T(8,128)(2,1)S(1)}) custom-call(s32[32]{0:T(128)S(1)} %shard_map.95.at_ref.refs_0_, bf16[128,8192]{1,0:T(8,128)(2,1)S(1)} %get-tuple-element.25.refs_1_.normed_ref, ...), custom_call_target="tpu_custom_call" | custom-call | flops 2147483648 | bytes 4194304 | tf_op jit(solution)/shard_map/pallas_call | solution.py:314
  57.3 1.0 copy-done.10
  58.2 3.2 %collective-permute-start.17 = (bf16[512,512]{1,0:T(8,128)(2,1)S(1)}, bf16[512,512]{1,0:T(8,128)(2,1)S(1)}, u32[]{:S(2)}, u32[]{:S(2)}) collective-permute-start(bf16[512,512]{1,0:T(8,128)(2,1)S(1)} %get-tuple-element.43), channel_id=1, source_target_pairs={{0,12},{2,14},{4,0},{6,2},{8,4},{10,6},{12,8},{14,10},{1,13},{3,15... | collective-permute-start | bytes 1572872 | tf_op jit(solution)/shard_map/ppermute | solution.py:448
  61.5 12.2 %collective-permute-done.16.far_right_ref = bf16[512,512]{1,0:T(8,128)(2,1)S(1)} collective-permute-done((bf16[512,512]{1,0:T(8,128)(2,1)S(1)}, bf16[512,512]{1,0:T(8,128)(2,1)S(1)}, u32[]{:S(2)}, u32[]{:S(2)}) %collective-permute-start.16) | collective-permute-done | bytes 524320 | tf_op jit(solution)/shard_map/ppermute | solution.py:448
  73.9 5.1 %collective-permute-done.13.arrived_ref = bf16[128,4096]{1,0:T(8,128)(2,1)S(1)} collective-permute-done((bf16[128,4096]{1,0:T(8,128)(2,1)S(1)}, bf16[128,4096]{1,0:T(8,128)(2,1)S(1)}, u32[]{:S(2)}, u32[]{:S(2)}) %collective-permute-start.13) | collective-permute-done | bytes 1048608 | tf_op jit(solution)/shard_map/ppermute | solution.py:486
  79.0 1.8 %shard_map.105 = bf16[128,4096]{1,0:T(8,128)(2,1)} custom-call(f32[128,4096]{1,0:T(8,128)S(1)} %shard_map.101.after_ref.mine_ref, bf16[128,4096]{1,0:T(8,128)(2,1)S(1)} %collective-permute-done.13.arrived_ref, f32[8,128]{1,0:T(8,128)S(1)} %get-tuple-element.44.token_ref), custom_call_target="tpu_custom_call" | custom-call | flops 999999986991104 | bytes 999999995904 | tf_op jit(solution)/shard_map/pallas_call | solution.py:353
  80.8 9.3 %all-to-all-start = ((bf16[16,8,4096]{2,1,0:T(8,128)(2,1)}), bf16[16,8,4096]{2,1,0:T(8,128)(2,1)S(1)}, u32[]{:S(2)}, u32[]{:S(2)}) async-start(bf16[16,8,4096]{2,1,0:T(8,128)(2,1)} %bitcast.7), calls=%async_computation | async-start | bytes 2097152 | tf_op jit(solution)/shard_map/all_to_all | solution.py:496
  90.2 3.2 %collective-permute-start.19 = (bf16[1024,512]{1,0:T(8,128)(2,1)S(1)}, bf16[1024,512]{1,0:T(8,128)(2,1)}, u32[]{:S(2)}, u32[]{:S(2)}) collective-permute-start(bf16[1024,512]{1,0:T(8,128)(2,1)S(1)} %get-tuple-element.47), channel_id=1, source_target_pairs={{0,12},{2,14},{4,0},{6,2},{8,4},{10,6},{12,8},{14,10},{1,13},{3,15... | collective-permute-start | bytes 3145736 | tf_op jit(solution)/shard_map/ppermute | solution.py:448
  94.1 21.7 %all-to-all-done.parts_ref = bf16[16,8,4096]{2,1,0:T(8,128)(2,1)S(1)} async-done(((bf16[16,8,4096]{2,1,0:T(8,128)(2,1)}), bf16[16,8,4096]{2,1,0:T(8,128)(2,1)S(1)}, u32[]{:S(2)}, u32[]{:S(2)}) %all-to-all-start) | async-done | bytes 1048608 | tf_op jit(solution)/shard_map/all_to_all | solution.py:496
  115.8 1.7 %shard_map.107 = bf16[16,8,4096]{2,1,0:T(8,128)(2,1)} custom-call(bf16[16,8,4096]{2,1,0:T(8,128)(2,1)S(1)} %all-to-all-done.parts_ref, bf16[8,4096]{1,0:T(8,128)(2,1)S(1)} %shard_map.106.top_ref), custom_call_target="tpu_custom_call" | custom-call | flops 524288 | bytes 2097152 | tf_op jit(solution)/shard_map/pallas_call | solution.py:394
  117.5 5.3 %all-to-all-start.1 = ((bf16[16,8,4096]{2,1,0:T(8,128)(2,1)}), bf16[16,8,4096]{2,1,0:T(8,128)(2,1)}, u32[]{:S(2)}, u32[]{:S(2)}) async-start(bf16[16,8,4096]{2,1,0:T(8,128)(2,1)} %shard_map.107), calls=%async_computation.1 | async-start | bytes 2097152 | tf_op jit(solution)/shard_map/all_to_all | solution.py:501
  122.8 1.2 copy-done.11
  124.0 2.6 %shard_map.108 = bf16[2,1024,256]{2,1,0:T(8,128)(2,1)} custom-call(f32[2,8,2]{2,1,0:T(8,128)S(1)} %copy.16.factor_ref, bf16[1024,512]{1,0:T(8,128)(2,1)S(1)} %copy-done.11, bf16[1024,512]{1,0:T(8,128)(2,1)} %collective-permute-done.18.refs_1_, bf16[1024,512]{1,0:T(8,128)(2,1)} %collective-permute-done.19.refs_2_), custom_call_target="tpu_custom_call" | custom-call | flops 999999986991104 | bytes 999999995904 | tf_op jit(solution)/shard_map/pallas_call | solution.py:423
  126.6 23.5 %all-to-all-done.1 = bf16[16,8,4096]{2,1,0:T(8,128)(2,1)} async-done(((bf16[16,8,4096]{2,1,0:T(8,128)(2,1)}), bf16[16,8,4096]{2,1,0:T(8,128)(2,1)}, u32[]{:S(2)}, u32[]{:S(2)}) %all-to-all-start.1) | async-done | bytes 1048608 | tf_op jit(solution)/shard_map/all_to_all | solution.py:501
  150.1 2.3 %copy.24 = bf16[1,128,4096]{2,1,0:T(8,128)(2,1)} copy(bf16[1,128,4096]{2,1,0:T(8,128)(2,1)} %bitcast.8) | data formatting | bytes 2097152
  (56 shorter events, 4.1 us)
Async XLA Ops:
  1.9 16.1 %collective-permute-start.3 = (bf16[1024,256]{1,0:T(8,128)(2,1)S(1)}, bf16[1024,256]{1,0:T(8,128)(2,1)S(1)}, u32[]{:S(2)}, u32[]{:S(2)}) collective-permute-start(bf16[1024,256]{1,0:T(8,128)(2,1)S(1)} %get-tuple-element.49.refs_3_), channel_id=1, source_target_pairs={{0,4},{2,6},{4,8},{6,10},{8,12},{10,14},{12,0},{14,2},{1,5},{3,7},... | collective-permute-start | bytes 1572872 | tf_op jit(solution)/shard_map/ppermute | solution.py:448
  3.5 14.8 %collective-permute-start.4 = (bf16[1024,256]{1,0:T(8,128)(2,1)S(1)}, bf16[1024,256]{1,0:T(8,128)(2,1)S(1)}, u32[]{:S(2)}, u32[]{:S(2)}) collective-permute-start(bf16[1024,256]{1,0:T(8,128)(2,1)S(1)} %get-tuple-element.48.refs_7_), channel_id=1, source_target_pairs={{0,12},{2,14},{4,0},{6,2},{8,4},{10,6},{12,8},{14,10},{1,13},{3,15... | collective-permute-start | bytes 1572872 | tf_op jit(solution)/shard_map/ppermute | solution.py:448
  5.2 26.0 %collective-permute-start.2 = (bf16[2,1024,256]{2,1,0:T(8,128)(2,1)}, bf16[2,1024,256]{2,1,0:T(8,128)(2,1)S(1)}, u32[]{:S(2)}, u32[]{:S(2)}) collective-permute-start(bf16[2,1024,256]{2,1,0:T(8,128)(2,1)} %bitcast.20), channel_id=1, source_target_pairs={{0,2},{2,0},{4,6},{6,4},{8,10},{10,8},{12,14},{14,12},{1,3},{3,1},... | collective-permute-start | bytes 3145736 | tf_op jit(solution)/shard_map/ppermute | solution.py:448
  5.2 22.9 %collective-permute-start = (bf16[1024,256]{1,0:T(8,128)(2,1)S(1)}, bf16[1024,256]{1,0:T(8,128)(2,1)S(1)}, u32[]{:S(2)}, u32[]{:S(2)}) collective-permute-start(bf16[1024,256]{1,0:T(8,128)(2,1)S(1)} %get-tuple-element.49.refs_3_), channel_id=1, source_target_pairs={{0,12},{2,14},{4,0},{6,2},{8,4},{10,6},{12,8},{14,10},{1,13},{3,15... | collective-permute-start | bytes 1572872 | tf_op jit(solution)/shard_map/ppermute | solution.py:448
  6.8 24.3 %collective-permute-start.1 = (bf16[1024,256]{1,0:T(8,128)(2,1)S(1)}, bf16[1024,256]{1,0:T(8,128)(2,1)S(1)}, u32[]{:S(2)}, u32[]{:S(2)}) collective-permute-start(bf16[1024,256]{1,0:T(8,128)(2,1)S(1)} %get-tuple-element.48.refs_7_), channel_id=1, source_target_pairs={{0,4},{2,6},{4,8},{6,10},{8,12},{10,14},{12,0},{14,2},{1,5},{3,7},... | collective-permute-start | bytes 1572872 | tf_op jit(solution)/shard_map/ppermute | solution.py:448
  7.8 47.5 %copy-start.6 = (s32[32]{0:T(128)}, s32[32]{0:T(128)S(1)}, u32[]{:S(2)}) copy-start(s32[32]{0:T(128)S(1)} %shard_map.95.at_ref.refs_0_) | copy-start | bytes 388
  7.9 1.6 %copy-start = (bf16[1,128,8192]{2,1,0:T(8,128)(2,1)S(1)}, bf16[1,128,8192]{2,1,0:T(8,128)(2,1)}, u32[]{:S(2)}) copy-start(bf16[1,128,8192]{2,1,0:T(8,128)(2,1)} %param.8) | copy-start | bytes 6291460
  18.3 12.7 %collective-permute-start.5 = (bf16[1024,256]{1,0:T(8,128)(2,1)S(1)}, bf16[1024,256]{1,0:T(8,128)(2,1)S(1)}, u32[]{:S(2)}, u32[]{:S(2)}) collective-permute-start(bf16[1024,256]{1,0:T(8,128)(2,1)S(1)} %get-tuple-element.27.refs_4_), channel_id=1, source_target_pairs={{0,2},{2,0},{4,6},{6,4},{8,10},{10,8},{12,14},{14,12},{1,3},{3,1},... | collective-permute-start | bytes 1572872 | tf_op jit(solution)/shard_map/ppermute | solution.py:448
  18.3 12.8 %collective-permute-start.6 = (bf16[1024,256]{1,0:T(8,128)(2,1)S(1)}, bf16[1024,256]{1,0:T(8,128)(2,1)S(1)}, u32[]{:S(2)}, u32[]{:S(2)}) collective-permute-start(bf16[1024,256]{1,0:T(8,128)(2,1)S(1)} %get-tuple-element.28.refs_8_), channel_id=1, source_target_pairs={{0,2},{2,0},{4,6},{6,4},{8,10},{10,8},{12,14},{14,12},{1,3},{3,1},... | collective-permute-start | bytes 1572872 | tf_op jit(solution)/shard_map/ppermute | solution.py:448
  28.1 12.9 %collective-permute-start.11 = (bf16[1024,256]{1,0:T(8,128)(2,1)S(1)}, bf16[1024,256]{1,0:T(8,128)(2,1)S(1)}, u32[]{:S(2)}, u32[]{:S(2)}) collective-permute-start(bf16[1024,256]{1,0:T(8,128)(2,1)S(1)} %get-tuple-element.28.refs_8_), channel_id=1, source_target_pairs={{0,12},{2,14},{4,0},{6,2},{8,4},{10,6},{12,8},{14,10},{1,13},{3,15... | collective-permute-start | bytes 1572872 | tf_op jit(solution)/shard_map/ppermute | solution.py:448
  31.1 13.4 %collective-permute-start.8 = (bf16[1024,256]{1,0:T(8,128)(2,1)S(1)}, bf16[1024,256]{1,0:T(8,128)(2,1)S(1)}, u32[]{:S(2)}, u32[]{:S(2)}) collective-permute-start(bf16[1024,256]{1,0:T(8,128)(2,1)S(1)} %get-tuple-element.27.refs_4_), channel_id=1, source_target_pairs={{0,4},{2,6},{4,8},{6,10},{8,12},{10,14},{12,0},{14,2},{1,5},{3,7},... | collective-permute-start | bytes 1572872 | tf_op jit(solution)/shard_map/ppermute | solution.py:448
  31.1 24.3 %collective-permute-start.14 = (bf16[128,4096]{1,0:T(8,128)(2,1)S(1)}, bf16[128,4096]{1,0:T(8,128)(2,1)S(1)}, u32[]{:S(2)}, u32[]{:S(2)}) collective-permute-start(bf16[128,4096]{1,0:T(8,128)(2,1)S(1)} %get-tuple-element.39), channel_id=1, source_target_pairs={{0,2},{2,0},{4,6},{6,4},{8,10},{10,8},{12,14},{14,12},{1,3},{3,1},... | collective-permute-start | bytes 3145736 | tf_op jit(solution)/shard_map/ppermute | solution.py:448
  31.2 15.2 %copy-start.3 = (bf16[1,128,2048]{2,1,0:T(8,128)(2,1)S(1)}, bf16[1,128,2048]{2,1,0:T(8,128)(2,1)}, u32[]{:S(2)}) copy-start(bf16[1,128,2048]{2,1,0:T(8,128)(2,1)} %param.11) | copy-start | bytes 1572868
  31.2 15.2 %copy-start.4 = (bf16[1,128,2048]{2,1,0:T(8,128)(2,1)S(1)}, bf16[1,128,2048]{2,1,0:T(8,128)(2,1)}, u32[]{:S(2)}) copy-start(bf16[1,128,2048]{2,1,0:T(8,128)(2,1)} %param.12) | copy-start | bytes 1572868
  31.2 15.2 %copy-start.8 = (s32[128]{0:T(128)S(1)}, s32[128]{0:T(128)}, u32[]{:S(2)}) copy-start(s32[128]{0:T(128)} %param.14) | copy-start | bytes 1540
  33.9 10.5 %collective-permute-start.10 = (bf16[1024,256]{1,0:T(8,128)(2,1)S(1)}, bf16[1024,256]{1,0:T(8,128)(2,1)S(1)}, u32[]{:S(2)}, u32[]{:S(2)}) collective-permute-start(bf16[1024,256]{1,0:T(8,128)(2,1)S(1)} %get-tuple-element.31), channel_id=1, source_target_pairs={{0,2},{2,0},{4,6},{6,4},{8,10},{10,8},{12,14},{14,12},{1,3},{3,1},... | collective-permute-start | bytes 1572872 | tf_op jit(solution)/shard_map/ppermute | solution.py:448
  34.5 10.0 %collective-permute-start.7 = (bf16[1024,256]{1,0:T(8,128)(2,1)S(1)}, bf16[1024,256]{1,0:T(8,128)(2,1)S(1)}, u32[]{:S(2)}, u32[]{:S(2)}) collective-permute-start(bf16[1024,256]{1,0:T(8,128)(2,1)S(1)} %get-tuple-element.30), channel_id=1, source_target_pairs={{0,2},{2,0},{4,6},{6,4},{8,10},{10,8},{12,14},{14,12},{1,3},{3,1},... | collective-permute-start | bytes 1572872 | tf_op jit(solution)/shard_map/ppermute | solution.py:448
  41.0 3.4 %collective-permute-start.12 = (bf16[1024,256]{1,0:T(8,128)(2,1)S(1)}, bf16[1024,256]{1,0:T(8,128)(2,1)S(1)}, u32[]{:S(2)}, u32[]{:S(2)}) collective-permute-start(bf16[1024,256]{1,0:T(8,128)(2,1)S(1)} %collective-permute-done.11.refs_6_), channel_id=1, source_target_pairs={{0,2},{2,0},{4,6},{6,4},{8,10},{10,8},{12,14},{14,12},{1,3},{3,1},... | collective-permute-start | bytes 1572872 | tf_op jit(solution)/shard_map/ppermute | solution.py:448
  44.5 1.9 %collective-permute-start.9 = (bf16[1024,256]{1,0:T(8,128)(2,1)S(1)}, bf16[1024,256]{1,0:T(8,128)(2,1)S(1)}, u32[]{:S(2)}, u32[]{:S(2)}) collective-permute-start(bf16[1024,256]{1,0:T(8,128)(2,1)S(1)} %collective-permute-done.8.refs_3_), channel_id=1, source_target_pairs={{0,2},{2,0},{4,6},{6,4},{8,10},{10,8},{12,14},{14,12},{1,3},{3,1},... | collective-permute-start | bytes 1572872 | tf_op jit(solution)/shard_map/ppermute | solution.py:448
  46.4 3.1 %copy-start.1 = (bf16[1,128,8192]{2,1,0:T(8,128)(2,1)S(1)}, bf16[1,128,8192]{2,1,0:T(8,128)(2,1)}, u32[]{:S(2)}) copy-start(bf16[1,128,8192]{2,1,0:T(8,128)(2,1)} %param.8) | copy-start | bytes 6291460
  52.3 26.8 %collective-permute-start.13 = (bf16[128,4096]{1,0:T(8,128)(2,1)S(1)}, bf16[128,4096]{1,0:T(8,128)(2,1)S(1)}, u32[]{:S(2)}, u32[]{:S(2)}) collective-permute-start(bf16[128,4096]{1,0:T(8,128)(2,1)S(1)} %shard_map.102), channel_id=1, source_target_pairs={{0,1},{1,0},{2,3},{3,2},{4,5},{5,4},{6,7},{7,6},{8,9},{9,8},{10,11... | collective-permute-start | bytes 3145736 | tf_op jit(solution)/shard_map/ppermute | solution.py:486
  52.4 3.0 %collective-permute-start.15 = (bf16[128,512]{1,0:T(8,128)(2,1)S(1)}, bf16[128,512]{1,0:T(8,128)(2,1)S(1)}, u32[]{:S(2)}, u32[]{:S(2)}) collective-permute-start(bf16[128,512]{1,0:T(8,128)(2,1)S(1)} %get-tuple-element.35.grads_ref), channel_id=1, source_target_pairs={{0,2},{2,0},{4,6},{6,4},{8,10},{10,8},{12,14},{14,12},{1,3},{3,1},... | collective-permute-start | bytes 393224 | tf_op jit(solution)/shard_map/ppermute | solution.py:448
  58.2 15.4 %collective-permute-start.16 = (bf16[512,512]{1,0:T(8,128)(2,1)S(1)}, bf16[512,512]{1,0:T(8,128)(2,1)S(1)}, u32[]{:S(2)}, u32[]{:S(2)}) collective-permute-start(bf16[512,512]{1,0:T(8,128)(2,1)S(1)} %get-tuple-element.42), channel_id=1, source_target_pairs={{0,4},{2,6},{4,8},{6,10},{8,12},{10,14},{12,0},{14,2},{1,5},{3,7},... | collective-permute-start | bytes 1572872 | tf_op jit(solution)/shard_map/ppermute | solution.py:448
  58.2 15.4 %collective-permute-start.17 = (bf16[512,512]{1,0:T(8,128)(2,1)S(1)}, bf16[512,512]{1,0:T(8,128)(2,1)S(1)}, u32[]{:S(2)}, u32[]{:S(2)}) collective-permute-start(bf16[512,512]{1,0:T(8,128)(2,1)S(1)} %get-tuple-element.43), channel_id=1, source_target_pairs={{0,12},{2,14},{4,0},{6,2},{8,4},{10,6},{12,8},{14,10},{1,13},{3,15... | collective-permute-start | bytes 1572872 | tf_op jit(solution)/shard_map/ppermute | solution.py:448
  73.9 6.9 %copy-start.9 = (bf16[1024,512]{1,0:T(8,128)(2,1)}, bf16[1024,512]{1,0:T(8,128)(2,1)S(1)}, u32[]{:S(2)}) copy-start(bf16[1024,512]{1,0:T(8,128)(2,1)S(1)} %get-tuple-element.46) | copy-start | bytes 3145732
  79.0 14.4 %copy-start.2 = (bf16[128,4096]{1,0:T(8,128)(2,1)S(1)}, bf16[128,4096]{1,0:T(8,128)(2,1)}, u32[]{:S(2)}) copy-start(bf16[128,4096]{1,0:T(8,128)(2,1)} %in_ref.1) | copy-start | bytes 3145732
  79.0 14.4 %copy-start.7 = (s32[32]{0:T(128)S(1)}, s32[32]{0:T(128)}, u32[]{:S(2)}) copy-start(s32[32]{0:T(128)} %copy-done.6) | copy-start | bytes 388
  79.0 15.0 %copy-start.12 = (s32[1,2,8,2]{2,3,1,0:T(2,128)S(1)}, s32[1,2,8,2]{2,3,1,0:T(2,128)}, u32[]{:S(2)}) copy-start(s32[1,2,8,2]{2,3,1,0:T(2,128)} %param.15) | copy-start | bytes 388
  80.8 35.0 %all-to-all-start = ((bf16[16,8,4096]{2,1,0:T(8,128)(2,1)}), bf16[16,8,4096]{2,1,0:T(8,128)(2,1)S(1)}, u32[]{:S(2)}, u32[]{:S(2)}) async-start(bf16[16,8,4096]{2,1,0:T(8,128)(2,1)} %bitcast.7), calls=%async_computation | async-start | bytes 2097152 | tf_op jit(solution)/shard_map/all_to_all | solution.py:496
  90.1 32.7 %collective-permute-start.18 = (bf16[1024,512]{1,0:T(8,128)(2,1)}, bf16[1024,512]{1,0:T(8,128)(2,1)}, u32[]{:S(2)}, u32[]{:S(2)}) collective-permute-start(bf16[1024,512]{1,0:T(8,128)(2,1)} %copy-done.9), channel_id=1, source_target_pairs={{0,4},{2,6},{4,8},{6,10},{8,12},{10,14},{12,0},{14,2},{1,5},{3,7},... | collective-permute-start | bytes 3145736 | tf_op jit(solution)/shard_map/ppermute | solution.py:448
  90.2 32.6 %collective-permute-start.19 = (bf16[1024,512]{1,0:T(8,128)(2,1)S(1)}, bf16[1024,512]{1,0:T(8,128)(2,1)}, u32[]{:S(2)}, u32[]{:S(2)}) collective-permute-start(bf16[1024,512]{1,0:T(8,128)(2,1)S(1)} %get-tuple-element.47), channel_id=1, source_target_pairs={{0,12},{2,14},{4,0},{6,2},{8,4},{10,6},{12,8},{14,10},{1,13},{3,15... | collective-permute-start | bytes 3145736 | tf_op jit(solution)/shard_map/ppermute | solution.py:448
  117.5 32.6 %all-to-all-start.1 = ((bf16[16,8,4096]{2,1,0:T(8,128)(2,1)}), bf16[16,8,4096]{2,1,0:T(8,128)(2,1)}, u32[]{:S(2)}, u32[]{:S(2)}) async-start(bf16[16,8,4096]{2,1,0:T(8,128)(2,1)} %shard_map.107), calls=%async_computation.1 | async-start | bytes 2097152 | tf_op jit(solution)/shard_map/all_to_all | solution.py:501
  (3 other events, 3.0 us)

commit v5 on v4

--- a/solution.py
+++ b/solution.py
@@ -245,41 +245,31 @@
     )(*arrays, after)
 
 
-def branch_kernel(at_ref, grads_ref, key_w_ref, value_w_ref, x_ref, gain_ref, rms_ref, inner_ref, out_ref):
+def branch_kernel(
+    at_ref, grads_ref, key_w_ref, value_w_ref, x_ref, gain_ref, rms_ref, inner_ref, out_ref, *, half
+):
     columns = key_w_ref.shape[1]
-    d_normed = dot(grads_ref[:, :columns], key_w_ref[...], NT)
-    d_normed = d_normed + dot(grads_ref[:, columns:], value_w_ref[...], NT)
+    key_grad, value_grad = grads_ref[:, :columns], grads_ref[:, columns:]
     rms = rms_ref[...]
-    x_hat = x_ref[...].astype(jnp.float32) * rms
-    gated = gain_ref[...].astype(jnp.float32) * d_normed
-    out_ref[...] = (rms * (gated - x_hat * inner_ref[...])).astype(out_ref.dtype)
+    shift = rms * inner_ref[...]
+    for i in range(out_ref.shape[1] // TILE):
+        at = pl.ds(pl.multiple_of((at_ref[half] + i) * TILE, TILE), TILE)
+        d_normed = dot(key_grad, key_w_ref[at, :], NT) + dot(value_grad, value_w_ref[at, :], NT)
+        gated = gain_ref[:, at].astype(jnp.float32) * d_normed
+        branch = rms * (gated - x_ref[:, at].astype(jnp.float32) * shift)
+        out_ref[:, i * TILE : (i + 1) * TILE] = branch.astype(out_ref.dtype)
 
 
 def partial_branch(places, half, kind, grads, key_w, value_w, x, gain, inv_rms, inner):
     tokens = grads.shape[0]
     columns = key_w.shape[1]
     width = TILE * HALF_TILES
-    whole = lambda i, at: (0, 0)
-    rows = lambda i, at: (at[half] + i, 0)
-    lanes = lambda i, at: (0, at[half] + i)
-    return pl.pallas_call(
-        branch_kernel,
-        grid_spec=pltpu.PrefetchScalarGridSpec(
-            num_scalar_prefetch=1,
-            grid=(HALF_TILES,),
-            in_specs=[
-                pl.BlockSpec((tokens, 2 * columns), whole),
-                pl.BlockSpec((TILE, columns), rows),
-                pl.BlockSpec((TILE, columns), rows),
-                pl.BlockSpec((tokens, TILE), lanes),
-                pl.BlockSpec((1, TILE), lanes),
-                pl.BlockSpec((tokens, 1), whole),
-                pl.BlockSpec((tokens, 1), whole),
-            ],
-            out_specs=pl.BlockSpec((tokens, TILE), lambda i, at: (0, i)),
-        ),
+    return pl.pallas_call(
+        lambda *refs: branch_kernel(*refs, half=half),
+        in_specs=[IN_SMEM] + in_vmem(7),
+        out_specs=pl.BlockSpec(memory_space=pltpu.VMEM),
         out_shape=jax.ShapeDtypeStruct((tokens, width), kind),
-        compiler_params=pltpu.CompilerParams(vmem_limit_bytes=8 * MIB),
+        compiler_params=pltpu.CompilerParams(vmem_limit_bytes=20 * MIB),
         cost_estimate=cost(
             4 * tokens * width * columns, 4 * width * columns + 2 * width * tokens
         ),
@@ -343,19 +333,28 @@
     )(right, left, far_right, far_left)
 
 
-def add_kernel(mine_ref, arrived_ref, token_ref, out_ref):
-    out_ref[...] = (mine_ref[...] + arrived_ref[...].astype(jnp.float32)).astype(out_ref.dtype)
+def add_kernel(mine_ref, arrived_ref, token_ref, out_ref, held, sems):
+    copies = []
+    rows = held.shape[0] // sems.shape[0]
+    for i in range(sems.shape[0]):
+        at = pl.ds(i * rows, rows)
+        held[at, :] = (mine_ref[at, :] + arrived_ref[at, :].astype(jnp.float32)).astype(held.dtype)
+        copies.append(pltpu.make_async_copy(held.at[at, :], out_ref.at[at, :], sems.at[i]))
+        copies[-1].start()
+    for copy in copies:
+        copy.wait()
 
 
 def add_halves(mine, arrived, token):
-    tokens, width = mine.shape
-    spec = pl.BlockSpec((tokens, TILE), lambda i: (0, i))
     return pl.pallas_call(
         add_kernel,
-        grid=(width // TILE,),
-        in_specs=[spec, spec, ANYWHERE],
-        out_specs=spec,
+        in_specs=in_vmem(2) + [ANYWHERE],
+        out_specs=ANYWHERE,
         out_shape=jax.ShapeDtypeStruct(mine.shape, jnp.bfloat16),
+        scratch_shapes=[
+            pltpu.VMEM(mine.shape, jnp.bfloat16),
+            pltpu.SemaphoreType.DMA((4,)),
+        ],
         compiler_params=pltpu.CompilerParams(vmem_limit_bytes=8 * MIB),
         cost_estimate=cost(1e15, 1e12),
     )(mine, arrived, token)
@@ -381,28 +380,69 @@
     )(places, array)
 
 
-def suffix_kernel(parts_ref, top_ref, out_ref):
-    running = top_ref[...].astype(jnp.float32)
-    for layer in reversed(range(parts_ref.shape[0])):
-        running = running + parts_ref[layer].astype(jnp.float32)
-        out_ref[layer] = running.astype(jnp.bfloat16)
+def suffix_kernel(parts_ref, top_ref, out_ref, held, sems):
+    copies = []
+    width = held.shape[2] // sems.shape[0]
+    for i in range(sems.shape[0]):
+        at = pl.ds(i * width, width)
+        running = top_ref[:, at].astype(jnp.float32)
+        for layer in reversed(range(parts_ref.shape[0])):
+            running = running + parts_ref[layer, :, at].astype(jnp.float32)
+            held[layer, :, at] = running.astype(jnp.bfloat16)
+        copies.append(
+            pltpu.make_async_copy(held.at[:, :, at], out_ref.at[:, :, at], sems.at[i])
+        )
+        copies[-1].start()
+    for copy in copies:
+        copy.wait()
 
 
 def suffix_sum(parts, top):
-    layers, rows, width = parts.shape
-    tile = min(width, 1024)
     return pl.pallas_call(
         suffix_kernel,
-        grid=(width // tile,),
-        in_specs=[
-            pl.BlockSpec((layers, rows, tile), lambda i: (0, 0, i)),
-            pl.BlockSpec((rows, tile), lambda i: (0, i)),
+        in_specs=in_vmem(2),
+        out_specs=ANYWHERE,
+        out_shape=jax.ShapeDtypeStruct(parts.shape, jnp.bfloat16),
+        scratch_shapes=[
+            pltpu.VMEM(parts.shape, jnp.bfloat16),
+            pltpu.SemaphoreType.DMA((4,)),
         ],
-        out_specs=pl.BlockSpec((layers, rows, tile), lambda i: (0, 0, i)),
-        out_shape=jax.ShapeDtypeStruct(parts.shape, jnp.bfloat16),
         compiler_params=pltpu.CompilerParams(vmem_limit_bytes=8 * MIB),
         cost_estimate=cost(parts.size, 4 * parts.size),
     )(parts, top)
+
+
+def move_kernel(in_ref, out_ref, held, in_sems, out_sems):
+    count = in_sems.shape[0]
+    rows = held.shape[0] // count
+    arriving, leaving = [], []
+    for i in range(count):
+        at = pl.ds(i * rows, rows)
+        arriving.append(pltpu.make_async_copy(in_ref.at[at, :], held.at[at, :], in_sems.at[i]))
+        leaving.append(pltpu.make_async_copy(held.at[at, :], out_ref.at[at, :], out_sems.at[i]))
+    for copy in arriving:
+        copy.start()
+    for i in range(count):
+        arriving[i].wait()
+        leaving[i].start()
+    for copy in leaving:
+        copy.wait()
+
+
+def moved(array):
+    return pl.pallas_call(
+        move_kernel,
+        in_specs=[ANYWHERE],
+        out_specs=ANYWHERE,
+        out_shape=jax.ShapeDtypeStruct(array.shape, array.dtype),
+        scratch_shapes=[
+            pltpu.VMEM(array.shape, array.dtype),
+            pltpu.SemaphoreType.DMA((4,)),
+            pltpu.SemaphoreType.DMA((4,)),
+        ],
+        compiler_params=pltpu.CompilerParams(vmem_limit_bytes=4 * MIB),
+        cost_estimate=cost(1, 1),
+    )(array)
 
 
 def scale_kernel(factor_ref, *refs):
@@ -502,7 +542,7 @@
         sums.reshape(token_count, branch.shape[1]), "pipe", 0, 0, tiled=True
     )
     weight_grad = scaled_grad([own, *received], jnp.exp2(-scale_exp[0].astype(jnp.float32)))
-    return (input_grad[None], weight_grad[None])
+    return (moved(input_grad)[None], weight_grad[None])
 
 
 def solution(mesh):

time: 153 us -> 151 us (0.987)
  local copies, waits for them, and re-layouts: 8.23 us -> 5.97 us
    unnamed x27 -> x28, local copies, waits for them, and re-layouts: 6.87 us -> 4.61 us
    pallas_call x4 -> x5, Pallas kernels: 8.93 us -> 8.18 us  [the longest x2 4.12 us: partial_branch(): pl.pallas_call(lambda *refs: branch_kernel(*refs, half=half), in_specs=[I...]
  transfers between devices with their start and end apart: 22 -> 22, of which waited for: 10 -> 10; matrix products, arithmetic and copies ran while one was open for 0% -> 0% of each run, Pallas kernels for 14% -> 13%
where the time goes in v5:
time: 151 us; the launch traced here: 150 us
  waiting for transfers between devices  90.2 us (60%)
  starting transfers between devices  31 us (21%)
  Pallas kernels  22 us (15%)
  local copies, waits for them, and re-layouts  5.97 us (4%)
    ppermute x19, waiting for transfers between devices, on_device(): send = lambda piece, pairs: lax.ppermute(piece, 'dp', pairs)  39.2 us
    all_to_all x1, waiting for transfers between devices, on_device(): lax.all_to_all(sums.reshape(token_count, branch.shape[1]), 'pipe', 0, 0,...  23.5 us
    all_to_all x1, waiting for transfers between devices, on_device(): parts = lax.all_to_all(branch, 'pipe', 0, 0, tiled=True)  21.7 us
    ppermute x19, starting transfers between devices, on_device(): send = lambda piece, pairs: lax.ppermute(piece, 'dp', pairs)  16.3 us
    all_to_all x1, starting transfers between devices, on_device(): parts = lax.all_to_all(branch, 'pipe', 0, 0, tiled=True)  9.31 us
    ppermute x1, waiting for transfers between devices, on_device(): lax.ppermute(share(THEIRS, jnp.bfloat16), 'tensor', [(0, 1), (1, 0)])  5.81 us
    all_to_all x1, starting transfers between devices, on_device(): lax.all_to_all(sums.reshape(token_count, branch.shape[1]), 'pipe', 0, 0,...  5.28 us
    unnamed x28, local copies, waits for them, and re-layouts  4.61 us
  transfers between devices with their start and end apart: 22, of which 10 were waited for; matrix products, arithmetic and copies ran while one was open for 0% of the time, Pallas kernels for 13%

profile of v5, /device:TPU:16, one launch (start us, length us, event | category | flops | bytes accessed | tf_op | source)
XLA Modules:
  0.0 150.3 jit_solution(11070136916581045606)
XLA Ops:
  0.6 1.3 slice_bitcast_fusion
  1.9 1.6 %collective-permute-start.3 = (bf16[1024,256]{1,0:T(8,128)(2,1)S(1)}, bf16[1024,256]{1,0:T(8,128)(2,1)S(1)}, u32[]{:S(2)}, u32[]{:S(2)}) collective-permute-start(bf16[1024,256]{1,0:T(8,128)(2,1)S(1)} %get-tuple-element.49.refs_3_), channel_id=1, source_target_pairs={{0,4},{2,6},{4,8},{6,10},{8,12},{10,14},{12,0},{14,2},{1,5},{3,7},... | collective-permute-start | bytes 1572872 | tf_op jit(solution)/shard_map/ppermute | solution.py:488
  3.5 1.7 %collective-permute-start.4 = (bf16[1024,256]{1,0:T(8,128)(2,1)S(1)}, bf16[1024,256]{1,0:T(8,128)(2,1)S(1)}, u32[]{:S(2)}, u32[]{:S(2)}) collective-permute-start(bf16[1024,256]{1,0:T(8,128)(2,1)S(1)} %get-tuple-element.48.refs_7_), channel_id=1, source_target_pairs={{0,12},{2,14},{4,0},{6,2},{8,4},{10,6},{12,8},{14,10},{1,13},{3,15... | collective-permute-start | bytes 1572872 | tf_op jit(solution)/shard_map/ppermute | solution.py:488
  5.2 1.5 %collective-permute-start = (bf16[1024,256]{1,0:T(8,128)(2,1)S(1)}, bf16[1024,256]{1,0:T(8,128)(2,1)S(1)}, u32[]{:S(2)}, u32[]{:S(2)}) collective-permute-start(bf16[1024,256]{1,0:T(8,128)(2,1)S(1)} %get-tuple-element.49.refs_3_), channel_id=1, source_target_pairs={{0,12},{2,14},{4,0},{6,2},{8,4},{10,6},{12,8},{14,10},{1,13},{3,15... | collective-permute-start | bytes 1572872 | tf_op jit(solution)/shard_map/ppermute | solution.py:488
  7.9 1.6 %copy-done = bf16[1,128,8192]{2,1,0:T(8,128)(2,1)S(1)} copy-done((bf16[1,128,8192]{2,1,0:T(8,128)(2,1)S(1)}, bf16[1,128,8192]{2,1,0:T(8,128)(2,1)}, u32[]{:S(2)}) %copy-start) | copy-done | bytes 2097176
  9.5 0.8 copy-done.5
  10.2 2.1 %shard_map.96 = (bf16[128,8192]{1,0:T(8,128)(2,1)S(1)}, f32[128,1]{1,0:T(8,128)S(1)}, bf16[128,4096]{1,0:T(8,128)(2,1)S(1)}) custom-call(s32[32]{0:T(128)S(1)} %shard_map.95.at_ref.refs_0_, bf16[128,8192]{1,0:T(8,128)(2,1)S(1)} %bitcast.15, bf16[1,8192]{1,0:T(2,128)(2,1)S(1)} %copy-done.5), custom_call_target="tpu_custom_call" | custom-call | flops 1 | bytes 1 | tf_op jit(solution)/shard_map/pallas_call | solution.py:102
  12.3 5.7 %collective-permute-done.3.refs_0_ = bf16[1024,256]{1,0:T(8,128)(2,1)S(1)} collective-permute-done((bf16[1024,256]{1,0:T(8,128)(2,1)S(1)}, bf16[1024,256]{1,0:T(8,128)(2,1)S(1)}, u32[]{:S(2)}, u32[]{:S(2)}) %collective-permute-start.3) | collective-permute-done | bytes 524320 | tf_op jit(solution)/shard_map/ppermute | solution.py:488
  18.8 9.3 %collective-permute-done.refs_6_.refs_0_ = bf16[1024,256]{1,0:T(8,128)(2,1)S(1)} collective-permute-done((bf16[1024,256]{1,0:T(8,128)(2,1)S(1)}, bf16[1024,256]{1,0:T(8,128)(2,1)S(1)}, u32[]{:S(2)}, u32[]{:S(2)}) %collective-permute-start) | collective-permute-done | bytes 524320 | tf_op jit(solution)/shard_map/ppermute | solution.py:488
  28.1 3.0 %collective-permute-start.11 = (bf16[1024,256]{1,0:T(8,128)(2,1)S(1)}, bf16[1024,256]{1,0:T(8,128)(2,1)S(1)}, u32[]{:S(2)}, u32[]{:S(2)}) collective-permute-start(bf16[1024,256]{1,0:T(8,128)(2,1)S(1)} %get-tuple-element.28.refs_8_), channel_id=1, source_target_pairs={{0,12},{2,14},{4,0},{6,2},{8,4},{10,6},{12,8},{14,10},{1,13},{3,15... | collective-permute-start | bytes 1572872 | tf_op jit(solution)/shard_map/ppermute | solution.py:488
  31.2 2.7 %shard_map.98 = (f32[128,256]{1,0:T(8,128)S(1)}, f32[128,256]{1,0:T(8,128)S(1)}, bf16[8192,256]{1,0:T(8,128)(2,1)S(1)}, bf16[8192,256]{1,0:T(8,128)(2,1)S(1)}) custom-call(s32[32]{0:T(128)S(1)} %shard_map.95.at_ref.refs_0_, bf16[128,8192]{1,0:T(8,128)(2,1)S(1)} %get-tuple-element.25.refs_1_.normed_ref, ...), custom_call_target="tpu_custom_call" | custom-call | flops 1 | bytes 1 | tf_op jit(solution)/shard_map/pallas_call | solution.py:148
  34.6 6.5 %collective-permute-done.11.refs_6_ = bf16[1024,256]{1,0:T(8,128)(2,1)S(1)} collective-permute-done((bf16[1024,256]{1,0:T(8,128)(2,1)S(1)}, bf16[1024,256]{1,0:T(8,128)(2,1)S(1)}, u32[]{:S(2)}, u32[]{:S(2)}) %collective-permute-start.11) | collective-permute-done | bytes 524320 | tf_op jit(solution)/shard_map/ppermute | solution.py:488
  41.0 3.4 %collective-permute-done.8.refs_3_ = bf16[1024,256]{1,0:T(8,128)(2,1)S(1)} collective-permute-done((bf16[1024,256]{1,0:T(8,128)(2,1)S(1)}, bf16[1024,256]{1,0:T(8,128)(2,1)S(1)}, u32[]{:S(2)}, u32[]{:S(2)}) %collective-permute-start.8) | collective-permute-done | bytes 524320 | tf_op jit(solution)/shard_map/ppermute | solution.py:488
  44.5 1.9 %collective-permute-done.9.refs_4_ = bf16[1024,256]{1,0:T(8,128)(2,1)S(1)} collective-permute-done((bf16[1024,256]{1,0:T(8,128)(2,1)S(1)}, bf16[1024,256]{1,0:T(8,128)(2,1)S(1)}, u32[]{:S(2)}, u32[]{:S(2)}) %collective-permute-start.9) | collective-permute-done | bytes 524320 | tf_op jit(solution)/shard_map/ppermute | solution.py:488
  46.4 3.1 %shard_map.100 = (bf16[8192,256]{1,0:T(8,128)(2,1)S(1)}, bf16[8192,256]{1,0:T(8,128)(2,1)S(1)}, bf16[128,512]{1,0:T(8,128)(2,1)S(1)}, f32[128,1]{1,0:T(8,128)S(1)}) custom-call(s32[32]{0:T(128)S(1)} %shard_map.95.at_ref.refs_0_, bf16[128,8192]{1,0:T(8,128)(2,1)S(1)} %get-tuple-element.25.refs_1_.normed_ref, ...), custom_call_target="tpu_custom_call", output_to_operand_aliasing={{0}: (10, {}), {1}: (11, {})} | custom-call | flops 671088640 | bytes 7340032 | tf_op jit(solution)/shard_map/pallas_call | solution.py:215
  49.6 2.1 %shard_map.102 = bf16[128,4096]{1,0:T(8,128)(2,1)S(1)} custom-call(s32[32]{0:T(128)S(1)} %shard_map.95.at_ref.refs_0_, bf16[128,512]{1,0:T(8,128)(2,1)S(1)} %get-tuple-element.35.refs_1_.grads_ref, bf16[8192,256]{1,0:T(8,128)(2,1)S(1)} %get-tuple-element.36.refs_2_, bf16[8192,256]{1,0:T(8,128)(2,1)S(1)} %get-tuple-element.37.refs_3_, ...), custom_call_target="tpu_custom_call" | custom-call | flops 536870912 | bytes 5242880 | tf_op jit(solution)/shard_map/pallas_call | solution.py:267
  51.9 2.1 %shard_map.101.after_ref.mine_ref = f32[128,4096]{1,0:T(8,128)S(1)} custom-call(s32[32]{0:T(128)S(1)} %shard_map.95.at_ref.refs_0_, bf16[128,512]{1,0:T(8,128)(2,1)S(1)} %get-tuple-element.35.refs_1_.grads_ref, bf16[8192,256]{1,0:T(8,128)(2,1)S(1)} %get-tuple-element.36.refs_2_, bf16[8192,256]{1,0:T(8,128)(2,1)S(1)} %get-tuple-element.37.refs_3_, ...), custom_call_target="tpu_custom_call" | custom-call | flops 536870912 | bytes 5242880 | tf_op jit(solution)/shard_map/pallas_call | solution.py:267
  54.0 1.8 %shard_map.103 = (bf16[1024,512]{1,0:T(8,128)(2,1)S(1)}, bf16[1024,512]{1,0:T(8,128)(2,1)S(1)}, bf16[1024,512]{1,0:T(8,128)(2,1)S(1)}, bf16[512,512]{1,0:T(8,128)(2,1)S(1)}, bf16[512,512]{1,0:T(8,128)(2,1)S(1)}) custom-call(s32[32]{0:T(128)S(1)} %shard_map.95.at_ref.refs_0_, bf16[128,8192]{1,0:T(8,128)(2,1)S(1)} %get-tuple-element.25.refs_1_.normed_ref, ...), custom_call_target="tpu_custom_call" | custom-call | flops 2147483648 | bytes 4194304 | tf_op jit(solution)/shard_map/pallas_call | solution.py:304
  55.9 1.0 copy-done.11
  56.9 3.2 %collective-permute-start.17 = (bf16[512,512]{1,0:T(8,128)(2,1)S(1)}, bf16[512,512]{1,0:T(8,128)(2,1)S(1)}, u32[]{:S(2)}, u32[]{:S(2)}) collective-permute-start(bf16[512,512]{1,0:T(8,128)(2,1)S(1)} %get-tuple-element.43), channel_id=1, source_target_pairs={{0,12},{2,14},{4,0},{6,2},{8,4},{10,6},{12,8},{14,10},{1,13},{3,15... | collective-permute-start | bytes 1572872 | tf_op jit(solution)/shard_map/ppermute | solution.py:488
  60.1 12.2 %collective-permute-done.16.far_right_ref = bf16[512,512]{1,0:T(8,128)(2,1)S(1)} collective-permute-done((bf16[512,512]{1,0:T(8,128)(2,1)S(1)}, bf16[512,512]{1,0:T(8,128)(2,1)S(1)}, u32[]{:S(2)}, u32[]{:S(2)}) %collective-permute-start.16) | collective-permute-done | bytes 524320 | tf_op jit(solution)/shard_map/ppermute | solution.py:488
  72.6 5.8 %collective-permute-done.13.arrived_ref = bf16[128,4096]{1,0:T(8,128)(2,1)S(1)} collective-permute-done((bf16[128,4096]{1,0:T(8,128)(2,1)S(1)}, bf16[128,4096]{1,0:T(8,128)(2,1)S(1)}, u32[]{:S(2)}, u32[]{:S(2)}) %collective-permute-start.13) | collective-permute-done | bytes 1048608 | tf_op jit(solution)/shard_map/ppermute | solution.py:526
  78.4 1.0 shard_map.105
  79.5 9.3 %all-to-all-start = ((bf16[16,8,4096]{2,1,0:T(8,128)(2,1)}), bf16[16,8,4096]{2,1,0:T(8,128)(2,1)S(1)}, u32[]{:S(2)}, u32[]{:S(2)}) async-start(bf16[16,8,4096]{2,1,0:T(8,128)(2,1)} %bitcast.7), calls=%async_computation | async-start | bytes 2097152 | tf_op jit(solution)/shard_map/all_to_all | solution.py:536
  88.9 3.2 %collective-permute-start.19 = (bf16[1024,512]{1,0:T(8,128)(2,1)S(1)}, bf16[1024,512]{1,0:T(8,128)(2,1)}, u32[]{:S(2)}, u32[]{:S(2)}) collective-permute-start(bf16[1024,512]{1,0:T(8,128)(2,1)S(1)} %get-tuple-element.47), channel_id=1, source_target_pairs={{0,12},{2,14},{4,0},{6,2},{8,4},{10,6},{12,8},{14,10},{1,13},{3,15... | collective-permute-start | bytes 3145736 | tf_op jit(solution)/shard_map/ppermute | solution.py:488
  92.8 21.7 %all-to-all-done.parts_ref = bf16[16,8,4096]{2,1,0:T(8,128)(2,1)S(1)} async-done(((bf16[16,8,4096]{2,1,0:T(8,128)(2,1)}), bf16[16,8,4096]{2,1,0:T(8,128)(2,1)S(1)}, u32[]{:S(2)}, u32[]{:S(2)}) %all-to-all-start) | async-done | bytes 1048608 | tf_op jit(solution)/shard_map/all_to_all | solution.py:536
  114.5 1.0 shard_map.107
  115.6 5.3 %all-to-all-start.1 = ((bf16[16,8,4096]{2,1,0:T(8,128)(2,1)}), bf16[16,8,4096]{2,1,0:T(8,128)(2,1)}, u32[]{:S(2)}, u32[]{:S(2)}) async-start(bf16[16,8,4096]{2,1,0:T(8,128)(2,1)} %shard_map.107), calls=%async_computation.1 | async-start | bytes 2097152 | tf_op jit(solution)/shard_map/all_to_all | solution.py:541
  120.9 1.2 copy-done.12
  122.1 2.6 %shard_map.109 = bf16[2,1024,256]{2,1,0:T(8,128)(2,1)} custom-call(f32[2,8,2]{2,1,0:T(8,128)S(1)} %copy.16.factor_ref, bf16[1024,512]{1,0:T(8,128)(2,1)S(1)} %copy-done.12, bf16[1024,512]{1,0:T(8,128)(2,1)} %collective-permute-done.18.refs_1_, bf16[1024,512]{1,0:T(8,128)(2,1)} %collective-permute-done.19.refs_2_), custom_call_target="tpu_custom_call" | custom-call | flops 999999986991104 | bytes 999999995904 | tf_op jit(solution)/shard_map/pallas_call | solution.py:463
  124.7 23.5 %all-to-all-done.1 = bf16[16,8,4096]{2,1,0:T(8,128)(2,1)} async-done(((bf16[16,8,4096]{2,1,0:T(8,128)(2,1)}), bf16[16,8,4096]{2,1,0:T(8,128)(2,1)}, u32[]{:S(2)}, u32[]{:S(2)}) %all-to-all-start.1) | async-done | bytes 1048608 | tf_op jit(solution)/shard_map/all_to_all | solution.py:541
  148.2 2.0 %shard_map.108 = bf16[128,4096]{1,0:T(8,128)(2,1)} custom-call(bf16[128,4096]{1,0:T(8,128)(2,1)} %bitcast.8.in_ref), custom_call_target="tpu_custom_call" | custom-call | flops 1 | bytes 1 | tf_op jit(solution)/shard_map/pallas_call | solution.py:433
  (58 shorter events, 4.1 us)
Async XLA Ops:
  1.9 16.1 %collective-permute-start.3 = (bf16[1024,256]{1,0:T(8,128)(2,1)S(1)}, bf16[1024,256]{1,0:T(8,128)(2,1)S(1)}, u32[]{:S(2)}, u32[]{:S(2)}) collective-permute-start(bf16[1024,256]{1,0:T(8,128)(2,1)S(1)} %get-tuple-element.49.refs_3_), channel_id=1, source_target_pairs={{0,4},{2,6},{4,8},{6,10},{8,12},{10,14},{12,0},{14,2},{1,5},{3,7},... | collective-permute-start | bytes 1572872 | tf_op jit(solution)/shard_map/ppermute | solution.py:488
  3.5 14.8 %collective-permute-start.4 = (bf16[1024,256]{1,0:T(8,128)(2,1)S(1)}, bf16[1024,256]{1,0:T(8,128)(2,1)S(1)}, u32[]{:S(2)}, u32[]{:S(2)}) collective-permute-start(bf16[1024,256]{1,0:T(8,128)(2,1)S(1)} %get-tuple-element.48.refs_7_), channel_id=1, source_target_pairs={{0,12},{2,14},{4,0},{6,2},{8,4},{10,6},{12,8},{14,10},{1,13},{3,15... | collective-permute-start | bytes 1572872 | tf_op jit(solution)/shard_map/ppermute | solution.py:488
  5.2 26.0 %collective-permute-start.2 = (bf16[2,1024,256]{2,1,0:T(8,128)(2,1)}, bf16[2,1024,256]{2,1,0:T(8,128)(2,1)S(1)}, u32[]{:S(2)}, u32[]{:S(2)}) collective-permute-start(bf16[2,1024,256]{2,1,0:T(8,128)(2,1)} %bitcast.21), channel_id=1, source_target_pairs={{0,2},{2,0},{4,6},{6,4},{8,10},{10,8},{12,14},{14,12},{1,3},{3,1},... | collective-permute-start | bytes 3145736 | tf_op jit(solution)/shard_map/ppermute | solution.py:488
  5.2 22.9 %collective-permute-start = (bf16[1024,256]{1,0:T(8,128)(2,1)S(1)}, bf16[1024,256]{1,0:T(8,128)(2,1)S(1)}, u32[]{:S(2)}, u32[]{:S(2)}) collective-permute-start(bf16[1024,256]{1,0:T(8,128)(2,1)S(1)} %get-tuple-element.49.refs_3_), channel_id=1, source_target_pairs={{0,12},{2,14},{4,0},{6,2},{8,4},{10,6},{12,8},{14,10},{1,13},{3,15... | collective-permute-start | bytes 1572872 | tf_op jit(solution)/shard_map/ppermute | solution.py:488
  6.8 24.3 %collective-permute-start.1 = (bf16[1024,256]{1,0:T(8,128)(2,1)S(1)}, bf16[1024,256]{1,0:T(8,128)(2,1)S(1)}, u32[]{:S(2)}, u32[]{:S(2)}) collective-permute-start(bf16[1024,256]{1,0:T(8,128)(2,1)S(1)} %get-tuple-element.48.refs_7_), channel_id=1, source_target_pairs={{0,4},{2,6},{4,8},{6,10},{8,12},{10,14},{12,0},{14,2},{1,5},{3,7},... | collective-permute-start | bytes 1572872 | tf_op jit(solution)/shard_map/ppermute | solution.py:488
  7.8 46.2 %copy-start.7 = (s32[32]{0:T(128)}, s32[32]{0:T(128)S(1)}, u32[]{:S(2)}) copy-start(s32[32]{0:T(128)S(1)} %shard_map.95.at_ref.refs_0_) | copy-start | bytes 388
  18.3 12.7 %collective-permute-start.5 = (bf16[1024,256]{1,0:T(8,128)(2,1)S(1)}, bf16[1024,256]{1,0:T(8,128)(2,1)S(1)}, u32[]{:S(2)}, u32[]{:S(2)}) collective-permute-start(bf16[1024,256]{1,0:T(8,128)(2,1)S(1)} %get-tuple-element.27.refs_4_), channel_id=1, source_target_pairs={{0,2},{2,0},{4,6},{6,4},{8,10},{10,8},{12,14},{14,12},{1,3},{3,1},... | collective-permute-start | bytes 1572872 | tf_op jit(solution)/shard_map/ppermute | solution.py:488
  18.3 12.8 %collective-permute-start.6 = (bf16[1024,256]{1,0:T(8,128)(2,1)S(1)}, bf16[1024,256]{1,0:T(8,128)(2,1)S(1)}, u32[]{:S(2)}, u32[]{:S(2)}) collective-permute-start(bf16[1024,256]{1,0:T(8,128)(2,1)S(1)} %get-tuple-element.28.refs_8_), channel_id=1, source_target_pairs={{0,2},{2,0},{4,6},{6,4},{8,10},{10,8},{12,14},{14,12},{1,3},{3,1},... | collective-permute-start | bytes 1572872 | tf_op jit(solution)/shard_map/ppermute | solution.py:488
  28.1 12.9 %collective-permute-start.11 = (bf16[1024,256]{1,0:T(8,128)(2,1)S(1)}, bf16[1024,256]{1,0:T(8,128)(2,1)S(1)}, u32[]{:S(2)}, u32[]{:S(2)}) collective-permute-start(bf16[1024,256]{1,0:T(8,128)(2,1)S(1)} %get-tuple-element.28.refs_8_), channel_id=1, source_target_pairs={{0,12},{2,14},{4,0},{6,2},{8,4},{10,6},{12,8},{14,10},{1,13},{3,15... | collective-permute-start | bytes 1572872 | tf_op jit(solution)/shard_map/ppermute | solution.py:488
  31.1 13.4 %collective-permute-start.8 = (bf16[1024,256]{1,0:T(8,128)(2,1)S(1)}, bf16[1024,256]{1,0:T(8,128)(2,1)S(1)}, u32[]{:S(2)}, u32[]{:S(2)}) collective-permute-start(bf16[1024,256]{1,0:T(8,128)(2,1)S(1)} %get-tuple-element.27.refs_4_), channel_id=1, source_target_pairs={{0,4},{2,6},{4,8},{6,10},{8,12},{10,14},{12,0},{14,2},{1,5},{3,7},... | collective-permute-start | bytes 1572872 | tf_op jit(solution)/shard_map/ppermute | solution.py:488
  31.1 23.0 %collective-permute-start.14 = (bf16[128,4096]{1,0:T(8,128)(2,1)S(1)}, bf16[128,4096]{1,0:T(8,128)(2,1)S(1)}, u32[]{:S(2)}, u32[]{:S(2)}) collective-permute-start(bf16[128,4096]{1,0:T(8,128)(2,1)S(1)} %get-tuple-element.39), channel_id=1, source_target_pairs={{0,2},{2,0},{4,6},{6,4},{8,10},{10,8},{12,14},{14,12},{1,3},{3,1},... | collective-permute-start | bytes 3145736 | tf_op jit(solution)/shard_map/ppermute | solution.py:488
  31.2 15.2 %copy-start.3 = (bf16[1,128,2048]{2,1,0:T(8,128)(2,1)S(1)}, bf16[1,128,2048]{2,1,0:T(8,128)(2,1)}, u32[]{:S(2)}) copy-start(bf16[1,128,2048]{2,1,0:T(8,128)(2,1)} %param.11) | copy-start | bytes 1572868
  31.2 15.2 %copy-start.4 = (bf16[1,128,2048]{2,1,0:T(8,128)(2,1)S(1)}, bf16[1,128,2048]{2,1,0:T(8,128)(2,1)}, u32[]{:S(2)}) copy-start(bf16[1,128,2048]{2,1,0:T(8,128)(2,1)} %param.12) | copy-start | bytes 1572868
  31.2 15.2 %copy-start.9 = (s32[128]{0:T(128)S(1)}, s32[128]{0:T(128)}, u32[]{:S(2)}) copy-start(s32[128]{0:T(128)} %param.14) | copy-start | bytes 1540
  33.9 10.5 %collective-permute-start.10 = (bf16[1024,256]{1,0:T(8,128)(2,1)S(1)}, bf16[1024,256]{1,0:T(8,128)(2,1)S(1)}, u32[]{:S(2)}, u32[]{:S(2)}) collective-permute-start(bf16[1024,256]{1,0:T(8,128)(2,1)S(1)} %get-tuple-element.31), channel_id=1, source_target_pairs={{0,2},{2,0},{4,6},{6,4},{8,10},{10,8},{12,14},{14,12},{1,3},{3,1},... | collective-permute-start | bytes 1572872 | tf_op jit(solution)/shard_map/ppermute | solution.py:488
  34.5 10.0 %collective-permute-start.7 = (bf16[1024,256]{1,0:T(8,128)(2,1)S(1)}, bf16[1024,256]{1,0:T(8,128)(2,1)S(1)}, u32[]{:S(2)}, u32[]{:S(2)}) collective-permute-start(bf16[1024,256]{1,0:T(8,128)(2,1)S(1)} %get-tuple-element.30), channel_id=1, source_target_pairs={{0,2},{2,0},{4,6},{6,4},{8,10},{10,8},{12,14},{14,12},{1,3},{3,1},... | collective-permute-start | bytes 1572872 | tf_op jit(solution)/shard_map/ppermute | solution.py:488
  41.0 3.4 %collective-permute-start.12 = (bf16[1024,256]{1,0:T(8,128)(2,1)S(1)}, bf16[1024,256]{1,0:T(8,128)(2,1)S(1)}, u32[]{:S(2)}, u32[]{:S(2)}) collective-permute-start(bf16[1024,256]{1,0:T(8,128)(2,1)S(1)} %collective-permute-done.11.refs_6_), channel_id=1, source_target_pairs={{0,2},{2,0},{4,6},{6,4},{8,10},{10,8},{12,14},{14,12},{1,3},{3,1},... | collective-permute-start | bytes 1572872 | tf_op jit(solution)/shard_map/ppermute | solution.py:488
  44.5 1.9 %collective-permute-start.9 = (bf16[1024,256]{1,0:T(8,128)(2,1)S(1)}, bf16[1024,256]{1,0:T(8,128)(2,1)S(1)}, u32[]{:S(2)}, u32[]{:S(2)}) collective-permute-start(bf16[1024,256]{1,0:T(8,128)(2,1)S(1)} %collective-permute-done.8.refs_3_), channel_id=1, source_target_pairs={{0,2},{2,0},{4,6},{6,4},{8,10},{10,8},{12,14},{14,12},{1,3},{3,1},... | collective-permute-start | bytes 1572872 | tf_op jit(solution)/shard_map/ppermute | solution.py:488
  46.4 3.2 %copy-start.1 = (bf16[1,128,8192]{2,1,0:T(8,128)(2,1)S(1)}, bf16[1,128,8192]{2,1,0:T(8,128)(2,1)}, u32[]{:S(2)}) copy-start(bf16[1,128,8192]{2,1,0:T(8,128)(2,1)} %param.8) | copy-start | bytes 6291460
  46.4 3.2 %copy-start.6 = (bf16[1,8192]{1,0:T(2,128)(2,1)S(1)}, bf16[1,8192]{1,0:T(2,128)(2,1)}, u32[]{:S(2)}) copy-start(bf16[1,8192]{1,0:T(2,128)(2,1)} %refs_5_.3) | copy-start | bytes 49156
  51.6 26.8 %collective-permute-start.13 = (bf16[128,4096]{1,0:T(8,128)(2,1)S(1)}, bf16[128,4096]{1,0:T(8,128)(2,1)S(1)}, u32[]{:S(2)}, u32[]{:S(2)}) collective-permute-start(bf16[128,4096]{1,0:T(8,128)(2,1)S(1)} %shard_map.102), channel_id=1, source_target_pairs={{0,1},{1,0},{2,3},{3,2},{4,5},{5,4},{6,7},{7,6},{8,9},{9,8},{10,11... | collective-permute-start | bytes 3145736 | tf_op jit(solution)/shard_map/ppermute | solution.py:526
  51.7 2.3 %collective-permute-start.15 = (bf16[128,512]{1,0:T(8,128)(2,1)S(1)}, bf16[128,512]{1,0:T(8,128)(2,1)S(1)}, u32[]{:S(2)}, u32[]{:S(2)}) collective-permute-start(bf16[128,512]{1,0:T(8,128)(2,1)S(1)} %get-tuple-element.35.refs_1_.grads_ref), channel_id=1, source_target_pairs={{0,2},{2,0},{4,6},{6,4},{8,10},{10,8},{12,14},{14,12},{1,3},{3,1},... | collective-permute-start | bytes 393224 | tf_op jit(solution)/shard_map/ppermute | solution.py:488
  56.9 15.4 %collective-permute-start.16 = (bf16[512,512]{1,0:T(8,128)(2,1)S(1)}, bf16[512,512]{1,0:T(8,128)(2,1)S(1)}, u32[]{:S(2)}, u32[]{:S(2)}) collective-permute-start(bf16[512,512]{1,0:T(8,128)(2,1)S(1)} %get-tuple-element.42), channel_id=1, source_target_pairs={{0,4},{2,6},{4,8},{6,10},{8,12},{10,14},{12,0},{14,2},{1,5},{3,7},... | collective-permute-start | bytes 1572872 | tf_op jit(solution)/shard_map/ppermute | solution.py:488
  56.9 15.4 %collective-permute-start.17 = (bf16[512,512]{1,0:T(8,128)(2,1)S(1)}, bf16[512,512]{1,0:T(8,128)(2,1)S(1)}, u32[]{:S(2)}, u32[]{:S(2)}) collective-permute-start(bf16[512,512]{1,0:T(8,128)(2,1)S(1)} %get-tuple-element.43), channel_id=1, source_target_pairs={{0,12},{2,14},{4,0},{6,2},{8,4},{10,6},{12,8},{14,10},{1,13},{3,15... | collective-permute-start | bytes 1572872 | tf_op jit(solution)/shard_map/ppermute | solution.py:488
  72.6 6.9 %copy-start.10 = (bf16[1024,512]{1,0:T(8,128)(2,1)}, bf16[1024,512]{1,0:T(8,128)(2,1)S(1)}, u32[]{:S(2)}) copy-start(bf16[1024,512]{1,0:T(8,128)(2,1)S(1)} %get-tuple-element.46) | copy-start | bytes 3145732
  78.4 13.7 %copy-start.2 = (bf16[128,4096]{1,0:T(8,128)(2,1)S(1)}, bf16[128,4096]{1,0:T(8,128)(2,1)}, u32[]{:S(2)}) copy-start(bf16[128,4096]{1,0:T(8,128)(2,1)} %in_ref.1) | copy-start | bytes 3145732
  78.4 13.7 %copy-start.8 = (s32[32]{0:T(128)S(1)}, s32[32]{0:T(128)}, u32[]{:S(2)}) copy-start(s32[32]{0:T(128)} %copy-done.7) | copy-start | bytes 388
  78.4 14.3 %copy-start.13 = (s32[1,2,8,2]{2,3,1,0:T(2,128)S(1)}, s32[1,2,8,2]{2,3,1,0:T(2,128)}, u32[]{:S(2)}) copy-start(s32[1,2,8,2]{2,3,1,0:T(2,128)} %param.15) | copy-start | bytes 388
  79.5 35.0 %all-to-all-start = ((bf16[16,8,4096]{2,1,0:T(8,128)(2,1)}), bf16[16,8,4096]{2,1,0:T(8,128)(2,1)S(1)}, u32[]{:S(2)}, u32[]{:S(2)}) async-start(bf16[16,8,4096]{2,1,0:T(8,128)(2,1)} %bitcast.7), calls=%async_computation | async-start | bytes 2097152 | tf_op jit(solution)/shard_map/all_to_all | solution.py:536
  88.8 32.1 %collective-permute-start.18 = (bf16[1024,512]{1,0:T(8,128)(2,1)}, bf16[1024,512]{1,0:T(8,128)(2,1)}, u32[]{:S(2)}, u32[]{:S(2)}) collective-permute-start(bf16[1024,512]{1,0:T(8,128)(2,1)} %copy-done.10), channel_id=1, source_target_pairs={{0,4},{2,6},{4,8},{6,10},{8,12},{10,14},{12,0},{14,2},{1,5},{3,7},... | collective-permute-start | bytes 3145736 | tf_op jit(solution)/shard_map/ppermute | solution.py:488
  88.9 32.0 %collective-permute-start.19 = (bf16[1024,512]{1,0:T(8,128)(2,1)S(1)}, bf16[1024,512]{1,0:T(8,128)(2,1)}, u32[]{:S(2)}, u32[]{:S(2)}) collective-permute-start(bf16[1024,512]{1,0:T(8,128)(2,1)S(1)} %get-tuple-element.47), channel_id=1, source_target_pairs={{0,12},{2,14},{4,0},{6,2},{8,4},{10,6},{12,8},{14,10},{1,13},{3,15... | collective-permute-start | bytes 3145736 | tf_op jit(solution)/shard_map/ppermute | solution.py:488
  115.6 32.6 %all-to-all-start.1 = ((bf16[16,8,4096]{2,1,0:T(8,128)(2,1)}), bf16[16,8,4096]{2,1,0:T(8,128)(2,1)}, u32[]{:S(2)}, u32[]{:S(2)}) async-start(bf16[16,8,4096]{2,1,0:T(8,128)(2,1)} %shard_map.107), calls=%async_computation.1 | async-start | bytes 2097152 | tf_op jit(solution)/shard_map/all_to_all | solution.py:541
  (4 other events, 4.6 us)

commit v6 on v5

--- a/solution.py
+++ b/solution.py
@@ -61,10 +61,10 @@
     tensor_pos = lax.axis_index("tensor")
     before, after, across = lax.rem(me + 6, 8), lax.rem(me + 2, 8), lax.rem(me + 4, 8)
     sibling = lambda shard: shard + 1 - 2 * lax.rem(shard, 2)
-    order = (me, sibling(me), before, sibling(before), after)
-    order += (me, sibling(me), after, sibling(after), before)
-    order += (sibling(after), across, sibling(across))
-    order += (sibling(before), across, sibling(across))
+    order = (sibling(me), me, before, after)
+    order += (sibling(me), me, after, before)
+    order += (sibling(before), sibling(after), across, sibling(across))
+    order += (sibling(after), sibling(before), across, sibling(across))
     for i, shard in enumerate(order):
         out_ref[i] = shard
     out_ref[CORE] = lax.rem(me, 2)
@@ -124,10 +124,9 @@
     )(places, x, gain)
 
 
-def early_kernel(shards_ref, normed_ref, both_ref, *refs, count):
-    key_pieces, value_pieces = list(refs[: count - 1]), list(refs[count - 1 : 2 * count - 2])
-    key_pieces.insert(1, both_ref.at[0])
-    value_pieces.insert(1, both_ref.at[1])
+def early_kernel(shards_ref, normed_ref, pair_ref, *refs, count):
+    key_pieces = [pair_ref.at[0], *refs[: count - 1]]
+    value_pieces = [pair_ref.at[1], *refs[count - 1 : 2 * count - 2]]
     key_ref, value_ref, key_w_ref, value_w_ref, key_sems, value_sems = refs[2 * count - 2 :]
     key_f, copies = add_rows(shards_ref, normed_ref, key_pieces, key_w_ref, key_sems, 0, None)
     value_f, more = add_rows(
@@ -139,7 +138,7 @@
         copy.wait()
 
 
-def early_rows(shards, normed, both, key_pieces, value_pieces):
+def early_rows(shards, normed, pair, key_pieces, value_pieces):
     tokens, features = normed.shape
     depth, width = key_pieces[0].shape
     count = len(key_pieces) + 1
@@ -153,11 +152,14 @@
         scratch_shapes=[pltpu.SemaphoreType.DMA((count,))] * 2,
         compiler_params=pltpu.CompilerParams(vmem_limit_bytes=16 * MIB),
         cost_estimate=cost(1, 1),
-    )(shards, normed, both, *key_pieces, *value_pieces)
-
-
-def attention_kernel(shards_ref, normed_ref, *refs, count, first, features):
-    key_pieces, value_pieces = refs[:count], refs[count : 2 * count]
+    )(shards, normed, pair, *key_pieces, *value_pieces)
+
+
+def attention_kernel(
+    shards_ref, normed_ref, first_pair_ref, second_pair_ref, *refs, count, first, features
+):
+    key_pieces = [first_pair_ref.at[0], second_pair_ref.at[0], *refs[:count]]
+    value_pieces = [first_pair_ref.at[1], second_pair_ref.at[1], *refs[count : 2 * count]]
     key_part_ref, value_part_ref, _, _, query_ref, grad_ref, seg_ref = refs[
         2 * count : 2 * count + 7
     ]
@@ -168,7 +170,7 @@
         shards_ref, normed_ref, key_pieces, key_w_ref, key_sems, first, key_part_ref[...]
     )
     value_f, more = add_rows(
-        shards_ref, normed_ref, value_pieces, value_w_ref, value_sems, first + count, value_part_ref[...]
+        shards_ref, normed_ref, value_pieces, value_w_ref, value_sems, first + count + 2, value_part_ref[...]
     )
     tokens = query_ref.shape[0]
     width = key_f.shape[1]
@@ -205,44 +207,43 @@
         copy.wait()
 
 
-def attention_grads(shards, first, normed, key_pieces, value_pieces, early, query, grad_out, segments):
+def attention_grads(shards, first, normed, pairs, key_pieces, value_pieces, early, query, grad_out, segments):
     tokens, features = normed.shape
     depth, width = key_pieces[0].shape
     count = len(key_pieces)
     whole = jax.ShapeDtypeStruct((features, width), jnp.bfloat16)
     grads = jax.ShapeDtypeStruct((tokens, 2 * width), jnp.bfloat16)
-    at = 2 * count + 4
+    at = 2 * count + 6
     return pl.pallas_call(
         lambda *refs: attention_kernel(*refs, count=count, first=first, features=features),
-        in_specs=[IN_SMEM] + in_vmem(2 * count + 3) + [ANYWHERE] * 2 + in_vmem(3),
+        in_specs=[IN_SMEM] + in_vmem(2 * count + 5) + [ANYWHERE] * 2 + in_vmem(3),
         out_specs=[ANYWHERE] * 2 + in_vmem(2),
         out_shape=(whole, whole, grads, jax.ShapeDtypeStruct((tokens, 1), jnp.float32)),
         input_output_aliases={at: 0, at + 1: 1},
-        scratch_shapes=[pltpu.SemaphoreType.DMA((count,))] * 2,
+        scratch_shapes=[pltpu.SemaphoreType.DMA((count + 2,))] * 2,
         compiler_params=pltpu.CompilerParams(vmem_limit_bytes=20 * MIB),
         cost_estimate=cost(
             4 * tokens * depth * width * count + 8 * tokens * query.size,
             8 * depth * width * count + 4 * query.size,
             tokens * query.size // HD,
         ),
-    )(shards, normed, *key_pieces, *value_pieces, *early, query, grad_out, segments)
-
-
-def ordered_kernel(*refs):
-    del refs
-
-
-def ordered(arrays, after):
-    count = len(arrays)
-    return pl.pallas_call(
-        ordered_kernel,
-        in_specs=[ANYWHERE] * (count + 1),
-        out_specs=[ANYWHERE] * count,
-        out_shape=[jax.ShapeDtypeStruct(a.shape, a.dtype) for a in arrays],
-        input_output_aliases={i: i for i in range(count)},
-        compiler_params=pltpu.CompilerParams(vmem_limit_bytes=MIB),
+    )(shards, normed, *pairs, *key_pieces, *value_pieces, *early, query, grad_out, segments)
+
+
+def pair_kernel(first_ref, second_ref, *rest):
+    rest[-1][0] = first_ref[...]
+    rest[-1][1] = second_ref[...]
+
+
+def paired(first, second, *after):
+    return pl.pallas_call(
+        pair_kernel,
+        in_specs=in_vmem(2) + [ANYWHERE] * len(after),
+        out_specs=pl.BlockSpec(memory_space=pltpu.VMEM),
+        out_shape=jax.ShapeDtypeStruct((2, *first.shape), first.dtype),
+        compiler_params=pltpu.CompilerParams(vmem_limit_bytes=4 * MIB),
         cost_estimate=cost(1, 1),
-    )(*arrays, after)
+    )(first, second, *after)
 
 
 def branch_kernel(
@@ -487,31 +488,31 @@
     right, left, other = ring_pairs(lax.axis_size("dp"))
     send = lambda piece, pairs: lax.ppermute(piece, "dp", pairs)
     key_own, value_own = kv_weight[0, 0], kv_weight[0, 1]
-    both = send(kv_weight[0], other)
+    own_pair = send(kv_weight[0], other)
     key_l = send(key_own, right)
     value_r = send(value_own, left)
     key_r = send(key_own, left)
     value_l = send(value_own, right)
     places = all_places()
     normed, inv_rms, normed_other = norm(places, inputs, norm_gain)
-    key_l, value_r = ordered((key_l, value_r), inv_rms)
+    first_pair = send(paired(key_l, value_r, own_pair), other)
     key_2 = send(key_l, right)
     value_2 = send(value_r, left)
-    normed_sib = send(normed_other, other)
     early = early_rows(
         places,
         normed,
-        both,
-        [key_own, key_l, send(key_l, other), key_r],
-        [value_own, value_r, send(value_r, other), value_l],
-    )
-    key_r, value_l = ordered((key_r, value_l), early[0])
+        own_pair,
+        [key_own, key_l, key_r],
+        [value_own, value_r, value_l],
+    )
+    normed_sib = send(normed_other, other)
     key_w, value_w, grads, inner = attention_grads(
         places,
-        10,
+        8,
         normed,
-        [send(key_r, other), key_2, send(key_2, other)],
-        [send(value_l, other), value_2, send(value_2, other)],
+        [first_pair, send(paired(key_r, value_l, early[0]), other)],
+        [key_2, send(key_2, other)],
+        [value_2, send(value_2, other)],
         early,
         queries[0],
         out_grad[0],

time: 151 us -> 149 us (0.987)
  waiting for transfers between devices: 90.2 us -> 87.4 us
    ppermute x19 -> x17, waiting for transfers between devices: 39.2 us -> 36.7 us  [on_device(): send = lambda piece, pairs: lax.ppermute(piece, 'dp', pairs)]
    ppermute x19 -> x17, starting transfers between devices: 16.3 us -> 17.2 us  [on_device(): send = lambda piece, pairs: lax.ppermute(piece, 'dp', pairs)]
    unnamed x28 -> x26, local copies, waits for them, and re-layouts: 4.61 us -> 4.58 us
  transfers between devices with their start and end apart: 22 -> 20, of which waited for: 10 -> 10; matrix products, arithmetic and copies ran while one was open for 0% -> 1% of each run, Pallas kernels for 13% -> 13%
where the time goes in v6:
time: 149 us
  waiting for transfers between devices  87.4 us (59%)
  starting transfers between devices  32.2 us (22%)
  Pallas kernels  22.1 us (15%)
  local copies, waits for them, and re-layouts  5.93 us (4%)
    ppermute x17, waiting for transfers between devices, on_device(): send = lambda piece, pairs: lax.ppermute(piece, 'dp', pairs)  36.7 us
    all_to_all x1, waiting for transfers between devices, on_device(): lax.all_to_all(sums.reshape(token_count, branch.shape[1]), 'pipe', 0, 0,...  23.5 us
    all_to_all x1, waiting for transfers between devices, on_device(): parts = lax.all_to_all(branch, 'pipe', 0, 0, tiled=True)  21.7 us
    ppermute x17, starting transfers between devices, on_device(): send = lambda piece, pairs: lax.ppermute(piece, 'dp', pairs)  17.2 us
    all_to_all x1, starting transfers between devices, on_device(): parts = lax.all_to_all(branch, 'pipe', 0, 0, tiled=True)  9.29 us
    ppermute x1, waiting for transfers between devices, on_device(): lax.ppermute(share(THEIRS, jnp.bfloat16), 'tensor', [(0, 1), (1, 0)])  5.59 us
    all_to_all x1, starting transfers between devices, on_device(): lax.all_to_all(sums.reshape(token_count, branch.shape[1]), 'pipe', 0, 0,...  5.3 us
    unnamed x26, local copies, waits for them, and re-layouts  4.58 us
  transfers between devices with their start and end apart: 20, of which 10 were waited for; matrix products, arithmetic and copies ran while one was open for 1% of the time, Pallas kernels for 13%

profile of v6, /device:TPU:16, one launch (start us, length us, event | category | flops | bytes accessed | tf_op | source)
XLA Modules:
  0.0 148.8 jit_solution(5163496670229698459)
XLA Ops:
  0.7 1.3 slice_bitcast_fusion
  2.0 2.8 %collective-permute-start.1 = (bf16[1024,256]{1,0:T(8,128)(2,1)S(1)}, bf16[1024,256]{1,0:T(8,128)(2,1)S(1)}, u32[]{:S(2)}, u32[]{:S(2)}) collective-permute-start(bf16[1024,256]{1,0:T(8,128)(2,1)S(1)} %get-tuple-element.40.refs_6_), channel_id=1, source_target_pairs={{0,12},{2,14},{4,0},{6,2},{8,4},{10,6},{12,8},{14,10},{1,13},{3,15... | collective-permute-start | bytes 1572872 | tf_op jit(solution)/shard_map/ppermute | solution.py:489
  4.8 3.2 %collective-permute-start.4 = (bf16[1024,256]{1,0:T(8,128)(2,1)S(1)}, bf16[1024,256]{1,0:T(8,128)(2,1)S(1)}, u32[]{:S(2)}, u32[]{:S(2)}) collective-permute-start(bf16[1024,256]{1,0:T(8,128)(2,1)S(1)} %get-tuple-element.41.refs_3_), channel_id=1, source_target_pairs={{0,12},{2,14},{4,0},{6,2},{8,4},{10,6},{12,8},{14,10},{1,13},{3,15... | collective-permute-start | bytes 1572872 | tf_op jit(solution)/shard_map/ppermute | solution.py:489
  8.7 1.6 %copy-done = bf16[1,128,8192]{2,1,0:T(8,128)(2,1)S(1)} copy-done((bf16[1,128,8192]{2,1,0:T(8,128)(2,1)S(1)}, bf16[1,128,8192]{2,1,0:T(8,128)(2,1)}, u32[]{:S(2)}) %copy-start) | copy-done | bytes 2097176
  10.3 0.8 copy-done.5
  11.0 2.1 %shard_map.96 = (bf16[128,8192]{1,0:T(8,128)(2,1)S(1)}, f32[128,1]{1,0:T(8,128)S(1)}, bf16[128,4096]{1,0:T(8,128)(2,1)S(1)}) custom-call(s32[32]{0:T(128)S(1)} %shard_map.95.at_ref.refs_0_, bf16[128,8192]{1,0:T(8,128)(2,1)S(1)} %bitcast.15, bf16[1,8192]{1,0:T(2,128)(2,1)S(1)} %copy-done.5), custom_call_target="tpu_custom_call" | custom-call | flops 1 | bytes 1 | tf_op jit(solution)/shard_map/pallas_call | solution.py:102
  13.2 3.9 %collective-permute-done.1.second_ref.refs_7_ = bf16[1024,256]{1,0:T(8,128)(2,1)S(1)} collective-permute-done((bf16[1024,256]{1,0:T(8,128)(2,1)S(1)}, bf16[1024,256]{1,0:T(8,128)(2,1)S(1)}, u32[]{:S(2)}, u32[]{:S(2)}) %collective-permute-start.1) | collective-permute-done | bytes 524320 | tf_op jit(solution)/shard_map/ppermute | solution.py:489
  17.1 3.7 %collective-permute-start.9 = (bf16[1024,256]{1,0:T(8,128)(2,1)S(1)}, bf16[1024,256]{1,0:T(8,128)(2,1)S(1)}, u32[]{:S(2)}, u32[]{:S(2)}) collective-permute-start(bf16[1024,256]{1,0:T(8,128)(2,1)S(1)} %collective-permute-done.1.second_ref.refs_7_), channel_id=1, source_target_pairs={{0,12},{2,14},{4,0},{6,2},{8,4},{10,6},{12,8},{14,10},{1,13},{3,15... | collective-permute-start | bytes 1572872 | tf_op jit(solution)/shard_map/ppermute | solution.py:489
  20.8 7.5 %collective-permute-done.4.refs_5_.first_ref = bf16[1024,256]{1,0:T(8,128)(2,1)S(1)} collective-permute-done((bf16[1024,256]{1,0:T(8,128)(2,1)S(1)}, bf16[1024,256]{1,0:T(8,128)(2,1)S(1)}, u32[]{:S(2)}, u32[]{:S(2)}) %collective-permute-start.4) | collective-permute-done | bytes 524320 | tf_op jit(solution)/shard_map/ppermute | solution.py:489
  28.3 3.7 %collective-permute-done.5.refs_8_.second_ref = bf16[1024,256]{1,0:T(8,128)(2,1)S(1)} collective-permute-done((bf16[1024,256]{1,0:T(8,128)(2,1)S(1)}, bf16[1024,256]{1,0:T(8,128)(2,1)S(1)}, u32[]{:S(2)}, u32[]{:S(2)}) %collective-permute-start.5) | collective-permute-done | bytes 524320 | tf_op jit(solution)/shard_map/ppermute | solution.py:489
  32.0 2.3 %shard_map.98 = (f32[128,256]{1,0:T(8,128)S(1)}, f32[128,256]{1,0:T(8,128)S(1)}, bf16[8192,256]{1,0:T(8,128)(2,1)S(1)}, bf16[8192,256]{1,0:T(8,128)(2,1)S(1)}) custom-call(s32[32]{0:T(128)S(1)} %shard_map.95.at_ref.refs_0_, bf16[128,8192]{1,0:T(8,128)(2,1)S(1)} %get-tuple-element.21.refs_1_.normed_ref, ...), custom_call_target="tpu_custom_call" | custom-call | flops 1 | bytes 1 | tf_op jit(solution)/shard_map/pallas_call | solution.py:147
  35.3 3.8 %collective-permute-done.9.refs_6_ = bf16[1024,256]{1,0:T(8,128)(2,1)S(1)} collective-permute-done((bf16[1024,256]{1,0:T(8,128)(2,1)S(1)}, bf16[1024,256]{1,0:T(8,128)(2,1)S(1)}, u32[]{:S(2)}, u32[]{:S(2)}) %collective-permute-start.9) | collective-permute-done | bytes 524320 | tf_op jit(solution)/shard_map/ppermute | solution.py:489
  39.2 3.4 %collective-permute-done.7.refs_4_ = bf16[1024,256]{1,0:T(8,128)(2,1)S(1)} collective-permute-done((bf16[1024,256]{1,0:T(8,128)(2,1)S(1)}, bf16[1024,256]{1,0:T(8,128)(2,1)S(1)}, u32[]{:S(2)}, u32[]{:S(2)}) %collective-permute-start.7) | collective-permute-done | bytes 524320 | tf_op jit(solution)/shard_map/ppermute | solution.py:489
  42.6 1.9 %collective-permute-done.8.refs_5_ = bf16[1024,256]{1,0:T(8,128)(2,1)S(1)} collective-permute-done((bf16[1024,256]{1,0:T(8,128)(2,1)S(1)}, bf16[1024,256]{1,0:T(8,128)(2,1)S(1)}, u32[]{:S(2)}, u32[]{:S(2)}) %collective-permute-start.8) | collective-permute-done | bytes 524320 | tf_op jit(solution)/shard_map/ppermute | solution.py:489
  44.5 3.5 %shard_map.100 = (bf16[8192,256]{1,0:T(8,128)(2,1)S(1)}, bf16[8192,256]{1,0:T(8,128)(2,1)S(1)}, bf16[128,512]{1,0:T(8,128)(2,1)S(1)}, f32[128,1]{1,0:T(8,128)S(1)}) custom-call(s32[32]{0:T(128)S(1)} %shard_map.95.at_ref.refs_0_, bf16[128,8192]{1,0:T(8,128)(2,1)S(1)} %get-tuple-element.21.refs_1_.normed_ref, ...), custom_call_target="tpu_custom_call", output_to_operand_aliasing={{0}: (10, {}), {1}: (11, {})} | custom-call | flops 536870912 | bytes 5242880 | tf_op jit(solution)/shard_map/pallas_call | solution.py:217
  48.0 2.1 %shard_map.102 = bf16[128,4096]{1,0:T(8,128)(2,1)S(1)} custom-call(s32[32]{0:T(128)S(1)} %shard_map.95.at_ref.refs_0_, bf16[128,512]{1,0:T(8,128)(2,1)S(1)} %get-tuple-element.26.refs_1_.grads_ref, bf16[8192,256]{1,0:T(8,128)(2,1)S(1)} %get-tuple-element.27.refs_2_, bf16[8192,256]{1,0:T(8,128)(2,1)S(1)} %get-tuple-element.28.refs_3_, ...), custom_call_target="tpu_custom_call" | custom-call | flops 536870912 | bytes 5242880 | tf_op jit(solution)/shard_map/pallas_call | solution.py:268
  50.5 2.1 %shard_map.101.after_ref.mine_ref = f32[128,4096]{1,0:T(8,128)S(1)} custom-call(s32[32]{0:T(128)S(1)} %shard_map.95.at_ref.refs_0_, bf16[128,512]{1,0:T(8,128)(2,1)S(1)} %get-tuple-element.26.refs_1_.grads_ref, bf16[8192,256]{1,0:T(8,128)(2,1)S(1)} %get-tuple-element.27.refs_2_, bf16[8192,256]{1,0:T(8,128)(2,1)S(1)} %get-tuple-element.28.refs_3_, ...), custom_call_target="tpu_custom_call" | custom-call | flops 536870912 | bytes 5242880 | tf_op jit(solution)/shard_map/pallas_call | solution.py:268
  52.6 1.8 %shard_map.103 = (bf16[1024,512]{1,0:T(8,128)(2,1)S(1)}, bf16[1024,512]{1,0:T(8,128)(2,1)S(1)}, bf16[1024,512]{1,0:T(8,128)(2,1)S(1)}, bf16[512,512]{1,0:T(8,128)(2,1)S(1)}, bf16[512,512]{1,0:T(8,128)(2,1)S(1)}) custom-call(s32[32]{0:T(128)S(1)} %shard_map.95.at_ref.refs_0_, bf16[128,8192]{1,0:T(8,128)(2,1)S(1)} %get-tuple-element.21.refs_1_.normed_ref, ...), custom_call_target="tpu_custom_call" | custom-call | flops 2147483648 | bytes 4194304 | tf_op jit(solution)/shard_map/pallas_call | solution.py:305
  54.5 1.0 copy-done.10
  55.5 3.2 %collective-permute-start.15 = (bf16[512,512]{1,0:T(8,128)(2,1)S(1)}, bf16[512,512]{1,0:T(8,128)(2,1)S(1)}, u32[]{:S(2)}, u32[]{:S(2)}) collective-permute-start(bf16[512,512]{1,0:T(8,128)(2,1)S(1)} %get-tuple-element.35), channel_id=1, source_target_pairs={{0,12},{2,14},{4,0},{6,2},{8,4},{10,6},{12,8},{14,10},{1,13},{3,15... | collective-permute-start | bytes 1572872 | tf_op jit(solution)/shard_map/ppermute | solution.py:489
  58.7 12.3 %collective-permute-done.14.far_right_ref = bf16[512,512]{1,0:T(8,128)(2,1)S(1)} collective-permute-done((bf16[512,512]{1,0:T(8,128)(2,1)S(1)}, bf16[512,512]{1,0:T(8,128)(2,1)S(1)}, u32[]{:S(2)}, u32[]{:S(2)}) %collective-permute-start.14) | collective-permute-done | bytes 524320 | tf_op jit(solution)/shard_map/ppermute | solution.py:489
  71.3 5.6 %collective-permute-done.11.arrived_ref = bf16[128,4096]{1,0:T(8,128)(2,1)S(1)} collective-permute-done((bf16[128,4096]{1,0:T(8,128)(2,1)S(1)}, bf16[128,4096]{1,0:T(8,128)(2,1)S(1)}, u32[]{:S(2)}, u32[]{:S(2)}) %collective-permute-start.11) | collective-permute-done | bytes 1048608 | tf_op jit(solution)/shard_map/ppermute | solution.py:527
  76.9 1.0 shard_map.105
  78.0 9.3 %all-to-all-start = ((bf16[16,8,4096]{2,1,0:T(8,128)(2,1)}), bf16[16,8,4096]{2,1,0:T(8,128)(2,1)S(1)}, u32[]{:S(2)}, u32[]{:S(2)}) async-start(bf16[16,8,4096]{2,1,0:T(8,128)(2,1)} %bitcast.7), calls=%async_computation | async-start | bytes 2097152 | tf_op jit(solution)/shard_map/all_to_all | solution.py:537
  87.4 3.2 %collective-permute-start.17 = (bf16[1024,512]{1,0:T(8,128)(2,1)S(1)}, bf16[1024,512]{1,0:T(8,128)(2,1)}, u32[]{:S(2)}, u32[]{:S(2)}) collective-permute-start(bf16[1024,512]{1,0:T(8,128)(2,1)S(1)} %get-tuple-element.39), channel_id=1, source_target_pairs={{0,12},{2,14},{4,0},{6,2},{8,4},{10,6},{12,8},{14,10},{1,13},{3,15... | collective-permute-start | bytes 3145736 | tf_op jit(solution)/shard_map/ppermute | solution.py:489
  91.3 21.7 %all-to-all-done.parts_ref = bf16[16,8,4096]{2,1,0:T(8,128)(2,1)S(1)} async-done(((bf16[16,8,4096]{2,1,0:T(8,128)(2,1)}), bf16[16,8,4096]{2,1,0:T(8,128)(2,1)S(1)}, u32[]{:S(2)}, u32[]{:S(2)}) %all-to-all-start) | async-done | bytes 1048608 | tf_op jit(solution)/shard_map/all_to_all | solution.py:537
  113.0 1.0 shard_map.107
  114.0 5.3 %all-to-all-start.1 = ((bf16[16,8,4096]{2,1,0:T(8,128)(2,1)}), bf16[16,8,4096]{2,1,0:T(8,128)(2,1)}, u32[]{:S(2)}, u32[]{:S(2)}) async-start(bf16[16,8,4096]{2,1,0:T(8,128)(2,1)} %shard_map.107), calls=%async_computation.1 | async-start | bytes 2097152 | tf_op jit(solution)/shard_map/all_to_all | solution.py:542
  119.4 1.2 copy-done.11
  120.6 2.6 %shard_map.109 = bf16[2,1024,256]{2,1,0:T(8,128)(2,1)} custom-call(f32[2,8,2]{2,1,0:T(8,128)S(1)} %copy.12.factor_ref, bf16[1024,512]{1,0:T(8,128)(2,1)S(1)} %copy-done.11, bf16[1024,512]{1,0:T(8,128)(2,1)} %collective-permute-done.16.refs_1_, bf16[1024,512]{1,0:T(8,128)(2,1)} %collective-permute-done.17.refs_2_), custom_call_target="tpu_custom_call" | custom-call | flops 999999986991104 | bytes 999999995904 | tf_op jit(solution)/shard_map/pallas_call | solution.py:464
  123.2 23.5 %all-to-all-done.1 = bf16[16,8,4096]{2,1,0:T(8,128)(2,1)} async-done(((bf16[16,8,4096]{2,1,0:T(8,128)(2,1)}), bf16[16,8,4096]{2,1,0:T(8,128)(2,1)}, u32[]{:S(2)}, u32[]{:S(2)}) %all-to-all-start.1) | async-done | bytes 1048608 | tf_op jit(solution)/shard_map/all_to_all | solution.py:542
  146.7 2.0 %shard_map.108 = bf16[128,4096]{1,0:T(8,128)(2,1)} custom-call(bf16[128,4096]{1,0:T(8,128)(2,1)} %bitcast.8.in_ref), custom_call_target="tpu_custom_call" | custom-call | flops 1 | bytes 1 | tf_op jit(solution)/shard_map/pallas_call | solution.py:434
  (52 shorter events, 3.2 us)
Async XLA Ops:
  0.6 31.4 %collective-permute-start.2 = (bf16[2,1024,256]{2,1,0:T(8,128)(2,1)}, bf16[2,1024,256]{2,1,0:T(8,128)(2,1)S(1)}, u32[]{:S(2)}, u32[]{:S(2)}) collective-permute-start(bf16[2,1024,256]{2,1,0:T(8,128)(2,1)} %bitcast.21), channel_id=1, source_target_pairs={{0,2},{2,0},{4,6},{6,4},{8,10},{10,8},{12,14},{14,12},{1,3},{3,1},... | collective-permute-start | bytes 3145736 | tf_op jit(solution)/shard_map/ppermute | solution.py:489
  2.0 15.1 %collective-permute-start.1 = (bf16[1024,256]{1,0:T(8,128)(2,1)S(1)}, bf16[1024,256]{1,0:T(8,128)(2,1)S(1)}, u32[]{:S(2)}, u32[]{:S(2)}) collective-permute-start(bf16[1024,256]{1,0:T(8,128)(2,1)S(1)} %get-tuple-element.40.refs_6_), channel_id=1, source_target_pairs={{0,12},{2,14},{4,0},{6,2},{8,4},{10,6},{12,8},{14,10},{1,13},{3,15... | collective-permute-start | bytes 1572872 | tf_op jit(solution)/shard_map/ppermute | solution.py:489
  4.8 16.0 %collective-permute-start = (bf16[1024,256]{1,0:T(8,128)(2,1)S(1)}, bf16[1024,256]{1,0:T(8,128)(2,1)S(1)}, u32[]{:S(2)}, u32[]{:S(2)}) collective-permute-start(bf16[1024,256]{1,0:T(8,128)(2,1)S(1)} %get-tuple-element.41.refs_3_), channel_id=1, source_target_pairs={{0,4},{2,6},{4,8},{6,10},{8,12},{10,14},{12,0},{14,2},{1,5},{3,7},... | collective-permute-start | bytes 1572872 | tf_op jit(solution)/shard_map/ppermute | solution.py:489
  4.8 23.5 %collective-permute-start.4 = (bf16[1024,256]{1,0:T(8,128)(2,1)S(1)}, bf16[1024,256]{1,0:T(8,128)(2,1)S(1)}, u32[]{:S(2)}, u32[]{:S(2)}) collective-permute-start(bf16[1024,256]{1,0:T(8,128)(2,1)S(1)} %get-tuple-element.41.refs_3_), channel_id=1, source_target_pairs={{0,12},{2,14},{4,0},{6,2},{8,4},{10,6},{12,8},{14,10},{1,13},{3,15... | collective-permute-start | bytes 1572872 | tf_op jit(solution)/shard_map/ppermute | solution.py:489
  8.1 24.0 %collective-permute-start.5 = (bf16[1024,256]{1,0:T(8,128)(2,1)S(1)}, bf16[1024,256]{1,0:T(8,128)(2,1)S(1)}, u32[]{:S(2)}, u32[]{:S(2)}) collective-permute-start(bf16[1024,256]{1,0:T(8,128)(2,1)S(1)} %get-tuple-element.40.refs_6_), channel_id=1, source_target_pairs={{0,4},{2,6},{4,8},{6,10},{8,12},{10,14},{12,0},{14,2},{1,5},{3,7},... | collective-permute-start | bytes 1572872 | tf_op jit(solution)/shard_map/ppermute | solution.py:489
  8.7 44.0 %copy-start.6 = (s32[32]{0:T(128)}, s32[32]{0:T(128)S(1)}, u32[]{:S(2)}) copy-start(s32[32]{0:T(128)S(1)} %shard_map.95.at_ref.refs_0_) | copy-start | bytes 388
  8.7 1.6 %copy-start = (bf16[1,128,8192]{2,1,0:T(8,128)(2,1)S(1)}, bf16[1,128,8192]{2,1,0:T(8,128)(2,1)}, u32[]{:S(2)}) copy-start(bf16[1,128,8192]{2,1,0:T(8,128)(2,1)} %param.8) | copy-start | bytes 6291460
  17.1 22.1 %collective-permute-start.9 = (bf16[1024,256]{1,0:T(8,128)(2,1)S(1)}, bf16[1024,256]{1,0:T(8,128)(2,1)S(1)}, u32[]{:S(2)}, u32[]{:S(2)}) collective-permute-start(bf16[1024,256]{1,0:T(8,128)(2,1)S(1)} %collective-permute-done.1.second_ref.refs_7_), channel_id=1, source_target_pairs={{0,12},{2,14},{4,0},{6,2},{8,4},{10,6},{12,8},{14,10},{1,13},{3,15... | collective-permute-start | bytes 1572872 | tf_op jit(solution)/shard_map/ppermute | solution.py:489
  20.8 21.8 %collective-permute-start.7 = (bf16[1024,256]{1,0:T(8,128)(2,1)S(1)}, bf16[1024,256]{1,0:T(8,128)(2,1)S(1)}, u32[]{:S(2)}, u32[]{:S(2)}) collective-permute-start(bf16[1024,256]{1,0:T(8,128)(2,1)S(1)} %collective-permute-done.first_ref.refs_4_), channel_id=1, source_target_pairs={{0,4},{2,6},{4,8},{6,10},{8,12},{10,14},{12,0},{14,2},{1,5},{3,7},... | collective-permute-start | bytes 1572872 | tf_op jit(solution)/shard_map/ppermute | solution.py:489
  34.4 10.1 %copy-start.3 = (bf16[1,128,2048]{2,1,0:T(8,128)(2,1)S(1)}, bf16[1,128,2048]{2,1,0:T(8,128)(2,1)}, u32[]{:S(2)}) copy-start(bf16[1,128,2048]{2,1,0:T(8,128)(2,1)} %param.11) | copy-start | bytes 1572868
  34.4 10.1 %copy-start.4 = (bf16[1,128,2048]{2,1,0:T(8,128)(2,1)S(1)}, bf16[1,128,2048]{2,1,0:T(8,128)(2,1)}, u32[]{:S(2)}) copy-start(bf16[1,128,2048]{2,1,0:T(8,128)(2,1)} %param.12) | copy-start | bytes 1572868
  34.4 10.1 %copy-start.8 = (s32[128]{0:T(128)S(1)}, s32[128]{0:T(128)}, u32[]{:S(2)}) copy-start(s32[128]{0:T(128)} %param.14) | copy-start | bytes 1540
  34.5 10.0 %collective-permute-start.6 = (bf16[2,1024,256]{2,1,0:T(8,128)(2,1)S(1)}, bf16[2,1024,256]{2,1,0:T(8,128)(2,1)S(1)}, u32[]{:S(2)}, u32[]{:S(2)}) collective-permute-start(bf16[2,1024,256]{2,1,0:T(8,128)(2,1)S(1)} %shard_map.99), channel_id=1, source_target_pairs={{0,2},{2,0},{4,6},{6,4},{8,10},{10,8},{12,14},{14,12},{1,3},{3,1},... | collective-permute-start | bytes 3145736 | tf_op jit(solution)/shard_map/ppermute | solution.py:489
  34.7 9.8 %collective-permute-start.3 = (bf16[2,1024,256]{2,1,0:T(8,128)(2,1)S(1)}, bf16[2,1024,256]{2,1,0:T(8,128)(2,1)S(1)}, u32[]{:S(2)}, u32[]{:S(2)}) collective-permute-start(bf16[2,1024,256]{2,1,0:T(8,128)(2,1)S(1)} %shard_map.97), channel_id=1, source_target_pairs={{0,2},{2,0},{4,6},{6,4},{8,10},{10,8},{12,14},{14,12},{1,3},{3,1},... | collective-permute-start | bytes 3145736 | tf_op jit(solution)/shard_map/ppermute | solution.py:489
  35.2 17.4 %collective-permute-start.12 = (bf16[128,4096]{1,0:T(8,128)(2,1)S(1)}, bf16[128,4096]{1,0:T(8,128)(2,1)S(1)}, u32[]{:S(2)}, u32[]{:S(2)}) collective-permute-start(bf16[128,4096]{1,0:T(8,128)(2,1)S(1)} %get-tuple-element.31), channel_id=1, source_target_pairs={{0,2},{2,0},{4,6},{6,4},{8,10},{10,8},{12,14},{14,12},{1,3},{3,1},... | collective-permute-start | bytes 3145736 | tf_op jit(solution)/shard_map/ppermute | solution.py:489
  39.2 3.4 %collective-permute-start.10 = (bf16[1024,256]{1,0:T(8,128)(2,1)S(1)}, bf16[1024,256]{1,0:T(8,128)(2,1)S(1)}, u32[]{:S(2)}, u32[]{:S(2)}) collective-permute-start(bf16[1024,256]{1,0:T(8,128)(2,1)S(1)} %collective-permute-done.9.refs_6_), channel_id=1, source_target_pairs={{0,2},{2,0},{4,6},{6,4},{8,10},{10,8},{12,14},{14,12},{1,3},{3,1},... | collective-permute-start | bytes 1572872 | tf_op jit(solution)/shard_map/ppermute | solution.py:489
  42.6 1.9 %collective-permute-start.8 = (bf16[1024,256]{1,0:T(8,128)(2,1)S(1)}, bf16[1024,256]{1,0:T(8,128)(2,1)S(1)}, u32[]{:S(2)}, u32[]{:S(2)}) collective-permute-start(bf16[1024,256]{1,0:T(8,128)(2,1)S(1)} %collective-permute-done.7.refs_4_), channel_id=1, source_target_pairs={{0,2},{2,0},{4,6},{6,4},{8,10},{10,8},{12,14},{14,12},{1,3},{3,1},... | collective-permute-start | bytes 1572872 | tf_op jit(solution)/shard_map/ppermute | solution.py:489
  44.5 3.5 %copy-start.1 = (bf16[1,128,8192]{2,1,0:T(8,128)(2,1)S(1)}, bf16[1,128,8192]{2,1,0:T(8,128)(2,1)}, u32[]{:S(2)}) copy-start(bf16[1,128,8192]{2,1,0:T(8,128)(2,1)} %param.8) | copy-start | bytes 6291460
  50.1 26.8 %collective-permute-start.11 = (bf16[128,4096]{1,0:T(8,128)(2,1)S(1)}, bf16[128,4096]{1,0:T(8,128)(2,1)S(1)}, u32[]{:S(2)}, u32[]{:S(2)}) collective-permute-start(bf16[128,4096]{1,0:T(8,128)(2,1)S(1)} %shard_map.102), channel_id=1, source_target_pairs={{0,1},{1,0},{2,3},{3,2},{4,5},{5,4},{6,7},{7,6},{8,9},{9,8},{10,11... | collective-permute-start | bytes 3145736 | tf_op jit(solution)/shard_map/ppermute | solution.py:527
  50.5 2.1 %collective-permute-start.13 = (bf16[128,512]{1,0:T(8,128)(2,1)S(1)}, bf16[128,512]{1,0:T(8,128)(2,1)S(1)}, u32[]{:S(2)}, u32[]{:S(2)}) collective-permute-start(bf16[128,512]{1,0:T(8,128)(2,1)S(1)} %get-tuple-element.26.refs_1_.grads_ref), channel_id=1, source_target_pairs={{0,2},{2,0},{4,6},{6,4},{8,10},{10,8},{12,14},{14,12},{1,3},{3,1},... | collective-permute-start | bytes 393224 | tf_op jit(solution)/shard_map/ppermute | solution.py:489
  54.5 1.0 copy-start.10
  55.5 15.6 %collective-permute-start.14 = (bf16[512,512]{1,0:T(8,128)(2,1)S(1)}, bf16[512,512]{1,0:T(8,128)(2,1)S(1)}, u32[]{:S(2)}, u32[]{:S(2)}) collective-permute-start(bf16[512,512]{1,0:T(8,128)(2,1)S(1)} %get-tuple-element.34), channel_id=1, source_target_pairs={{0,4},{2,6},{4,8},{6,10},{8,12},{10,14},{12,0},{14,2},{1,5},{3,7},... | collective-permute-start | bytes 1572872 | tf_op jit(solution)/shard_map/ppermute | solution.py:489
  55.5 15.6 %collective-permute-start.15 = (bf16[512,512]{1,0:T(8,128)(2,1)S(1)}, bf16[512,512]{1,0:T(8,128)(2,1)S(1)}, u32[]{:S(2)}, u32[]{:S(2)}) collective-permute-start(bf16[512,512]{1,0:T(8,128)(2,1)S(1)} %get-tuple-element.35), channel_id=1, source_target_pairs={{0,12},{2,14},{4,0},{6,2},{8,4},{10,6},{12,8},{14,10},{1,13},{3,15... | collective-permute-start | bytes 1572872 | tf_op jit(solution)/shard_map/ppermute | solution.py:489
  71.3 6.7 %copy-start.9 = (bf16[1024,512]{1,0:T(8,128)(2,1)}, bf16[1024,512]{1,0:T(8,128)(2,1)S(1)}, u32[]{:S(2)}) copy-start(bf16[1024,512]{1,0:T(8,128)(2,1)S(1)} %get-tuple-element.38) | copy-start | bytes 3145732
  76.9 13.7 %copy-start.2 = (bf16[128,4096]{1,0:T(8,128)(2,1)S(1)}, bf16[128,4096]{1,0:T(8,128)(2,1)}, u32[]{:S(2)}) copy-start(bf16[128,4096]{1,0:T(8,128)(2,1)} %in_ref.1) | copy-start | bytes 3145732
  76.9 13.7 %copy-start.7 = (s32[32]{0:T(128)S(1)}, s32[32]{0:T(128)}, u32[]{:S(2)}) copy-start(s32[32]{0:T(128)} %copy-done.6) | copy-start | bytes 388
  76.9 14.2 %copy-start.12 = (s32[1,2,8,2]{2,3,1,0:T(2,128)S(1)}, s32[1,2,8,2]{2,3,1,0:T(2,128)}, u32[]{:S(2)}) copy-start(s32[1,2,8,2]{2,3,1,0:T(2,128)} %param.15) | copy-start | bytes 388
  78.0 35.0 %all-to-all-start = ((bf16[16,8,4096]{2,1,0:T(8,128)(2,1)}), bf16[16,8,4096]{2,1,0:T(8,128)(2,1)S(1)}, u32[]{:S(2)}, u32[]{:S(2)}) async-start(bf16[16,8,4096]{2,1,0:T(8,128)(2,1)} %bitcast.7), calls=%async_computation | async-start | bytes 2097152 | tf_op jit(solution)/shard_map/all_to_all | solution.py:537
  87.3 32.1 %collective-permute-start.16 = (bf16[1024,512]{1,0:T(8,128)(2,1)}, bf16[1024,512]{1,0:T(8,128)(2,1)}, u32[]{:S(2)}, u32[]{:S(2)}) collective-permute-start(bf16[1024,512]{1,0:T(8,128)(2,1)} %copy-done.9), channel_id=1, source_target_pairs={{0,4},{2,6},{4,8},{6,10},{8,12},{10,14},{12,0},{14,2},{1,5},{3,7},... | collective-permute-start | bytes 3145736 | tf_op jit(solution)/shard_map/ppermute | solution.py:489
  87.4 32.0 %collective-permute-start.17 = (bf16[1024,512]{1,0:T(8,128)(2,1)S(1)}, bf16[1024,512]{1,0:T(8,128)(2,1)}, u32[]{:S(2)}, u32[]{:S(2)}) collective-permute-start(bf16[1024,512]{1,0:T(8,128)(2,1)S(1)} %get-tuple-element.39), channel_id=1, source_target_pairs={{0,12},{2,14},{4,0},{6,2},{8,4},{10,6},{12,8},{14,10},{1,13},{3,15... | collective-permute-start | bytes 3145736 | tf_op jit(solution)/shard_map/ppermute | solution.py:489
  114.0 32.6 %all-to-all-start.1 = ((bf16[16,8,4096]{2,1,0:T(8,128)(2,1)}), bf16[16,8,4096]{2,1,0:T(8,128)(2,1)}, u32[]{:S(2)}, u32[]{:S(2)}) async-start(bf16[16,8,4096]{2,1,0:T(8,128)(2,1)} %shard_map.107), calls=%async_computation.1 | async-start | bytes 2097152 | tf_op jit(solution)/shard_map/all_to_all | solution.py:542
  119.4 1.2 copy-start.11
  (1 other events, 0.8 us)

commit v7 on v6

--- a/solution.py
+++ b/solution.py
@@ -361,38 +361,42 @@
     )(mine, arrived, token)
 
 
-def copy_kernel(at_ref, in_ref, out_ref):
-    out_ref[...] = in_ref[...]
+def top_kernel(at_ref, in_ref, out_ref):
+    half = out_ref.shape[0]
+    both = in_ref[...].astype(jnp.float32)
+    out_ref[...] = jnp.where(lax.rem(at_ref[STAGE], 2) == 0, both[:half], both[half:])
 
 
 def take_rows(places, array, rows):
     width = array.shape[1]
     return pl.pallas_call(
-        copy_kernel,
+        top_kernel,
         grid_spec=pltpu.PrefetchScalarGridSpec(
             num_scalar_prefetch=1,
             grid=(1,),
-            in_specs=[pl.BlockSpec((rows, width), lambda i, at: (at[STAGE], 0))],
+            in_specs=[pl.BlockSpec((2 * rows, width), lambda i, at: (at[STAGE] // 2, 0))],
             out_specs=pl.BlockSpec((rows, width), lambda i, at: (0, 0)),
         ),
-        out_shape=jax.ShapeDtypeStruct((rows, width), array.dtype),
-        compiler_params=pltpu.CompilerParams(vmem_limit_bytes=MIB),
+        out_shape=jax.ShapeDtypeStruct((rows, width), jnp.float32),
+        compiler_params=pltpu.CompilerParams(vmem_limit_bytes=2 * MIB),
         cost_estimate=cost(1, 1),
     )(places, array)
 
 
 def suffix_kernel(parts_ref, top_ref, out_ref, held, sems):
     copies = []
-    width = held.shape[2] // sems.shape[0]
+    rows = top_ref.shape[0]
+    width = held.shape[1] // sems.shape[0]
     for i in range(sems.shape[0]):
         at = pl.ds(i * width, width)
-        running = top_ref[:, at].astype(jnp.float32)
-        for layer in reversed(range(parts_ref.shape[0])):
-            running = running + parts_ref[layer, :, at].astype(jnp.float32)
-            held[layer, :, at] = running.astype(jnp.bfloat16)
-        copies.append(
-            pltpu.make_async_copy(held.at[:, :, at], out_ref.at[:, :, at], sems.at[i])
-        )
+        running = top_ref[:, at]
+        for first in reversed(range(0, held.shape[0], 2 * rows)):
+            two = pl.ds(first, 2 * rows)
+            layers = parts_ref[two, at].astype(jnp.float32)
+            later = running + layers[rows:]
+            running = later + layers[:rows]
+            held[two, at] = jnp.concatenate([running, later], 0).astype(jnp.bfloat16)
+        copies.append(pltpu.make_async_copy(held.at[:, at], out_ref.at[:, at], sems.at[i]))
         copies[-1].start()
     for copy in copies:
         copy.wait()
@@ -536,12 +540,8 @@
     branch = add_halves(mine, arrived, token)
     parts = lax.all_to_all(branch, "pipe", 0, 0, tiled=True)
     rows = token_count // pipe_count
-    sums = suffix_sum(
-        parts.reshape(pipe_count, rows, branch.shape[1]), take_rows(places, top_grad, rows)
-    )
-    input_grad = lax.all_to_all(
-        sums.reshape(token_count, branch.shape[1]), "pipe", 0, 0, tiled=True
-    )
+    sums = suffix_sum(parts, take_rows(places, top_grad, rows))
+    input_grad = lax.all_to_all(sums, "pipe", 0, 0, tiled=True)
     weight_grad = scaled_grad([own, *received], jnp.exp2(-scale_exp[0].astype(jnp.float32)))
     return (moved(input_grad)[None], weight_grad[None])
 

time: 149 us -> 149 us (level)
  no operation moved by 1% of the time
where the time goes in v7:
time: 149 us
  waiting for transfers between devices  87.4 us (59%)
  starting transfers between devices  32.2 us (22%)
  Pallas kernels  22.1 us (15%)
  local copies, waits for them, and re-layouts  5.93 us (4%)
    ppermute x17, waiting for transfers between devices, on_device(): send = lambda piece, pairs: lax.ppermute(piece, 'dp', pairs)  36.7 us
    all_to_all x1, waiting for transfers between devices, on_device(): input_grad = lax.all_to_all(sums, 'pipe', 0, 0, tiled=True)  23.5 us
    all_to_all x1, waiting for transfers between devices, on_device(): parts = lax.all_to_all(branch, 'pipe', 0, 0, tiled=True)  21.7 us
    ppermute x17, starting transfers between devices, on_device(): send = lambda piece, pairs: lax.ppermute(piece, 'dp', pairs)  17.2 us
    all_to_all x1, starting transfers between devices, on_device(): parts = lax.all_to_all(branch, 'pipe', 0, 0, tiled=True)  9.29 us
    ppermute x1, waiting for transfers between devices, on_device(): lax.ppermute(share(THEIRS, jnp.bfloat16), 'tensor', [(0, 1), (1, 0)])  5.59 us
    all_to_all x1, starting transfers between devices, on_device(): input_grad = lax.all_to_all(sums, 'pipe', 0, 0, tiled=True)  5.3 us
    unnamed x26, local copies, waits for them, and re-layouts  4.58 us
  transfers between devices with their start and end apart: 20, of which 10 were waited for; matrix products, arithmetic and copies ran while one was open for 1% of the time, Pallas kernels for 13%

profile of v7, /device:TPU:16, one launch (start us, length us, event | category | flops | bytes accessed | tf_op | source)
XLA Modules:
  0.0 148.8 jit_solution(7727201410637380004)
XLA Ops:
  0.7 1.3 slice_bitcast_fusion
  2.0 2.8 %collective-permute-start.1 = (bf16[1024,256]{1,0:T(8,128)(2,1)S(1)}, bf16[1024,256]{1,0:T(8,128)(2,1)S(1)}, u32[]{:S(2)}, u32[]{:S(2)}) collective-permute-start(bf16[1024,256]{1,0:T(8,128)(2,1)S(1)} %get-tuple-element.40.refs_6_), channel_id=1, source_target_pairs={{0,12},{2,14},{4,0},{6,2},{8,4},{10,6},{12,8},{14,10},{1,13},{3,15... | collective-permute-start | bytes 1572872 | tf_op jit(solution)/shard_map/ppermute | solution.py:493
  4.8 3.2 %collective-permute-start.4 = (bf16[1024,256]{1,0:T(8,128)(2,1)S(1)}, bf16[1024,256]{1,0:T(8,128)(2,1)S(1)}, u32[]{:S(2)}, u32[]{:S(2)}) collective-permute-start(bf16[1024,256]{1,0:T(8,128)(2,1)S(1)} %get-tuple-element.41.refs_3_), channel_id=1, source_target_pairs={{0,12},{2,14},{4,0},{6,2},{8,4},{10,6},{12,8},{14,10},{1,13},{3,15... | collective-permute-start | bytes 1572872 | tf_op jit(solution)/shard_map/ppermute | solution.py:493
  8.7 1.6 %copy-done = bf16[1,128,8192]{2,1,0:T(8,128)(2,1)S(1)} copy-done((bf16[1,128,8192]{2,1,0:T(8,128)(2,1)S(1)}, bf16[1,128,8192]{2,1,0:T(8,128)(2,1)}, u32[]{:S(2)}) %copy-start) | copy-done | bytes 2097176
  10.3 0.8 copy-done.5
  11.0 2.1 %shard_map.96 = (bf16[128,8192]{1,0:T(8,128)(2,1)S(1)}, f32[128,1]{1,0:T(8,128)S(1)}, bf16[128,4096]{1,0:T(8,128)(2,1)S(1)}) custom-call(s32[32]{0:T(128)S(1)} %shard_map.95.at_ref.refs_0_, bf16[128,8192]{1,0:T(8,128)(2,1)S(1)} %bitcast.17, bf16[1,8192]{1,0:T(2,128)(2,1)S(1)} %copy-done.5), custom_call_target="tpu_custom_call" | custom-call | flops 1 | bytes 1 | tf_op jit(solution)/shard_map/pallas_call | solution.py:102
  13.2 3.9 %collective-permute-done.1.second_ref.refs_7_ = bf16[1024,256]{1,0:T(8,128)(2,1)S(1)} collective-permute-done((bf16[1024,256]{1,0:T(8,128)(2,1)S(1)}, bf16[1024,256]{1,0:T(8,128)(2,1)S(1)}, u32[]{:S(2)}, u32[]{:S(2)}) %collective-permute-start.1) | collective-permute-done | bytes 524320 | tf_op jit(solution)/shard_map/ppermute | solution.py:493
  17.1 3.7 %collective-permute-start.9 = (bf16[1024,256]{1,0:T(8,128)(2,1)S(1)}, bf16[1024,256]{1,0:T(8,128)(2,1)S(1)}, u32[]{:S(2)}, u32[]{:S(2)}) collective-permute-start(bf16[1024,256]{1,0:T(8,128)(2,1)S(1)} %collective-permute-done.1.second_ref.refs_7_), channel_id=1, source_target_pairs={{0,12},{2,14},{4,0},{6,2},{8,4},{10,6},{12,8},{14,10},{1,13},{3,15... | collective-permute-start | bytes 1572872 | tf_op jit(solution)/shard_map/ppermute | solution.py:493
  20.8 7.5 %collective-permute-done.4.refs_5_.first_ref = bf16[1024,256]{1,0:T(8,128)(2,1)S(1)} collective-permute-done((bf16[1024,256]{1,0:T(8,128)(2,1)S(1)}, bf16[1024,256]{1,0:T(8,128)(2,1)S(1)}, u32[]{:S(2)}, u32[]{:S(2)}) %collective-permute-start.4) | collective-permute-done | bytes 524320 | tf_op jit(solution)/shard_map/ppermute | solution.py:493
  28.3 3.7 %collective-permute-done.5.refs_8_.second_ref = bf16[1024,256]{1,0:T(8,128)(2,1)S(1)} collective-permute-done((bf16[1024,256]{1,0:T(8,128)(2,1)S(1)}, bf16[1024,256]{1,0:T(8,128)(2,1)S(1)}, u32[]{:S(2)}, u32[]{:S(2)}) %collective-permute-start.5) | collective-permute-done | bytes 524320 | tf_op jit(solution)/shard_map/ppermute | solution.py:493
  32.0 2.3 %shard_map.98 = (f32[128,256]{1,0:T(8,128)S(1)}, f32[128,256]{1,0:T(8,128)S(1)}, bf16[8192,256]{1,0:T(8,128)(2,1)S(1)}, bf16[8192,256]{1,0:T(8,128)(2,1)S(1)}) custom-call(s32[32]{0:T(128)S(1)} %shard_map.95.at_ref.refs_0_, bf16[128,8192]{1,0:T(8,128)(2,1)S(1)} %get-tuple-element.21.refs_1_.normed_ref, ...), custom_call_target="tpu_custom_call" | custom-call | flops 1 | bytes 1 | tf_op jit(solution)/shard_map/pallas_call | solution.py:147
  35.3 3.8 %collective-permute-done.9.refs_6_ = bf16[1024,256]{1,0:T(8,128)(2,1)S(1)} collective-permute-done((bf16[1024,256]{1,0:T(8,128)(2,1)S(1)}, bf16[1024,256]{1,0:T(8,128)(2,1)S(1)}, u32[]{:S(2)}, u32[]{:S(2)}) %collective-permute-start.9) | collective-permute-done | bytes 524320 | tf_op jit(solution)/shard_map/ppermute | solution.py:493
  39.2 3.4 %collective-permute-done.7.refs_4_ = bf16[1024,256]{1,0:T(8,128)(2,1)S(1)} collective-permute-done((bf16[1024,256]{1,0:T(8,128)(2,1)S(1)}, bf16[1024,256]{1,0:T(8,128)(2,1)S(1)}, u32[]{:S(2)}, u32[]{:S(2)}) %collective-permute-start.7) | collective-permute-done | bytes 524320 | tf_op jit(solution)/shard_map/ppermute | solution.py:493
  42.6 1.9 %collective-permute-done.8.refs_5_ = bf16[1024,256]{1,0:T(8,128)(2,1)S(1)} collective-permute-done((bf16[1024,256]{1,0:T(8,128)(2,1)S(1)}, bf16[1024,256]{1,0:T(8,128)(2,1)S(1)}, u32[]{:S(2)}, u32[]{:S(2)}) %collective-permute-start.8) | collective-permute-done | bytes 524320 | tf_op jit(solution)/shard_map/ppermute | solution.py:493
  44.5 3.5 %shard_map.100 = (bf16[8192,256]{1,0:T(8,128)(2,1)S(1)}, bf16[8192,256]{1,0:T(8,128)(2,1)S(1)}, bf16[128,512]{1,0:T(8,128)(2,1)S(1)}, f32[128,1]{1,0:T(8,128)S(1)}) custom-call(s32[32]{0:T(128)S(1)} %shard_map.95.at_ref.refs_0_, bf16[128,8192]{1,0:T(8,128)(2,1)S(1)} %get-tuple-element.21.refs_1_.normed_ref, ...), custom_call_target="tpu_custom_call", output_to_operand_aliasing={{0}: (10, {}), {1}: (11, {})} | custom-call | flops 536870912 | bytes 5242880 | tf_op jit(solution)/shard_map/pallas_call | solution.py:217
  48.0 2.1 %shard_map.102 = bf16[128,4096]{1,0:T(8,128)(2,1)S(1)} custom-call(s32[32]{0:T(128)S(1)} %shard_map.95.at_ref.refs_0_, bf16[128,512]{1,0:T(8,128)(2,1)S(1)} %get-tuple-element.26.refs_1_.grads_ref, bf16[8192,256]{1,0:T(8,128)(2,1)S(1)} %get-tuple-element.27.refs_2_, bf16[8192,256]{1,0:T(8,128)(2,1)S(1)} %get-tuple-element.28.refs_3_, ...), custom_call_target="tpu_custom_call" | custom-call | flops 536870912 | bytes 5242880 | tf_op jit(solution)/shard_map/pallas_call | solution.py:268
  50.5 2.1 %shard_map.101.after_ref.mine_ref = f32[128,4096]{1,0:T(8,128)S(1)} custom-call(s32[32]{0:T(128)S(1)} %shard_map.95.at_ref.refs_0_, bf16[128,512]{1,0:T(8,128)(2,1)S(1)} %get-tuple-element.26.refs_1_.grads_ref, bf16[8192,256]{1,0:T(8,128)(2,1)S(1)} %get-tuple-element.27.refs_2_, bf16[8192,256]{1,0:T(8,128)(2,1)S(1)} %get-tuple-element.28.refs_3_, ...), custom_call_target="tpu_custom_call" | custom-call | flops 536870912 | bytes 5242880 | tf_op jit(solution)/shard_map/pallas_call | solution.py:268
  52.6 1.8 %shard_map.103 = (bf16[1024,512]{1,0:T(8,128)(2,1)S(1)}, bf16[1024,512]{1,0:T(8,128)(2,1)S(1)}, bf16[1024,512]{1,0:T(8,128)(2,1)S(1)}, bf16[512,512]{1,0:T(8,128)(2,1)S(1)}, bf16[512,512]{1,0:T(8,128)(2,1)S(1)}) custom-call(s32[32]{0:T(128)S(1)} %shard_map.95.at_ref.refs_0_, bf16[128,8192]{1,0:T(8,128)(2,1)S(1)} %get-tuple-element.21.refs_1_.normed_ref, ...), custom_call_target="tpu_custom_call" | custom-call | flops 2147483648 | bytes 4194304 | tf_op jit(solution)/shard_map/pallas_call | solution.py:305
  54.5 1.0 copy-done.10
  55.5 3.2 %collective-permute-start.15 = (bf16[512,512]{1,0:T(8,128)(2,1)S(1)}, bf16[512,512]{1,0:T(8,128)(2,1)S(1)}, u32[]{:S(2)}, u32[]{:S(2)}) collective-permute-start(bf16[512,512]{1,0:T(8,128)(2,1)S(1)} %get-tuple-element.35), channel_id=1, source_target_pairs={{0,12},{2,14},{4,0},{6,2},{8,4},{10,6},{12,8},{14,10},{1,13},{3,15... | collective-permute-start | bytes 1572872 | tf_op jit(solution)/shard_map/ppermute | solution.py:493
  58.7 12.3 %collective-permute-done.14.far_right_ref = bf16[512,512]{1,0:T(8,128)(2,1)S(1)} collective-permute-done((bf16[512,512]{1,0:T(8,128)(2,1)S(1)}, bf16[512,512]{1,0:T(8,128)(2,1)S(1)}, u32[]{:S(2)}, u32[]{:S(2)}) %collective-permute-start.14) | collective-permute-done | bytes 524320 | tf_op jit(solution)/shard_map/ppermute | solution.py:493
  71.3 5.6 %collective-permute-done.11.arrived_ref = bf16[128,4096]{1,0:T(8,128)(2,1)S(1)} collective-permute-done((bf16[128,4096]{1,0:T(8,128)(2,1)S(1)}, bf16[128,4096]{1,0:T(8,128)(2,1)S(1)}, u32[]{:S(2)}, u32[]{:S(2)}) %collective-permute-start.11) | collective-permute-done | bytes 1048608 | tf_op jit(solution)/shard_map/ppermute | solution.py:531
  76.9 1.0 shard_map.105
  78.0 9.3 %all-to-all-start = ((bf16[16,8,4096]{2,1,0:T(8,128)(2,1)}), bf16[16,8,4096]{2,1,0:T(8,128)(2,1)S(1)}, u32[]{:S(2)}, u32[]{:S(2)}) async-start(bf16[16,8,4096]{2,1,0:T(8,128)(2,1)} %bitcast.7), calls=%async_computation | async-start | bytes 2097152 | tf_op jit(solution)/shard_map/all_to_all | solution.py:541
  87.4 3.2 %collective-permute-start.17 = (bf16[1024,512]{1,0:T(8,128)(2,1)S(1)}, bf16[1024,512]{1,0:T(8,128)(2,1)}, u32[]{:S(2)}, u32[]{:S(2)}) collective-permute-start(bf16[1024,512]{1,0:T(8,128)(2,1)S(1)} %get-tuple-element.39), channel_id=1, source_target_pairs={{0,12},{2,14},{4,0},{6,2},{8,4},{10,6},{12,8},{14,10},{1,13},{3,15... | collective-permute-start | bytes 3145736 | tf_op jit(solution)/shard_map/ppermute | solution.py:493
  91.3 21.7 %all-to-all-done = bf16[16,8,4096]{2,1,0:T(8,128)(2,1)S(1)} async-done(((bf16[16,8,4096]{2,1,0:T(8,128)(2,1)}), bf16[16,8,4096]{2,1,0:T(8,128)(2,1)S(1)}, u32[]{:S(2)}, u32[]{:S(2)}) %all-to-all-start) | async-done | bytes 1048608 | tf_op jit(solution)/shard_map/all_to_all | solution.py:541
  113.0 1.0 shard_map.107
  114.0 5.3 %all-to-all-start.1 = ((bf16[16,8,4096]{2,1,0:T(8,128)(2,1)}), bf16[16,8,4096]{2,1,0:T(8,128)(2,1)}, u32[]{:S(2)}, u32[]{:S(2)}) async-start(bf16[16,8,4096]{2,1,0:T(8,128)(2,1)} %bitcast.9), calls=%async_computation.1 | async-start | bytes 2097152 | tf_op jit(solution)/shard_map/all_to_all | solution.py:544
  119.4 1.2 copy-done.11
  120.6 2.6 %shard_map.109 = bf16[2,1024,256]{2,1,0:T(8,128)(2,1)} custom-call(f32[2,8,2]{2,1,0:T(8,128)S(1)} %copy.12.factor_ref, bf16[1024,512]{1,0:T(8,128)(2,1)S(1)} %copy-done.11, bf16[1024,512]{1,0:T(8,128)(2,1)} %collective-permute-done.16.refs_1_, bf16[1024,512]{1,0:T(8,128)(2,1)} %collective-permute-done.17.refs_2_), custom_call_target="tpu_custom_call" | custom-call | flops 999999986991104 | bytes 999999995904 | tf_op jit(solution)/shard_map/pallas_call | solution.py:468
  123.2 23.5 %all-to-all-done.1 = bf16[16,8,4096]{2,1,0:T(8,128)(2,1)} async-done(((bf16[16,8,4096]{2,1,0:T(8,128)(2,1)}), bf16[16,8,4096]{2,1,0:T(8,128)(2,1)}, u32[]{:S(2)}, u32[]{:S(2)}) %all-to-all-start.1) | async-done | bytes 1048608 | tf_op jit(solution)/shard_map/all_to_all | solution.py:544
  146.7 2.0 %shard_map.108 = bf16[128,4096]{1,0:T(8,128)(2,1)} custom-call(bf16[128,4096]{1,0:T(8,128)(2,1)} %bitcast.10.in_ref), custom_call_target="tpu_custom_call" | custom-call | flops 1 | bytes 1 | tf_op jit(solution)/shard_map/pallas_call | solution.py:438
  (52 shorter events, 3.2 us)
Async XLA Ops:
  0.6 31.4 %collective-permute-start.2 = (bf16[2,1024,256]{2,1,0:T(8,128)(2,1)}, bf16[2,1024,256]{2,1,0:T(8,128)(2,1)S(1)}, u32[]{:S(2)}, u32[]{:S(2)}) collective-permute-start(bf16[2,1024,256]{2,1,0:T(8,128)(2,1)} %bitcast.24), channel_id=1, source_target_pairs={{0,2},{2,0},{4,6},{6,4},{8,10},{10,8},{12,14},{14,12},{1,3},{3,1},... | collective-permute-start | bytes 3145736 | tf_op jit(solution)/shard_map/ppermute | solution.py:493
  2.0 15.1 %collective-permute-start.1 = (bf16[1024,256]{1,0:T(8,128)(2,1)S(1)}, bf16[1024,256]{1,0:T(8,128)(2,1)S(1)}, u32[]{:S(2)}, u32[]{:S(2)}) collective-permute-start(bf16[1024,256]{1,0:T(8,128)(2,1)S(1)} %get-tuple-element.40.refs_6_), channel_id=1, source_target_pairs={{0,12},{2,14},{4,0},{6,2},{8,4},{10,6},{12,8},{14,10},{1,13},{3,15... | collective-permute-start | bytes 1572872 | tf_op jit(solution)/shard_map/ppermute | solution.py:493
  4.8 16.0 %collective-permute-start = (bf16[1024,256]{1,0:T(8,128)(2,1)S(1)}, bf16[1024,256]{1,0:T(8,128)(2,1)S(1)}, u32[]{:S(2)}, u32[]{:S(2)}) collective-permute-start(bf16[1024,256]{1,0:T(8,128)(2,1)S(1)} %get-tuple-element.41.refs_3_), channel_id=1, source_target_pairs={{0,4},{2,6},{4,8},{6,10},{8,12},{10,14},{12,0},{14,2},{1,5},{3,7},... | collective-permute-start | bytes 1572872 | tf_op jit(solution)/shard_map/ppermute | solution.py:493
  4.8 23.5 %collective-permute-start.4 = (bf16[1024,256]{1,0:T(8,128)(2,1)S(1)}, bf16[1024,256]{1,0:T(8,128)(2,1)S(1)}, u32[]{:S(2)}, u32[]{:S(2)}) collective-permute-start(bf16[1024,256]{1,0:T(8,128)(2,1)S(1)} %get-tuple-element.41.refs_3_), channel_id=1, source_target_pairs={{0,12},{2,14},{4,0},{6,2},{8,4},{10,6},{12,8},{14,10},{1,13},{3,15... | collective-permute-start | bytes 1572872 | tf_op jit(solution)/shard_map/ppermute | solution.py:493
  8.1 24.0 %collective-permute-start.5 = (bf16[1024,256]{1,0:T(8,128)(2,1)S(1)}, bf16[1024,256]{1,0:T(8,128)(2,1)S(1)}, u32[]{:S(2)}, u32[]{:S(2)}) collective-permute-start(bf16[1024,256]{1,0:T(8,128)(2,1)S(1)} %get-tuple-element.40.refs_6_), channel_id=1, source_target_pairs={{0,4},{2,6},{4,8},{6,10},{8,12},{10,14},{12,0},{14,2},{1,5},{3,7},... | collective-permute-start | bytes 1572872 | tf_op jit(solution)/shard_map/ppermute | solution.py:493
  8.7 44.0 %copy-start.6 = (s32[32]{0:T(128)}, s32[32]{0:T(128)S(1)}, u32[]{:S(2)}) copy-start(s32[32]{0:T(128)S(1)} %shard_map.95.at_ref.refs_0_) | copy-start | bytes 388
  8.7 1.6 %copy-start = (bf16[1,128,8192]{2,1,0:T(8,128)(2,1)S(1)}, bf16[1,128,8192]{2,1,0:T(8,128)(2,1)}, u32[]{:S(2)}) copy-start(bf16[1,128,8192]{2,1,0:T(8,128)(2,1)} %param.8) | copy-start | bytes 6291460
  17.1 22.1 %collective-permute-start.9 = (bf16[1024,256]{1,0:T(8,128)(2,1)S(1)}, bf16[1024,256]{1,0:T(8,128)(2,1)S(1)}, u32[]{:S(2)}, u32[]{:S(2)}) collective-permute-start(bf16[1024,256]{1,0:T(8,128)(2,1)S(1)} %collective-permute-done.1.second_ref.refs_7_), channel_id=1, source_target_pairs={{0,12},{2,14},{4,0},{6,2},{8,4},{10,6},{12,8},{14,10},{1,13},{3,15... | collective-permute-start | bytes 1572872 | tf_op jit(solution)/shard_map/ppermute | solution.py:493
  20.8 21.8 %collective-permute-start.7 = (bf16[1024,256]{1,0:T(8,128)(2,1)S(1)}, bf16[1024,256]{1,0:T(8,128)(2,1)S(1)}, u32[]{:S(2)}, u32[]{:S(2)}) collective-permute-start(bf16[1024,256]{1,0:T(8,128)(2,1)S(1)} %collective-permute-done.first_ref.refs_4_), channel_id=1, source_target_pairs={{0,4},{2,6},{4,8},{6,10},{8,12},{10,14},{12,0},{14,2},{1,5},{3,7},... | collective-permute-start | bytes 1572872 | tf_op jit(solution)/shard_map/ppermute | solution.py:493
  34.4 10.1 %copy-start.3 = (bf16[1,128,2048]{2,1,0:T(8,128)(2,1)S(1)}, bf16[1,128,2048]{2,1,0:T(8,128)(2,1)}, u32[]{:S(2)}) copy-start(bf16[1,128,2048]{2,1,0:T(8,128)(2,1)} %param.11) | copy-start | bytes 1572868
  34.4 10.1 %copy-start.4 = (bf16[1,128,2048]{2,1,0:T(8,128)(2,1)S(1)}, bf16[1,128,2048]{2,1,0:T(8,128)(2,1)}, u32[]{:S(2)}) copy-start(bf16[1,128,2048]{2,1,0:T(8,128)(2,1)} %param.12) | copy-start | bytes 1572868
  34.4 10.1 %copy-start.8 = (s32[128]{0:T(128)S(1)}, s32[128]{0:T(128)}, u32[]{:S(2)}) copy-start(s32[128]{0:T(128)} %param.14) | copy-start | bytes 1540
  34.5 10.0 %collective-permute-start.6 = (bf16[2,1024,256]{2,1,0:T(8,128)(2,1)S(1)}, bf16[2,1024,256]{2,1,0:T(8,128)(2,1)S(1)}, u32[]{:S(2)}, u32[]{:S(2)}) collective-permute-start(bf16[2,1024,256]{2,1,0:T(8,128)(2,1)S(1)} %shard_map.99), channel_id=1, source_target_pairs={{0,2},{2,0},{4,6},{6,4},{8,10},{10,8},{12,14},{14,12},{1,3},{3,1},... | collective-permute-start | bytes 3145736 | tf_op jit(solution)/shard_map/ppermute | solution.py:493
  34.7 9.8 %collective-permute-start.3 = (bf16[2,1024,256]{2,1,0:T(8,128)(2,1)S(1)}, bf16[2,1024,256]{2,1,0:T(8,128)(2,1)S(1)}, u32[]{:S(2)}, u32[]{:S(2)}) collective-permute-start(bf16[2,1024,256]{2,1,0:T(8,128)(2,1)S(1)} %shard_map.97), channel_id=1, source_target_pairs={{0,2},{2,0},{4,6},{6,4},{8,10},{10,8},{12,14},{14,12},{1,3},{3,1},... | collective-permute-start | bytes 3145736 | tf_op jit(solution)/shard_map/ppermute | solution.py:493
  35.2 17.4 %collective-permute-start.12 = (bf16[128,4096]{1,0:T(8,128)(2,1)S(1)}, bf16[128,4096]{1,0:T(8,128)(2,1)S(1)}, u32[]{:S(2)}, u32[]{:S(2)}) collective-permute-start(bf16[128,4096]{1,0:T(8,128)(2,1)S(1)} %get-tuple-element.31), channel_id=1, source_target_pairs={{0,2},{2,0},{4,6},{6,4},{8,10},{10,8},{12,14},{14,12},{1,3},{3,1},... | collective-permute-start | bytes 3145736 | tf_op jit(solution)/shard_map/ppermute | solution.py:493
  39.2 3.4 %collective-permute-start.10 = (bf16[1024,256]{1,0:T(8,128)(2,1)S(1)}, bf16[1024,256]{1,0:T(8,128)(2,1)S(1)}, u32[]{:S(2)}, u32[]{:S(2)}) collective-permute-start(bf16[1024,256]{1,0:T(8,128)(2,1)S(1)} %collective-permute-done.9.refs_6_), channel_id=1, source_target_pairs={{0,2},{2,0},{4,6},{6,4},{8,10},{10,8},{12,14},{14,12},{1,3},{3,1},... | collective-permute-start | bytes 1572872 | tf_op jit(solution)/shard_map/ppermute | solution.py:493
  42.6 1.9 %collective-permute-start.8 = (bf16[1024,256]{1,0:T(8,128)(2,1)S(1)}, bf16[1024,256]{1,0:T(8,128)(2,1)S(1)}, u32[]{:S(2)}, u32[]{:S(2)}) collective-permute-start(bf16[1024,256]{1,0:T(8,128)(2,1)S(1)} %collective-permute-done.7.refs_4_), channel_id=1, source_target_pairs={{0,2},{2,0},{4,6},{6,4},{8,10},{10,8},{12,14},{14,12},{1,3},{3,1},... | collective-permute-start | bytes 1572872 | tf_op jit(solution)/shard_map/ppermute | solution.py:493
  44.5 3.5 %copy-start.1 = (bf16[1,128,8192]{2,1,0:T(8,128)(2,1)S(1)}, bf16[1,128,8192]{2,1,0:T(8,128)(2,1)}, u32[]{:S(2)}) copy-start(bf16[1,128,8192]{2,1,0:T(8,128)(2,1)} %param.8) | copy-start | bytes 6291460
  50.1 26.8 %collective-permute-start.11 = (bf16[128,4096]{1,0:T(8,128)(2,1)S(1)}, bf16[128,4096]{1,0:T(8,128)(2,1)S(1)}, u32[]{:S(2)}, u32[]{:S(2)}) collective-permute-start(bf16[128,4096]{1,0:T(8,128)(2,1)S(1)} %shard_map.102), channel_id=1, source_target_pairs={{0,1},{1,0},{2,3},{3,2},{4,5},{5,4},{6,7},{7,6},{8,9},{9,8},{10,11... | collective-permute-start | bytes 3145736 | tf_op jit(solution)/shard_map/ppermute | solution.py:531
  50.5 2.1 %collective-permute-start.13 = (bf16[128,512]{1,0:T(8,128)(2,1)S(1)}, bf16[128,512]{1,0:T(8,128)(2,1)S(1)}, u32[]{:S(2)}, u32[]{:S(2)}) collective-permute-start(bf16[128,512]{1,0:T(8,128)(2,1)S(1)} %get-tuple-element.26.refs_1_.grads_ref), channel_id=1, source_target_pairs={{0,2},{2,0},{4,6},{6,4},{8,10},{10,8},{12,14},{14,12},{1,3},{3,1},... | collective-permute-start | bytes 393224 | tf_op jit(solution)/shard_map/ppermute | solution.py:493
  54.5 1.0 copy-start.10
  55.5 15.6 %collective-permute-start.14 = (bf16[512,512]{1,0:T(8,128)(2,1)S(1)}, bf16[512,512]{1,0:T(8,128)(2,1)S(1)}, u32[]{:S(2)}, u32[]{:S(2)}) collective-permute-start(bf16[512,512]{1,0:T(8,128)(2,1)S(1)} %get-tuple-element.34), channel_id=1, source_target_pairs={{0,4},{2,6},{4,8},{6,10},{8,12},{10,14},{12,0},{14,2},{1,5},{3,7},... | collective-permute-start | bytes 1572872 | tf_op jit(solution)/shard_map/ppermute | solution.py:493
  55.5 15.6 %collective-permute-start.15 = (bf16[512,512]{1,0:T(8,128)(2,1)S(1)}, bf16[512,512]{1,0:T(8,128)(2,1)S(1)}, u32[]{:S(2)}, u32[]{:S(2)}) collective-permute-start(bf16[512,512]{1,0:T(8,128)(2,1)S(1)} %get-tuple-element.35), channel_id=1, source_target_pairs={{0,12},{2,14},{4,0},{6,2},{8,4},{10,6},{12,8},{14,10},{1,13},{3,15... | collective-permute-start | bytes 1572872 | tf_op jit(solution)/shard_map/ppermute | solution.py:493
  71.3 6.7 %copy-start.9 = (bf16[1024,512]{1,0:T(8,128)(2,1)}, bf16[1024,512]{1,0:T(8,128)(2,1)S(1)}, u32[]{:S(2)}) copy-start(bf16[1024,512]{1,0:T(8,128)(2,1)S(1)} %get-tuple-element.38) | copy-start | bytes 3145732
  76.9 13.7 %copy-start.2 = (bf16[128,4096]{1,0:T(8,128)(2,1)S(1)}, bf16[128,4096]{1,0:T(8,128)(2,1)}, u32[]{:S(2)}) copy-start(bf16[128,4096]{1,0:T(8,128)(2,1)} %in_ref.1) | copy-start | bytes 3145732
  76.9 13.7 %copy-start.7 = (s32[32]{0:T(128)S(1)}, s32[32]{0:T(128)}, u32[]{:S(2)}) copy-start(s32[32]{0:T(128)} %copy-done.6) | copy-start | bytes 388
  76.9 14.3 %copy-start.12 = (s32[1,2,8,2]{2,3,1,0:T(2,128)S(1)}, s32[1,2,8,2]{2,3,1,0:T(2,128)}, u32[]{:S(2)}) copy-start(s32[1,2,8,2]{2,3,1,0:T(2,128)} %param.15) | copy-start | bytes 388
  78.0 35.0 %all-to-all-start = ((bf16[16,8,4096]{2,1,0:T(8,128)(2,1)}), bf16[16,8,4096]{2,1,0:T(8,128)(2,1)S(1)}, u32[]{:S(2)}, u32[]{:S(2)}) async-start(bf16[16,8,4096]{2,1,0:T(8,128)(2,1)} %bitcast.7), calls=%async_computation | async-start | bytes 2097152 | tf_op jit(solution)/shard_map/all_to_all | solution.py:541
  87.3 32.1 %collective-permute-start.16 = (bf16[1024,512]{1,0:T(8,128)(2,1)}, bf16[1024,512]{1,0:T(8,128)(2,1)}, u32[]{:S(2)}, u32[]{:S(2)}) collective-permute-start(bf16[1024,512]{1,0:T(8,128)(2,1)} %copy-done.9), channel_id=1, source_target_pairs={{0,4},{2,6},{4,8},{6,10},{8,12},{10,14},{12,0},{14,2},{1,5},{3,7},... | collective-permute-start | bytes 3145736 | tf_op jit(solution)/shard_map/ppermute | solution.py:493
  87.4 32.0 %collective-permute-start.17 = (bf16[1024,512]{1,0:T(8,128)(2,1)S(1)}, bf16[1024,512]{1,0:T(8,128)(2,1)}, u32[]{:S(2)}, u32[]{:S(2)}) collective-permute-start(bf16[1024,512]{1,0:T(8,128)(2,1)S(1)} %get-tuple-element.39), channel_id=1, source_target_pairs={{0,12},{2,14},{4,0},{6,2},{8,4},{10,6},{12,8},{14,10},{1,13},{3,15... | collective-permute-start | bytes 3145736 | tf_op jit(solution)/shard_map/ppermute | solution.py:493
  114.0 32.6 %all-to-all-start.1 = ((bf16[16,8,4096]{2,1,0:T(8,128)(2,1)}), bf16[16,8,4096]{2,1,0:T(8,128)(2,1)}, u32[]{:S(2)}, u32[]{:S(2)}) async-start(bf16[16,8,4096]{2,1,0:T(8,128)(2,1)} %bitcast.9), calls=%async_computation.1 | async-start | bytes 2097152 | tf_op jit(solution)/shard_map/all_to_all | solution.py:544
  119.4 1.2 copy-start.11
  (1 other events, 0.8 us)

commit v8 on v7

--- a/solution.py
+++ b/solution.py
@@ -442,8 +442,8 @@
         out_shape=jax.ShapeDtypeStruct(array.shape, array.dtype),
         scratch_shapes=[
             pltpu.VMEM(array.shape, array.dtype),
-            pltpu.SemaphoreType.DMA((4,)),
-            pltpu.SemaphoreType.DMA((4,)),
+            pltpu.SemaphoreType.DMA((8,)),
+            pltpu.SemaphoreType.DMA((8,)),
         ],
         compiler_params=pltpu.CompilerParams(vmem_limit_bytes=4 * MIB),
         cost_estimate=cost(1, 1),

time: 149 us -> 149 us (level)
  no operation moved by 1% of the time
where the time goes in v8:
time: 149 us
  waiting for transfers between devices  87.4 us (59%)
  starting transfers between devices  32.2 us (22%)
  Pallas kernels  22.2 us (15%)
  local copies, waits for them, and re-layouts  5.93 us (4%)
    ppermute x17, waiting for transfers between devices, on_device(): send = lambda piece, pairs: lax.ppermute(piece, 'dp', pairs)  36.7 us
    all_to_all x1, waiting for transfers between devices, on_device(): input_grad = lax.all_to_all(sums, 'pipe', 0, 0, tiled=True)  23.5 us
    all_to_all x1, waiting for transfers between devices, on_device(): parts = lax.all_to_all(branch, 'pipe', 0, 0, tiled=True)  21.7 us
    ppermute x17, starting transfers between devices, on_device(): send = lambda piece, pairs: lax.ppermute(piece, 'dp', pairs)  17.2 us
    all_to_all x1, starting transfers between devices, on_device(): parts = lax.all_to_all(branch, 'pipe', 0, 0, tiled=True)  9.29 us
    ppermute x1, waiting for transfers between devices, on_device(): lax.ppermute(share(THEIRS, jnp.bfloat16), 'tensor', [(0, 1), (1, 0)])  5.59 us
    all_to_all x1, starting transfers between devices, on_device(): input_grad = lax.all_to_all(sums, 'pipe', 0, 0, tiled=True)  5.3 us
    unnamed x26, local copies, waits for them, and re-layouts  4.58 us
  transfers between devices with their start and end apart: 20, of which 10 were waited for; matrix products, arithmetic and copies ran while one was open for 1% of the time, Pallas kernels for 13%

profile of v8, /device:TPU:16, one launch (start us, length us, event | category | flops | bytes accessed | tf_op | source)
XLA Modules:
  0.0 148.9 jit_solution(15731953209511681569)
XLA Ops:
  0.7 1.3 slice_bitcast_fusion
  2.0 2.8 %collective-permute-start.1 = (bf16[1024,256]{1,0:T(8,128)(2,1)S(1)}, bf16[1024,256]{1,0:T(8,128)(2,1)S(1)}, u32[]{:S(2)}, u32[]{:S(2)}) collective-permute-start(bf16[1024,256]{1,0:T(8,128)(2,1)S(1)} %get-tuple-element.40.refs_6_), channel_id=1, source_target_pairs={{0,12},{2,14},{4,0},{6,2},{8,4},{10,6},{12,8},{14,10},{1,13},{3,15... | collective-permute-start | bytes 1572872 | tf_op jit(solution)/shard_map/ppermute | solution.py:493
  4.8 3.2 %collective-permute-start.4 = (bf16[1024,256]{1,0:T(8,128)(2,1)S(1)}, bf16[1024,256]{1,0:T(8,128)(2,1)S(1)}, u32[]{:S(2)}, u32[]{:S(2)}) collective-permute-start(bf16[1024,256]{1,0:T(8,128)(2,1)S(1)} %get-tuple-element.41.refs_3_), channel_id=1, source_target_pairs={{0,12},{2,14},{4,0},{6,2},{8,4},{10,6},{12,8},{14,10},{1,13},{3,15... | collective-permute-start | bytes 1572872 | tf_op jit(solution)/shard_map/ppermute | solution.py:493
  8.7 1.6 %copy-done = bf16[1,128,8192]{2,1,0:T(8,128)(2,1)S(1)} copy-done((bf16[1,128,8192]{2,1,0:T(8,128)(2,1)S(1)}, bf16[1,128,8192]{2,1,0:T(8,128)(2,1)}, u32[]{:S(2)}) %copy-start) | copy-done | bytes 2097176
  10.3 0.8 copy-done.5
  11.0 2.1 %shard_map.96 = (bf16[128,8192]{1,0:T(8,128)(2,1)S(1)}, f32[128,1]{1,0:T(8,128)S(1)}, bf16[128,4096]{1,0:T(8,128)(2,1)S(1)}) custom-call(s32[32]{0:T(128)S(1)} %shard_map.95.at_ref.refs_0_, bf16[128,8192]{1,0:T(8,128)(2,1)S(1)} %bitcast.17, bf16[1,8192]{1,0:T(2,128)(2,1)S(1)} %copy-done.5), custom_call_target="tpu_custom_call" | custom-call | flops 1 | bytes 1 | tf_op jit(solution)/shard_map/pallas_call | solution.py:102
  13.2 3.9 %collective-permute-done.1.second_ref.refs_7_ = bf16[1024,256]{1,0:T(8,128)(2,1)S(1)} collective-permute-done((bf16[1024,256]{1,0:T(8,128)(2,1)S(1)}, bf16[1024,256]{1,0:T(8,128)(2,1)S(1)}, u32[]{:S(2)}, u32[]{:S(2)}) %collective-permute-start.1) | collective-permute-done | bytes 524320 | tf_op jit(solution)/shard_map/ppermute | solution.py:493
  17.1 3.7 %collective-permute-start.9 = (bf16[1024,256]{1,0:T(8,128)(2,1)S(1)}, bf16[1024,256]{1,0:T(8,128)(2,1)S(1)}, u32[]{:S(2)}, u32[]{:S(2)}) collective-permute-start(bf16[1024,256]{1,0:T(8,128)(2,1)S(1)} %collective-permute-done.1.second_ref.refs_7_), channel_id=1, source_target_pairs={{0,12},{2,14},{4,0},{6,2},{8,4},{10,6},{12,8},{14,10},{1,13},{3,15... | collective-permute-start | bytes 1572872 | tf_op jit(solution)/shard_map/ppermute | solution.py:493
  20.8 7.5 %collective-permute-done.4.refs_5_.first_ref = bf16[1024,256]{1,0:T(8,128)(2,1)S(1)} collective-permute-done((bf16[1024,256]{1,0:T(8,128)(2,1)S(1)}, bf16[1024,256]{1,0:T(8,128)(2,1)S(1)}, u32[]{:S(2)}, u32[]{:S(2)}) %collective-permute-start.4) | collective-permute-done | bytes 524320 | tf_op jit(solution)/shard_map/ppermute | solution.py:493
  28.3 3.7 %collective-permute-done.5.refs_8_.second_ref = bf16[1024,256]{1,0:T(8,128)(2,1)S(1)} collective-permute-done((bf16[1024,256]{1,0:T(8,128)(2,1)S(1)}, bf16[1024,256]{1,0:T(8,128)(2,1)S(1)}, u32[]{:S(2)}, u32[]{:S(2)}) %collective-permute-start.5) | collective-permute-done | bytes 524320 | tf_op jit(solution)/shard_map/ppermute | solution.py:493
  32.0 2.3 %shard_map.98 = (f32[128,256]{1,0:T(8,128)S(1)}, f32[128,256]{1,0:T(8,128)S(1)}, bf16[8192,256]{1,0:T(8,128)(2,1)S(1)}, bf16[8192,256]{1,0:T(8,128)(2,1)S(1)}) custom-call(s32[32]{0:T(128)S(1)} %shard_map.95.at_ref.refs_0_, bf16[128,8192]{1,0:T(8,128)(2,1)S(1)} %get-tuple-element.21.refs_1_.normed_ref, ...), custom_call_target="tpu_custom_call" | custom-call | flops 1 | bytes 1 | tf_op jit(solution)/shard_map/pallas_call | solution.py:147
  35.3 3.8 %collective-permute-done.9.refs_6_ = bf16[1024,256]{1,0:T(8,128)(2,1)S(1)} collective-permute-done((bf16[1024,256]{1,0:T(8,128)(2,1)S(1)}, bf16[1024,256]{1,0:T(8,128)(2,1)S(1)}, u32[]{:S(2)}, u32[]{:S(2)}) %collective-permute-start.9) | collective-permute-done | bytes 524320 | tf_op jit(solution)/shard_map/ppermute | solution.py:493
  39.2 3.4 %collective-permute-done.7.refs_4_ = bf16[1024,256]{1,0:T(8,128)(2,1)S(1)} collective-permute-done((bf16[1024,256]{1,0:T(8,128)(2,1)S(1)}, bf16[1024,256]{1,0:T(8,128)(2,1)S(1)}, u32[]{:S(2)}, u32[]{:S(2)}) %collective-permute-start.7) | collective-permute-done | bytes 524320 | tf_op jit(solution)/shard_map/ppermute | solution.py:493
  42.6 1.9 %collective-permute-done.8.refs_5_ = bf16[1024,256]{1,0:T(8,128)(2,1)S(1)} collective-permute-done((bf16[1024,256]{1,0:T(8,128)(2,1)S(1)}, bf16[1024,256]{1,0:T(8,128)(2,1)S(1)}, u32[]{:S(2)}, u32[]{:S(2)}) %collective-permute-start.8) | collective-permute-done | bytes 524320 | tf_op jit(solution)/shard_map/ppermute | solution.py:493
  44.5 3.5 %shard_map.100 = (bf16[8192,256]{1,0:T(8,128)(2,1)S(1)}, bf16[8192,256]{1,0:T(8,128)(2,1)S(1)}, bf16[128,512]{1,0:T(8,128)(2,1)S(1)}, f32[128,1]{1,0:T(8,128)S(1)}) custom-call(s32[32]{0:T(128)S(1)} %shard_map.95.at_ref.refs_0_, bf16[128,8192]{1,0:T(8,128)(2,1)S(1)} %get-tuple-element.21.refs_1_.normed_ref, ...), custom_call_target="tpu_custom_call", output_to_operand_aliasing={{0}: (10, {}), {1}: (11, {})} | custom-call | flops 536870912 | bytes 5242880 | tf_op jit(solution)/shard_map/pallas_call | solution.py:217
  48.0 2.1 %shard_map.102 = bf16[128,4096]{1,0:T(8,128)(2,1)S(1)} custom-call(s32[32]{0:T(128)S(1)} %shard_map.95.at_ref.refs_0_, bf16[128,512]{1,0:T(8,128)(2,1)S(1)} %get-tuple-element.26.refs_1_.grads_ref, bf16[8192,256]{1,0:T(8,128)(2,1)S(1)} %get-tuple-element.27.refs_2_, bf16[8192,256]{1,0:T(8,128)(2,1)S(1)} %get-tuple-element.28.refs_3_, ...), custom_call_target="tpu_custom_call" | custom-call | flops 536870912 | bytes 5242880 | tf_op jit(solution)/shard_map/pallas_call | solution.py:268
  50.5 2.1 %shard_map.101.after_ref.mine_ref = f32[128,4096]{1,0:T(8,128)S(1)} custom-call(s32[32]{0:T(128)S(1)} %shard_map.95.at_ref.refs_0_, bf16[128,512]{1,0:T(8,128)(2,1)S(1)} %get-tuple-element.26.refs_1_.grads_ref, bf16[8192,256]{1,0:T(8,128)(2,1)S(1)} %get-tuple-element.27.refs_2_, bf16[8192,256]{1,0:T(8,128)(2,1)S(1)} %get-tuple-element.28.refs_3_, ...), custom_call_target="tpu_custom_call" | custom-call | flops 536870912 | bytes 5242880 | tf_op jit(solution)/shard_map/pallas_call | solution.py:268
  52.6 1.8 %shard_map.103 = (bf16[1024,512]{1,0:T(8,128)(2,1)S(1)}, bf16[1024,512]{1,0:T(8,128)(2,1)S(1)}, bf16[1024,512]{1,0:T(8,128)(2,1)S(1)}, bf16[512,512]{1,0:T(8,128)(2,1)S(1)}, bf16[512,512]{1,0:T(8,128)(2,1)S(1)}) custom-call(s32[32]{0:T(128)S(1)} %shard_map.95.at_ref.refs_0_, bf16[128,8192]{1,0:T(8,128)(2,1)S(1)} %get-tuple-element.21.refs_1_.normed_ref, ...), custom_call_target="tpu_custom_call" | custom-call | flops 2147483648 | bytes 4194304 | tf_op jit(solution)/shard_map/pallas_call | solution.py:305
  54.5 1.0 copy-done.10
  55.5 3.2 %collective-permute-start.15 = (bf16[512,512]{1,0:T(8,128)(2,1)S(1)}, bf16[512,512]{1,0:T(8,128)(2,1)S(1)}, u32[]{:S(2)}, u32[]{:S(2)}) collective-permute-start(bf16[512,512]{1,0:T(8,128)(2,1)S(1)} %get-tuple-element.35), channel_id=1, source_target_pairs={{0,12},{2,14},{4,0},{6,2},{8,4},{10,6},{12,8},{14,10},{1,13},{3,15... | collective-permute-start | bytes 1572872 | tf_op jit(solution)/shard_map/ppermute | solution.py:493
  58.7 12.3 %collective-permute-done.14.far_right_ref = bf16[512,512]{1,0:T(8,128)(2,1)S(1)} collective-permute-done((bf16[512,512]{1,0:T(8,128)(2,1)S(1)}, bf16[512,512]{1,0:T(8,128)(2,1)S(1)}, u32[]{:S(2)}, u32[]{:S(2)}) %collective-permute-start.14) | collective-permute-done | bytes 524320 | tf_op jit(solution)/shard_map/ppermute | solution.py:493
  71.3 5.6 %collective-permute-done.11.arrived_ref = bf16[128,4096]{1,0:T(8,128)(2,1)S(1)} collective-permute-done((bf16[128,4096]{1,0:T(8,128)(2,1)S(1)}, bf16[128,4096]{1,0:T(8,128)(2,1)S(1)}, u32[]{:S(2)}, u32[]{:S(2)}) %collective-permute-start.11) | collective-permute-done | bytes 1048608 | tf_op jit(solution)/shard_map/ppermute | solution.py:531
  76.9 1.0 shard_map.105
  78.0 9.3 %all-to-all-start = ((bf16[16,8,4096]{2,1,0:T(8,128)(2,1)}), bf16[16,8,4096]{2,1,0:T(8,128)(2,1)S(1)}, u32[]{:S(2)}, u32[]{:S(2)}) async-start(bf16[16,8,4096]{2,1,0:T(8,128)(2,1)} %bitcast.7), calls=%async_computation | async-start | bytes 2097152 | tf_op jit(solution)/shard_map/all_to_all | solution.py:541
  87.4 3.2 %collective-permute-start.17 = (bf16[1024,512]{1,0:T(8,128)(2,1)S(1)}, bf16[1024,512]{1,0:T(8,128)(2,1)}, u32[]{:S(2)}, u32[]{:S(2)}) collective-permute-start(bf16[1024,512]{1,0:T(8,128)(2,1)S(1)} %get-tuple-element.39), channel_id=1, source_target_pairs={{0,12},{2,14},{4,0},{6,2},{8,4},{10,6},{12,8},{14,10},{1,13},{3,15... | collective-permute-start | bytes 3145736 | tf_op jit(solution)/shard_map/ppermute | solution.py:493
  91.3 21.7 %all-to-all-done = bf16[16,8,4096]{2,1,0:T(8,128)(2,1)S(1)} async-done(((bf16[16,8,4096]{2,1,0:T(8,128)(2,1)}), bf16[16,8,4096]{2,1,0:T(8,128)(2,1)S(1)}, u32[]{:S(2)}, u32[]{:S(2)}) %all-to-all-start) | async-done | bytes 1048608 | tf_op jit(solution)/shard_map/all_to_all | solution.py:541
  113.0 1.0 shard_map.107
  114.0 5.3 %all-to-all-start.1 = ((bf16[16,8,4096]{2,1,0:T(8,128)(2,1)}), bf16[16,8,4096]{2,1,0:T(8,128)(2,1)}, u32[]{:S(2)}, u32[]{:S(2)}) async-start(bf16[16,8,4096]{2,1,0:T(8,128)(2,1)} %bitcast.9), calls=%async_computation.1 | async-start | bytes 2097152 | tf_op jit(solution)/shard_map/all_to_all | solution.py:544
  119.4 1.2 copy-done.11
  120.6 2.6 %shard_map.109 = bf16[2,1024,256]{2,1,0:T(8,128)(2,1)} custom-call(f32[2,8,2]{2,1,0:T(8,128)S(1)} %copy.12.factor_ref, bf16[1024,512]{1,0:T(8,128)(2,1)S(1)} %copy-done.11, bf16[1024,512]{1,0:T(8,128)(2,1)} %collective-permute-done.16.refs_1_, bf16[1024,512]{1,0:T(8,128)(2,1)} %collective-permute-done.17.refs_2_), custom_call_target="tpu_custom_call" | custom-call | flops 999999986991104 | bytes 999999995904 | tf_op jit(solution)/shard_map/pallas_call | solution.py:468
  123.2 23.5 %all-to-all-done.1 = bf16[16,8,4096]{2,1,0:T(8,128)(2,1)} async-done(((bf16[16,8,4096]{2,1,0:T(8,128)(2,1)}), bf16[16,8,4096]{2,1,0:T(8,128)(2,1)}, u32[]{:S(2)}, u32[]{:S(2)}) %all-to-all-start.1) | async-done | bytes 1048608 | tf_op jit(solution)/shard_map/all_to_all | solution.py:544
  146.7 2.1 %shard_map.108 = bf16[128,4096]{1,0:T(8,128)(2,1)} custom-call(bf16[128,4096]{1,0:T(8,128)(2,1)} %bitcast.10.in_ref), custom_call_target="tpu_custom_call" | custom-call | flops 1 | bytes 1 | tf_op jit(solution)/shard_map/pallas_call | solution.py:438
  (52 shorter events, 3.2 us)
Async XLA Ops:
  0.6 31.4 %collective-permute-start.2 = (bf16[2,1024,256]{2,1,0:T(8,128)(2,1)}, bf16[2,1024,256]{2,1,0:T(8,128)(2,1)S(1)}, u32[]{:S(2)}, u32[]{:S(2)}) collective-permute-start(bf16[2,1024,256]{2,1,0:T(8,128)(2,1)} %bitcast.24), channel_id=1, source_target_pairs={{0,2},{2,0},{4,6},{6,4},{8,10},{10,8},{12,14},{14,12},{1,3},{3,1},... | collective-permute-start | bytes 3145736 | tf_op jit(solution)/shard_map/ppermute | solution.py:493
  2.0 15.1 %collective-permute-start.1 = (bf16[1024,256]{1,0:T(8,128)(2,1)S(1)}, bf16[1024,256]{1,0:T(8,128)(2,1)S(1)}, u32[]{:S(2)}, u32[]{:S(2)}) collective-permute-start(bf16[1024,256]{1,0:T(8,128)(2,1)S(1)} %get-tuple-element.40.refs_6_), channel_id=1, source_target_pairs={{0,12},{2,14},{4,0},{6,2},{8,4},{10,6},{12,8},{14,10},{1,13},{3,15... | collective-permute-start | bytes 1572872 | tf_op jit(solution)/shard_map/ppermute | solution.py:493
  4.8 16.0 %collective-permute-start = (bf16[1024,256]{1,0:T(8,128)(2,1)S(1)}, bf16[1024,256]{1,0:T(8,128)(2,1)S(1)}, u32[]{:S(2)}, u32[]{:S(2)}) collective-permute-start(bf16[1024,256]{1,0:T(8,128)(2,1)S(1)} %get-tuple-element.41.refs_3_), channel_id=1, source_target_pairs={{0,4},{2,6},{4,8},{6,10},{8,12},{10,14},{12,0},{14,2},{1,5},{3,7},... | collective-permute-start | bytes 1572872 | tf_op jit(solution)/shard_map/ppermute | solution.py:493
  4.8 23.5 %collective-permute-start.4 = (bf16[1024,256]{1,0:T(8,128)(2,1)S(1)}, bf16[1024,256]{1,0:T(8,128)(2,1)S(1)}, u32[]{:S(2)}, u32[]{:S(2)}) collective-permute-start(bf16[1024,256]{1,0:T(8,128)(2,1)S(1)} %get-tuple-element.41.refs_3_), channel_id=1, source_target_pairs={{0,12},{2,14},{4,0},{6,2},{8,4},{10,6},{12,8},{14,10},{1,13},{3,15... | collective-permute-start | bytes 1572872 | tf_op jit(solution)/shard_map/ppermute | solution.py:493
  8.1 24.0 %collective-permute-start.5 = (bf16[1024,256]{1,0:T(8,128)(2,1)S(1)}, bf16[1024,256]{1,0:T(8,128)(2,1)S(1)}, u32[]{:S(2)}, u32[]{:S(2)}) collective-permute-start(bf16[1024,256]{1,0:T(8,128)(2,1)S(1)} %get-tuple-element.40.refs_6_), channel_id=1, source_target_pairs={{0,4},{2,6},{4,8},{6,10},{8,12},{10,14},{12,0},{14,2},{1,5},{3,7},... | collective-permute-start | bytes 1572872 | tf_op jit(solution)/shard_map/ppermute | solution.py:493
  8.7 44.0 %copy-start.6 = (s32[32]{0:T(128)}, s32[32]{0:T(128)S(1)}, u32[]{:S(2)}) copy-start(s32[32]{0:T(128)S(1)} %shard_map.95.at_ref.refs_0_) | copy-start | bytes 388
  8.7 1.6 %copy-start = (bf16[1,128,8192]{2,1,0:T(8,128)(2,1)S(1)}, bf16[1,128,8192]{2,1,0:T(8,128)(2,1)}, u32[]{:S(2)}) copy-start(bf16[1,128,8192]{2,1,0:T(8,128)(2,1)} %param.8) | copy-start | bytes 6291460
  17.1 22.1 %collective-permute-start.9 = (bf16[1024,256]{1,0:T(8,128)(2,1)S(1)}, bf16[1024,256]{1,0:T(8,128)(2,1)S(1)}, u32[]{:S(2)}, u32[]{:S(2)}) collective-permute-start(bf16[1024,256]{1,0:T(8,128)(2,1)S(1)} %collective-permute-done.1.second_ref.refs_7_), channel_id=1, source_target_pairs={{0,12},{2,14},{4,0},{6,2},{8,4},{10,6},{12,8},{14,10},{1,13},{3,15... | collective-permute-start | bytes 1572872 | tf_op jit(solution)/shard_map/ppermute | solution.py:493
  20.8 21.8 %collective-permute-start.7 = (bf16[1024,256]{1,0:T(8,128)(2,1)S(1)}, bf16[1024,256]{1,0:T(8,128)(2,1)S(1)}, u32[]{:S(2)}, u32[]{:S(2)}) collective-permute-start(bf16[1024,256]{1,0:T(8,128)(2,1)S(1)} %collective-permute-done.first_ref.refs_4_), channel_id=1, source_target_pairs={{0,4},{2,6},{4,8},{6,10},{8,12},{10,14},{12,0},{14,2},{1,5},{3,7},... | collective-permute-start | bytes 1572872 | tf_op jit(solution)/shard_map/ppermute | solution.py:493
  34.4 10.1 %copy-start.3 = (bf16[1,128,2048]{2,1,0:T(8,128)(2,1)S(1)}, bf16[1,128,2048]{2,1,0:T(8,128)(2,1)}, u32[]{:S(2)}) copy-start(bf16[1,128,2048]{2,1,0:T(8,128)(2,1)} %param.11) | copy-start | bytes 1572868
  34.4 10.1 %copy-start.4 = (bf16[1,128,2048]{2,1,0:T(8,128)(2,1)S(1)}, bf16[1,128,2048]{2,1,0:T(8,128)(2,1)}, u32[]{:S(2)}) copy-start(bf16[1,128,2048]{2,1,0:T(8,128)(2,1)} %param.12) | copy-start | bytes 1572868
  34.4 10.1 %copy-start.8 = (s32[128]{0:T(128)S(1)}, s32[128]{0:T(128)}, u32[]{:S(2)}) copy-start(s32[128]{0:T(128)} %param.14) | copy-start | bytes 1540
  34.5 10.0 %collective-permute-start.6 = (bf16[2,1024,256]{2,1,0:T(8,128)(2,1)S(1)}, bf16[2,1024,256]{2,1,0:T(8,128)(2,1)S(1)}, u32[]{:S(2)}, u32[]{:S(2)}) collective-permute-start(bf16[2,1024,256]{2,1,0:T(8,128)(2,1)S(1)} %shard_map.99), channel_id=1, source_target_pairs={{0,2},{2,0},{4,6},{6,4},{8,10},{10,8},{12,14},{14,12},{1,3},{3,1},... | collective-permute-start | bytes 3145736 | tf_op jit(solution)/shard_map/ppermute | solution.py:493
  34.7 9.8 %collective-permute-start.3 = (bf16[2,1024,256]{2,1,0:T(8,128)(2,1)S(1)}, bf16[2,1024,256]{2,1,0:T(8,128)(2,1)S(1)}, u32[]{:S(2)}, u32[]{:S(2)}) collective-permute-start(bf16[2,1024,256]{2,1,0:T(8,128)(2,1)S(1)} %shard_map.97), channel_id=1, source_target_pairs={{0,2},{2,0},{4,6},{6,4},{8,10},{10,8},{12,14},{14,12},{1,3},{3,1},... | collective-permute-start | bytes 3145736 | tf_op jit(solution)/shard_map/ppermute | solution.py:493
  35.2 17.4 %collective-permute-start.12 = (bf16[128,4096]{1,0:T(8,128)(2,1)S(1)}, bf16[128,4096]{1,0:T(8,128)(2,1)S(1)}, u32[]{:S(2)}, u32[]{:S(2)}) collective-permute-start(bf16[128,4096]{1,0:T(8,128)(2,1)S(1)} %get-tuple-element.31), channel_id=1, source_target_pairs={{0,2},{2,0},{4,6},{6,4},{8,10},{10,8},{12,14},{14,12},{1,3},{3,1},... | collective-permute-start | bytes 3145736 | tf_op jit(solution)/shard_map/ppermute | solution.py:493
  39.2 3.4 %collective-permute-start.10 = (bf16[1024,256]{1,0:T(8,128)(2,1)S(1)}, bf16[1024,256]{1,0:T(8,128)(2,1)S(1)}, u32[]{:S(2)}, u32[]{:S(2)}) collective-permute-start(bf16[1024,256]{1,0:T(8,128)(2,1)S(1)} %collective-permute-done.9.refs_6_), channel_id=1, source_target_pairs={{0,2},{2,0},{4,6},{6,4},{8,10},{10,8},{12,14},{14,12},{1,3},{3,1},... | collective-permute-start | bytes 1572872 | tf_op jit(solution)/shard_map/ppermute | solution.py:493
  42.6 1.9 %collective-permute-start.8 = (bf16[1024,256]{1,0:T(8,128)(2,1)S(1)}, bf16[1024,256]{1,0:T(8,128)(2,1)S(1)}, u32[]{:S(2)}, u32[]{:S(2)}) collective-permute-start(bf16[1024,256]{1,0:T(8,128)(2,1)S(1)} %collective-permute-done.7.refs_4_), channel_id=1, source_target_pairs={{0,2},{2,0},{4,6},{6,4},{8,10},{10,8},{12,14},{14,12},{1,3},{3,1},... | collective-permute-start | bytes 1572872 | tf_op jit(solution)/shard_map/ppermute | solution.py:493
  44.5 3.5 %copy-start.1 = (bf16[1,128,8192]{2,1,0:T(8,128)(2,1)S(1)}, bf16[1,128,8192]{2,1,0:T(8,128)(2,1)}, u32[]{:S(2)}) copy-start(bf16[1,128,8192]{2,1,0:T(8,128)(2,1)} %param.8) | copy-start | bytes 6291460
  50.1 26.8 %collective-permute-start.11 = (bf16[128,4096]{1,0:T(8,128)(2,1)S(1)}, bf16[128,4096]{1,0:T(8,128)(2,1)S(1)}, u32[]{:S(2)}, u32[]{:S(2)}) collective-permute-start(bf16[128,4096]{1,0:T(8,128)(2,1)S(1)} %shard_map.102), channel_id=1, source_target_pairs={{0,1},{1,0},{2,3},{3,2},{4,5},{5,4},{6,7},{7,6},{8,9},{9,8},{10,11... | collective-permute-start | bytes 3145736 | tf_op jit(solution)/shard_map/ppermute | solution.py:531
  50.5 2.1 %collective-permute-start.13 = (bf16[128,512]{1,0:T(8,128)(2,1)S(1)}, bf16[128,512]{1,0:T(8,128)(2,1)S(1)}, u32[]{:S(2)}, u32[]{:S(2)}) collective-permute-start(bf16[128,512]{1,0:T(8,128)(2,1)S(1)} %get-tuple-element.26.refs_1_.grads_ref), channel_id=1, source_target_pairs={{0,2},{2,0},{4,6},{6,4},{8,10},{10,8},{12,14},{14,12},{1,3},{3,1},... | collective-permute-start | bytes 393224 | tf_op jit(solution)/shard_map/ppermute | solution.py:493
  54.5 1.0 copy-start.10
  55.5 15.6 %collective-permute-start.14 = (bf16[512,512]{1,0:T(8,128)(2,1)S(1)}, bf16[512,512]{1,0:T(8,128)(2,1)S(1)}, u32[]{:S(2)}, u32[]{:S(2)}) collective-permute-start(bf16[512,512]{1,0:T(8,128)(2,1)S(1)} %get-tuple-element.34), channel_id=1, source_target_pairs={{0,4},{2,6},{4,8},{6,10},{8,12},{10,14},{12,0},{14,2},{1,5},{3,7},... | collective-permute-start | bytes 1572872 | tf_op jit(solution)/shard_map/ppermute | solution.py:493
  55.5 15.6 %collective-permute-start.15 = (bf16[512,512]{1,0:T(8,128)(2,1)S(1)}, bf16[512,512]{1,0:T(8,128)(2,1)S(1)}, u32[]{:S(2)}, u32[]{:S(2)}) collective-permute-start(bf16[512,512]{1,0:T(8,128)(2,1)S(1)} %get-tuple-element.35), channel_id=1, source_target_pairs={{0,12},{2,14},{4,0},{6,2},{8,4},{10,6},{12,8},{14,10},{1,13},{3,15... | collective-permute-start | bytes 1572872 | tf_op jit(solution)/shard_map/ppermute | solution.py:493
  71.3 6.7 %copy-start.9 = (bf16[1024,512]{1,0:T(8,128)(2,1)}, bf16[1024,512]{1,0:T(8,128)(2,1)S(1)}, u32[]{:S(2)}) copy-start(bf16[1024,512]{1,0:T(8,128)(2,1)S(1)} %get-tuple-element.38) | copy-start | bytes 3145732
  76.9 13.7 %copy-start.2 = (bf16[128,4096]{1,0:T(8,128)(2,1)S(1)}, bf16[128,4096]{1,0:T(8,128)(2,1)}, u32[]{:S(2)}) copy-start(bf16[128,4096]{1,0:T(8,128)(2,1)} %in_ref.1) | copy-start | bytes 3145732
  76.9 13.7 %copy-start.7 = (s32[32]{0:T(128)S(1)}, s32[32]{0:T(128)}, u32[]{:S(2)}) copy-start(s32[32]{0:T(128)} %copy-done.6) | copy-start | bytes 388
  76.9 14.3 %copy-start.12 = (s32[1,2,8,2]{2,3,1,0:T(2,128)S(1)}, s32[1,2,8,2]{2,3,1,0:T(2,128)}, u32[]{:S(2)}) copy-start(s32[1,2,8,2]{2,3,1,0:T(2,128)} %param.15) | copy-start | bytes 388
  78.0 35.0 %all-to-all-start = ((bf16[16,8,4096]{2,1,0:T(8,128)(2,1)}), bf16[16,8,4096]{2,1,0:T(8,128)(2,1)S(1)}, u32[]{:S(2)}, u32[]{:S(2)}) async-start(bf16[16,8,4096]{2,1,0:T(8,128)(2,1)} %bitcast.7), calls=%async_computation | async-start | bytes 2097152 | tf_op jit(solution)/shard_map/all_to_all | solution.py:541
  87.3 32.1 %collective-permute-start.16 = (bf16[1024,512]{1,0:T(8,128)(2,1)}, bf16[1024,512]{1,0:T(8,128)(2,1)}, u32[]{:S(2)}, u32[]{:S(2)}) collective-permute-start(bf16[1024,512]{1,0:T(8,128)(2,1)} %copy-done.9), channel_id=1, source_target_pairs={{0,4},{2,6},{4,8},{6,10},{8,12},{10,14},{12,0},{14,2},{1,5},{3,7},... | collective-permute-start | bytes 3145736 | tf_op jit(solution)/shard_map/ppermute | solution.py:493
  87.4 32.0 %collective-permute-start.17 = (bf16[1024,512]{1,0:T(8,128)(2,1)S(1)}, bf16[1024,512]{1,0:T(8,128)(2,1)}, u32[]{:S(2)}, u32[]{:S(2)}) collective-permute-start(bf16[1024,512]{1,0:T(8,128)(2,1)S(1)} %get-tuple-element.39), channel_id=1, source_target_pairs={{0,12},{2,14},{4,0},{6,2},{8,4},{10,6},{12,8},{14,10},{1,13},{3,15... | collective-permute-start | bytes 3145736 | tf_op jit(solution)/shard_map/ppermute | solution.py:493
  114.0 32.6 %all-to-all-start.1 = ((bf16[16,8,4096]{2,1,0:T(8,128)(2,1)}), bf16[16,8,4096]{2,1,0:T(8,128)(2,1)}, u32[]{:S(2)}, u32[]{:S(2)}) async-start(bf16[16,8,4096]{2,1,0:T(8,128)(2,1)} %bitcast.9), calls=%async_computation.1 | async-start | bytes 2097152 | tf_op jit(solution)/shard_map/all_to_all | solution.py:544
  119.4 1.2 copy-start.11
  (1 other events, 0.8 us)
